TPU v7x, 32 devices: a whole 2x2x4 slice. The times are simulated.
32 devices in a mesh: down: 16 (over z, y, core), cross: 2 (over x).
Axes of the slice: x: 2, y: 2, z: 4, core: 2. Of those that a mesh axis runs over, the one named last changes fastest.
Arguments:
- right_side: float32 [128, 64, 256], P('down', 'cross'), may hold values from -6 to 6
- kappa: float32 [128, 64, 256], P('down', 'cross'), may hold values from 0.3 to 3
- band_mask: int32 [128, 64, 256], P('down', 'cross'), may hold values 0 or 1
- tile_route: int32 [16, 8], P('down', 'cross'), may hold values from -1 to 3, as said below
Outputs:
- pressure: float32 [128, 64, 256], P('down', 'cross')
Inputs may be any that keep to these rules, and one draw needn't show every extreme that they name: `tile_route`: within the tiles of one device each value other than -1 occurs at most once; in every draw some owner receives 2 tiles from every device of its cross-slope group.
All inputs are finite; a program needn't handle non-finite values. No bound on the sum of `band_mask` on one device may be relied on, other than what follows from the above.
Results may differ from a plain program's by a relative error of at most 0.0003.
Values sent between devices are 32-bit elements; how exact they have to be, the bound alone decides.
No kernel may reach another device: no remote copies, remote signals or barrier semaphores. Data moves between devices by JAX's collectives and lax.ppermute only.
A program may use at most 64 MiB of HBM per device.

v0:
```python
import jax
import jax.numpy as jnp
from jax import lax
from jax.sharding import PartitionSpec as P

TPD = 4
SLOTS = 2
BLOCK_SWEEPS = 4
COARSE_ITERS = 12


OMEGA = 0.8
SNOW_FACTOR = 3.0


def with_halo(block, sides, width):
    for axis, dim in sides:
        count = lax.axis_size(axis)
        forward = [(i, i + 1) for i in range(count - 1)]
        backward = [(target, source) for source, target in forward]
        low = lax.ppermute(
            lax.slice_in_dim(block, block.shape[dim] - width, None, axis=dim), axis, forward
        )
        high = lax.ppermute(lax.slice_in_dim(block, 0, width, axis=dim), axis, backward)
        block = jnp.concatenate([low, block, high], axis=dim)
    return block


def pad_all(field):
    return jnp.pad(field, [(0, 0)] * (field.ndim - 3) + [(1, 1)] * 3)


def pad_vertical(field):
    return jnp.pad(field, ((0, 0), (0, 0), (1, 1)))


def center(padded):
    return padded[..., 1:-1, 1:-1, 1:-1]


def neighbours(padded):
    return [
        padded[..., 2:, 1:-1, 1:-1],
        padded[..., :-2, 1:-1, 1:-1],
        padded[..., 1:-1, 2:, 1:-1],
        padded[..., 1:-1, :-2, 1:-1],
        padded[..., 1:-1, 1:-1, 2:],
        padded[..., 1:-1, 1:-1, :-2],
    ]


def stencil(field_pad, conduct_pad, scale):
    middle = center(field_pad)
    kmiddle = center(conduct_pad)
    total = jnp.zeros_like(middle)
    for other, kother in zip(neighbours(field_pad), neighbours(conduct_pad)):
        total = total + scale * (kmiddle + kother) * (middle - other)
    return total


def diagonal(conduct_pad, scale):
    kmiddle = center(conduct_pad)
    total = jnp.zeros_like(kmiddle)
    for kother in neighbours(conduct_pad):
        total = total + scale * (kmiddle + kother)
    return total


def block_smooth(residual, conduct):
    conduct_pad = pad_all(conduct)
    diag = diagonal(conduct_pad, 2.0)
    safe = jnp.where(diag > 0, diag, 1.0)
    fix = OMEGA * residual / safe
    for sweep in range(BLOCK_SWEEPS - 1):
        fix = fix + OMEGA * (residual - stencil(pad_all(fix), conduct_pad, 2.0)) / safe
    return fix


def coarse_solve(totals, link_down, link_cross, outflow):
    link_up = jnp.concatenate([jnp.zeros_like(link_down[:1]), link_down[:-1]], 0)
    link_back = jnp.concatenate([jnp.zeros_like(link_cross[:, :1]), link_cross[:, :-1]], 1)

    def operate(field):
        padded = jnp.pad(field, 1)
        return (
            outflow * field
            - link_down * padded[2:, 1:-1]
            - link_up * padded[:-2, 1:-1]
            - link_cross * padded[1:-1, 2:]
            - link_back * padded[1:-1, :-2]
        )

    def sweep(step, carry):
        answer, resid, search, norm_now = carry
        image = operate(search)
        alpha = norm_now / jnp.sum(search * image)
        answer = answer + alpha * search
        resid = resid - alpha * image
        norm_next = jnp.sum(resid * resid)
        search = resid + norm_next / norm_now * search
        return (answer, resid, search, norm_next)

    start = (jnp.zeros_like(totals), totals, totals, jnp.sum(totals * totals))
    return lax.fori_loop(0, COARSE_ITERS, sweep, start)[0]


def block_mean(fine):
    rows_here, cols_here, layers = fine.shape
    return (
        fine.reshape(rows_here // 2, 2, cols_here // 2, 2, layers // 2, 2).sum(axis=(1, 3, 5))
        * 0.125
    )


def body(right_side, kappa, band_mask, tile_route):
    conduct = kappa / (1.0 + SNOW_FACTOR * band_mask.astype(jnp.float32))
    rows_here, cols_here, layers = right_side.shape
    half_x, half_y, half_z = (rows_here // 2, cols_here // 2, layers // 2)
    tile_w = half_y // TPD
    both_ext = with_halo(jnp.stack([conduct, right_side]), (("down", 1), ("cross", 2)), 2)
    conduct_ext = both_ext[0]
    source_wide = both_ext[1][1:-1, 1:-1]
    conduct_near = conduct_ext[1:-1, 1:-1]
    near_pad = pad_vertical(conduct_near)
    diag_fine = diagonal(near_pad, 0.5)
    row_ids = lax.axis_index("down") * rows_here - 1 + jnp.arange(rows_here + 2)
    col_ids = lax.axis_index("cross") * cols_here - 1 + jnp.arange(cols_here + 2)
    row_ok = (row_ids >= 0) & (row_ids < rows_here * lax.axis_size("down"))
    col_ok = (col_ids >= 0) & (col_ids < cols_here * lax.axis_size("cross"))
    inside = row_ok[:, None, None] & col_ok[None, :, None]
    wide_pad = pad_vertical(conduct_ext)
    diag_wide = diagonal(wide_pad, 0.5)
    safe_wide = jnp.where(inside, diag_wide, 1.0)

    def wide_sweep(field):
        field_ext = with_halo(field, (("down", 0), ("cross", 1)), 2)
        flux = stencil(pad_vertical(field_ext), wide_pad, 0.5)
        return field_ext[1:-1, 1:-1] + jnp.where(
            inside, OMEGA * (source_wide - flux) / safe_wide, 0.0
        )

    pressure = OMEGA * right_side / diag_fine
    pressure_wide = wide_sweep(pressure)
    residual = right_side - stencil(pad_vertical(pressure_wide), near_pad, 0.5)
    pressure = pressure_wide[1:-1, 1:-1]
    coarse_res = residual.reshape(half_x, 2, half_y, 2, half_z, 2).sum(axis=(1, 3, 5))
    coarse_con = block_mean(conduct)
    next_down = block_mean(conduct_ext[rows_here + 2 : rows_here + 4, 2:-2])[0]
    prev_down = block_mean(conduct_ext[0:2, 2:-2])[0]
    next_cross = block_mean(conduct_ext[2:-2, cols_here + 2 : cols_here + 4])[:, 0]
    prev_cross = block_mean(conduct_ext[2:-2, 0:2])[:, 0]
    link_down = 2.0 * jnp.sum(coarse_con[-1] + next_down)
    link_up = 2.0 * jnp.sum(coarse_con[0] + prev_down)
    link_cross = 2.0 * jnp.sum(coarse_con[:, -1] + next_cross)
    link_back = 2.0 * jnp.sum(coarse_con[:, 0] + prev_cross)
    vertical = 2.0 * jnp.sum(coarse_con[:, :, 0] + coarse_con[:, :, -1])
    outflow = link_down + link_up + link_cross + link_back + vertical
    totals = jnp.sum(coarse_res)
    summary = jnp.stack([totals, link_down, link_cross, outflow])[None, :]
    tiles_res = coarse_res.reshape(half_x, TPD, tile_w, half_z).transpose(1, 0, 2, 3)
    tiles_con = coarse_con.reshape(half_x, TPD, tile_w, half_z).transpose(1, 0, 2, 3)
    route = tile_route[0]
    n_cross = lax.axis_size("cross")
    onehot = (route[None, :] == jnp.arange(n_cross * SLOTS)[:, None]).astype(jnp.float32)
    send_res = jnp.einsum("st,txyz->sxyz", onehot, tiles_res, precision=lax.Precision.HIGHEST)
    send_con = jnp.einsum("st,txyz->sxyz", onehot, tiles_con, precision=lax.Precision.HIGHEST)
    send_res = send_res.reshape(n_cross, SLOTS, half_x, tile_w, half_z)
    send_con = send_con.reshape(n_cross, SLOTS, half_x, tile_w, half_z)
    fixes = block_smooth(
        lax.all_to_all(send_res, "cross", split_axis=0, concat_axis=0, tiled=True),
        lax.all_to_all(send_con, "cross", split_axis=0, concat_axis=0, tiled=True),
    )
    returned = lax.all_to_all(fixes, "cross", split_axis=0, concat_axis=0, tiled=True)
    returned = returned.reshape(n_cross * SLOTS, half_x, tile_w, half_z)
    tile_fix = jnp.einsum("st,sxyz->txyz", onehot, returned, precision=lax.Precision.HIGHEST)
    tile_fix = tile_fix.transpose(1, 0, 2, 3).reshape(half_x, half_y, half_z)
    n_down = lax.axis_size("down")
    n_cross_all = lax.axis_size("cross")
    table = lax.all_gather(summary, ("down", "cross"), axis=0, tiled=True).reshape(
        n_down, n_cross_all, 4
    )
    answer = coarse_solve(table[:, :, 0], table[:, :, 1], table[:, :, 2], table[:, :, 3])
    brick_fix = lax.dynamic_slice(
        answer, (lax.axis_index("down"), lax.axis_index("cross")), (1, 1)
    )[0, 0]
    correction = tile_fix + brick_fix
    fine_fix = jnp.broadcast_to(
        correction[:, None, :, None, :, None], (half_x, 2, half_y, 2, half_z, 2)
    ).reshape(rows_here, cols_here, layers)
    pressure = pressure + fine_fix
    pressure_wide = wide_sweep(pressure)
    flux = stencil(pad_vertical(pressure_wide), near_pad, 0.5)
    pressure = pressure_wide[1:-1, 1:-1] + OMEGA * (right_side - flux) / diag_fine
    return pressure


def solution(mesh):
    return jax.shard_map(
        body,
        mesh=mesh,
        in_specs=(
            P("down", "cross", None),
            P("down", "cross", None),
            P("down", "cross", None),
            P("down", "cross"),
        ),
        out_specs=P("down", "cross", None),
        check_vma=False,
    )
```

profile of v0, /device:TPU:0, one launch (start us, length us, event | category | flops | bytes accessed | tf_op | source)
XLA Modules:
  0.0 233.9 jit_solution(4063128983996653998)
XLA Ops:
  2.0 2.4 %collective-permute-start = (f32[2,2,32,256]{3,2,1,0:T(8,128)S(1)}, f32[2,2,32,256]{3,2,1,0:T(8,128)S(1)}, u32[]{:S(2)}, u32[]{:S(2)}) collective-permute-start(f32[2,2,32,256]{3,2,1,0:T(8,128)S(1)} %get-tuple-element.209), channel_id=1, source_target_pairs={{0,2},{2,4},{4,6},{6,8},{8,10},{10,12},{12,14},{14,16},{16,18},{18... | collective-permute-start | bytes 393224 | tf_op jit(solution)/shard_map/ppermute | solution.py:21
  4.4 1.4 collective-permute-start.1
  5.8 18.1 %reshape.115 = f32[4,2,16,2,128,2]{5,4,3,2,1,0:T(8,128)} reshape(f32[8,32,256]{2,1,0:T(8,128)S(1)} %add_divide_fusion) | data formatting | bytes 524288 | tf_op jit(solution)/shard_map/reshape | solution.py:110
  23.9 7.0 %reduce_sum.170 = f32[4,16,128]{2,1,0:T(8,128)S(1)} reduce(f32[4,2,16,2,128,2]{5,4,3,2,1,0:T(8,128)} %reshape.115, f32[]{:T(128)} %constant.27.clone.1), dimensions={1,3,5}, to_apply=%region_1.2 | reduce | flops 57344 | bytes 294916 | tf_op jit(solution)/shard_map/reduce_sum | solution.py:110
  31.8 3.6 %all-to-all-start.1 = ((f32[2,2,4,4,128]{4,1,3,2,0:T(2,128)}), f32[2,2,4,4,128]{4,1,3,2,0:T(2,128)S(1)}, u32[]{:S(2)}, u32[]{:S(2)}) async-start(f32[2,2,4,4,128]{4,1,3,2,0:T(2,128)} %copy.29), calls=%async_computation.1 | async-start | bytes 65536 | tf_op jit(solution)/shard_map/all_to_all | solution.py:171
  35.6 3.9 %collective-permute-start.2 = (f32[2,12,2,256]{3,2,1,0:T(2,128)S(1)}, f32[2,12,2,256]{3,2,1,0:T(2,128)S(1)}, u32[]{:S(2)}, u32[]{:S(2)}) collective-permute-start(f32[2,12,2,256]{3,2,1,0:T(2,128)S(1)} %get-tuple-element.207), channel_id=1, source_target_pairs={{0,1},{2,3},{4,5},{6,7},{8,9},{10,11},{12,13},{14,15},{16,17},{18,... | collective-permute-start | bytes 147464 | tf_op jit(solution)/shard_map/ppermute | solution.py:21
  39.5 1.3 collective-permute-start.3
  42.2 3.3 %collective-permute-done.3 = f32[2,12,2,256]{3,2,1,0:T(2,128)S(1)} collective-permute-done((f32[2,12,2,256]{3,2,1,0:T(2,128)S(1)}, f32[2,12,2,256]{3,2,1,0:T(2,128)S(1)}, u32[]{:S(2)}, u32[]{:S(2)}) %collective-permute-start.3) | collective-permute-done | bytes 49184 | tf_op jit(solution)/shard_map/ppermute | solution.py:24
  46.6 2.1 reduce_sum.173
  49.0 2.1 reduce_sum.181
  53.0 3.1 %collective-permute-start.4 = (f32[2,32,256]{2,1,0:T(8,128)S(1)}, f32[2,32,256]{2,1,0:T(8,128)S(1)}, u32[]{:S(2)}, u32[]{:S(2)}) collective-permute-start(f32[2,32,256]{2,1,0:T(8,128)S(1)} %get-tuple-element.217), channel_id=1, source_target_pairs={{0,2},{2,4},{4,6},{6,8},{8,10},{10,12},{12,14},{14,16},{16,18},{18... | collective-permute-start | bytes 196616 | tf_op jit(solution)/shard_map/ppermute | solution.py:21
  56.2 1.3 collective-permute-start.5
  58.8 3.5 %collective-permute-done.5 = f32[2,32,256]{2,1,0:T(8,128)S(1)} collective-permute-done((f32[2,32,256]{2,1,0:T(8,128)S(1)}, f32[2,32,256]{2,1,0:T(8,128)S(1)}, u32[]{:S(2)}, u32[]{:S(2)}) %collective-permute-start.5) | collective-permute-done | bytes 65568 | tf_op jit(solution)/shard_map/ppermute | solution.py:24
  62.3 1.6 collective-permute-start.6
  63.9 1.3 collective-permute-start.7
  68.3 1.3 collective-permute-done.7
  69.7 2.0 select_add_fusion.2
  73.5 42.8 %all-reduce.13 = f32[128]{0:T(128)S(1)} all-reduce(f32[128]{0:T(128)S(1)} %maximum_dynamic-update-slice_fusion), channel_id=2, replica_groups=mesh['down'=16,'cross'=2] {'down','cross'}, use_global_device_ids=true, to_apply=%add.13 | all-reduce | flops 128 | bytes 1024
  116.5 18.1 %reshape.112 = f32[4,2,16,2,128,2]{5,4,3,2,1,0:T(8,128)} reshape(f32[8,32,256]{2,1,0:T(8,128)S(1)} %get-tuple-element.195) | data formatting | bytes 524288 | tf_op jit(solution)/shard_map/reshape | solution.py:146
  134.6 7.0 %reduce_sum.169 = f32[4,16,128]{2,1,0:T(8,128)S(1)} reduce(f32[4,2,16,2,128,2]{5,4,3,2,1,0:T(8,128)} %reshape.112, f32[]{:T(128)} %constant.27.clone.1), dimensions={1,3,5}, to_apply=%region_0.1 | reduce | flops 57344 | bytes 294916 | tf_op jit(solution)/shard_map/reduce_sum | solution.py:146
  142.6 3.5 %all-to-all-start = ((f32[2,2,4,4,128]{4,1,3,2,0:T(2,128)}), f32[2,2,4,4,128]{4,1,3,2,0:T(2,128)S(1)}, u32[]{:S(2)}, u32[]{:S(2)}) async-start(f32[2,2,4,4,128]{4,1,3,2,0:T(2,128)} %copy.26), calls=%async_computation | async-start | bytes 65536 | tf_op jit(solution)/shard_map/all_to_all | solution.py:170
  147.4 2.8 %all-to-all-done = f32[2,2,4,4,128]{4,1,3,2,0:T(2,128)S(1)} async-done(((f32[2,2,4,4,128]{4,1,3,2,0:T(2,128)}), f32[2,2,4,4,128]{4,1,3,2,0:T(2,128)S(1)}, u32[]{:S(2)}, u32[]{:S(2)}) %all-to-all-start) | async-done | bytes 32800 | tf_op jit(solution)/shard_map/all_to_all | solution.py:170
  151.4 3.3 %all-to-all-start.2 = ((f32[2,2,4,4,128]{4,1,3,2,0:T(2,128)}), f32[2,2,4,4,128]{4,1,3,2,0:T(2,128)S(1)}, u32[]{:S(2)}, u32[]{:S(2)}) async-start(f32[2,2,4,4,128]{4,1,3,2,0:T(2,128)} %divide_add_fusion), calls=%async_computation.2 | async-start | bytes 65536 | tf_op jit(solution)/shard_map/all_to_all | solution.py:173
  154.7 39.9 %while.19 = (s32[]{:T(128)}, f32[16,2]{0,1:T(2,128)S(1)}, f32[16,2]{0,1:T(2,128)S(1)}, f32[16,2]{0,1:T(2,128)S(1)}, f32[]{:T(128)}, /*index=5*/f32[16,2]{0,1:T(2...) while((s32[]{:T(128)}, f32[16,2]{0,1:T(2,128)S(1)}, ...), condition=%wide.region_20.21_spmd.clone, body=%wide.region_17.20_spmd.clone.sunk | while | flops 643 | bytes 2099 | solution.py:104
  196.1 6.3 %broadcast_in_dim.47 = f32[4,2,16,2,128,2]{5,4,3,2,1,0:T(8,128)} broadcast(f32[4,16,128]{2,1,0:T(8,128)S(1)} %bitcast.68), dimensions={0,2,4} | broadcast | bytes 294912 | tf_op jit(solution)/shard_map/broadcast_in_dim | solution.py:187
  202.5 12.7 %reshape.119 = f32[8,32,256]{2,1,0:T(8,128)S(1)} reshape(f32[4,2,16,2,128,2]{5,4,3,2,1,0:T(8,128)} %broadcast_in_dim.47) | data formatting | bytes 524288 | tf_op jit(solution)/shard_map/reshape | solution.py:189
  215.3 1.3 collective-permute-start.8
  216.6 1.3 collective-permute-start.9
  217.9 4.0 %collective-permute-done.9 = f32[2,32,256]{2,1,0:T(8,128)S(1)} collective-permute-done((f32[2,32,256]{2,1,0:T(8,128)S(1)}, f32[2,32,256]{2,1,0:T(8,128)S(1)}, u32[]{:S(2)}, u32[]{:S(2)}) %collective-permute-start.9) | collective-permute-done | bytes 65568 | tf_op jit(solution)/shard_map/ppermute | solution.py:24
  221.9 3.9 %collective-permute-start.10 = (f32[12,2,256]{2,1,0:T(2,128)S(1)}, f32[12,2,256]{2,1,0:T(2,128)S(1)}, u32[]{:S(2)}, u32[]{:S(2)}) collective-permute-start(f32[12,2,256]{2,1,0:T(2,128)S(1)} %get-tuple-element.211), channel_id=1, source_target_pairs={{0,1},{2,3},{4,5},{6,7},{8,9},{10,11},{12,13},{14,15},{16,17},{18,... | collective-permute-start | bytes 73736 | tf_op jit(solution)/shard_map/ppermute | solution.py:21
  225.8 1.3 collective-permute-start.11
  227.3 4.2 %collective-permute-done.11 = f32[12,2,256]{2,1,0:T(2,128)S(1)} collective-permute-done((f32[12,2,256]{2,1,0:T(2,128)S(1)}, f32[12,2,256]{2,1,0:T(2,128)S(1)}, u32[]{:S(2)}, u32[]{:S(2)}) %collective-permute-start.11) | collective-permute-done | bytes 24608 | tf_op jit(solution)/shard_map/ppermute | solution.py:24
  (113 shorter events, 35.0 us)
Async XLA Ops:
  2.0 33.5 %collective-permute-start = (f32[2,2,32,256]{3,2,1,0:T(8,128)S(1)}, f32[2,2,32,256]{3,2,1,0:T(8,128)S(1)}, u32[]{:S(2)}, u32[]{:S(2)}) collective-permute-start(f32[2,2,32,256]{3,2,1,0:T(8,128)S(1)} %get-tuple-element.209), channel_id=1, source_target_pairs={{0,2},{2,4},{4,6},{6,8},{8,10},{10,12},{12,14},{14,16},{16,18},{18... | collective-permute-start | bytes 393224 | tf_op jit(solution)/shard_map/ppermute | solution.py:21
  4.4 26.6 %copy-start.2 = (s32[1,4]{1,0:T(1,128)S(1)}, s32[1,4]{1,0:T(1,128)}, u32[]{:S(2)}) copy-start(s32[1,4]{1,0:T(1,128)} %param.9) | copy-start | bytes 52
  4.4 31.2 %copy-start = (f32[8,32,256]{2,1,0:T(8,128)S(1)}, f32[8,32,256]{2,1,0:T(8,128)}, u32[]{:S(2)}) copy-start(f32[8,32,256]{2,1,0:T(8,128)} %param.6) | copy-start | bytes 786436
  4.4 31.1 %collective-permute-start.1 = (f32[2,2,32,256]{3,2,1,0:T(8,128)S(1)}, f32[2,2,32,256]{3,2,1,0:T(8,128)S(1)}, u32[]{:S(2)}, u32[]{:S(2)}) collective-permute-start(f32[2,2,32,256]{3,2,1,0:T(8,128)S(1)} %get-tuple-element.210), channel_id=1, source_target_pairs={{2,0},{4,2},{6,4},{8,6},{10,8},{12,10},{14,12},{16,14},{18,16},{20... | collective-permute-start | bytes 393224 | tf_op jit(solution)/shard_map/ppermute | solution.py:24
  31.8 110.8 %all-to-all-start.1 = ((f32[2,2,4,4,128]{4,1,3,2,0:T(2,128)}), f32[2,2,4,4,128]{4,1,3,2,0:T(2,128)S(1)}, u32[]{:S(2)}, u32[]{:S(2)}) async-start(f32[2,2,4,4,128]{4,1,3,2,0:T(2,128)} %copy.29), calls=%async_computation.1 | async-start | bytes 65536 | tf_op jit(solution)/shard_map/all_to_all | solution.py:171
  35.6 6.6 %collective-permute-start.2 = (f32[2,12,2,256]{3,2,1,0:T(2,128)S(1)}, f32[2,12,2,256]{3,2,1,0:T(2,128)S(1)}, u32[]{:S(2)}, u32[]{:S(2)}) collective-permute-start(f32[2,12,2,256]{3,2,1,0:T(2,128)S(1)} %get-tuple-element.207), channel_id=1, source_target_pairs={{0,1},{2,3},{4,5},{6,7},{8,9},{10,11},{12,13},{14,15},{16,17},{18,... | collective-permute-start | bytes 147464 | tf_op jit(solution)/shard_map/ppermute | solution.py:21
  39.5 6.0 %collective-permute-start.3 = (f32[2,12,2,256]{3,2,1,0:T(2,128)S(1)}, f32[2,12,2,256]{3,2,1,0:T(2,128)S(1)}, u32[]{:S(2)}, u32[]{:S(2)}) collective-permute-start(f32[2,12,2,256]{3,2,1,0:T(2,128)S(1)} %get-tuple-element.208), channel_id=1, source_target_pairs={{1,0},{3,2},{5,4},{7,6},{9,8},{11,10},{13,12},{15,14},{17,16},{19,... | collective-permute-start | bytes 147464 | tf_op jit(solution)/shard_map/ppermute | solution.py:24
  53.0 5.7 %collective-permute-start.4 = (f32[2,32,256]{2,1,0:T(8,128)S(1)}, f32[2,32,256]{2,1,0:T(8,128)S(1)}, u32[]{:S(2)}, u32[]{:S(2)}) collective-permute-start(f32[2,32,256]{2,1,0:T(8,128)S(1)} %get-tuple-element.217), channel_id=1, source_target_pairs={{0,2},{2,4},{4,6},{6,8},{8,10},{10,12},{12,14},{14,16},{16,18},{18... | collective-permute-start | bytes 196616 | tf_op jit(solution)/shard_map/ppermute | solution.py:21
  56.2 6.1 %collective-permute-start.5 = (f32[2,32,256]{2,1,0:T(8,128)S(1)}, f32[2,32,256]{2,1,0:T(8,128)S(1)}, u32[]{:S(2)}, u32[]{:S(2)}) collective-permute-start(f32[2,32,256]{2,1,0:T(8,128)S(1)} %get-tuple-element.218), channel_id=1, source_target_pairs={{2,0},{4,2},{6,4},{8,6},{10,8},{12,10},{14,12},{16,14},{18,16},{20... | collective-permute-start | bytes 196616 | tf_op jit(solution)/shard_map/ppermute | solution.py:24
  62.3 6.0 %collective-permute-start.6 = (f32[12,2,256]{2,1,0:T(2,128)S(1)}, f32[12,2,256]{2,1,0:T(2,128)S(1)}, u32[]{:S(2)}, u32[]{:S(2)}) collective-permute-start(f32[12,2,256]{2,1,0:T(2,128)S(1)} %get-tuple-element.213), channel_id=1, source_target_pairs={{0,1},{2,3},{4,5},{6,7},{8,9},{10,11},{12,13},{14,15},{16,17},{18,... | collective-permute-start | bytes 73736 | tf_op jit(solution)/shard_map/ppermute | solution.py:21
  63.9 5.7 %collective-permute-start.7 = (f32[12,2,256]{2,1,0:T(2,128)S(1)}, f32[12,2,256]{2,1,0:T(2,128)S(1)}, u32[]{:S(2)}, u32[]{:S(2)}) collective-permute-start(f32[12,2,256]{2,1,0:T(2,128)S(1)} %get-tuple-element.214), channel_id=1, source_target_pairs={{1,0},{3,2},{5,4},{7,6},{9,8},{11,10},{13,12},{15,14},{17,16},{19,... | collective-permute-start | bytes 73736 | tf_op jit(solution)/shard_map/ppermute | solution.py:24
  142.6 7.5 %all-to-all-start = ((f32[2,2,4,4,128]{4,1,3,2,0:T(2,128)}), f32[2,2,4,4,128]{4,1,3,2,0:T(2,128)S(1)}, u32[]{:S(2)}, u32[]{:S(2)}) async-start(f32[2,2,4,4,128]{4,1,3,2,0:T(2,128)} %copy.26), calls=%async_computation | async-start | bytes 65536 | tf_op jit(solution)/shard_map/all_to_all | solution.py:170
  151.4 43.8 %all-to-all-start.2 = ((f32[2,2,4,4,128]{4,1,3,2,0:T(2,128)}), f32[2,2,4,4,128]{4,1,3,2,0:T(2,128)S(1)}, u32[]{:S(2)}, u32[]{:S(2)}) async-start(f32[2,2,4,4,128]{4,1,3,2,0:T(2,128)} %divide_add_fusion), calls=%async_computation.2 | async-start | bytes 65536 | tf_op jit(solution)/shard_map/all_to_all | solution.py:173
  196.1 35.5 %copy-start.1 = (f32[12,36,256]{2,1,0:T(8,128)S(1)}, f32[12,36,256]{2,1,0:T(8,128)}, u32[]{:S(2)}) copy-start(f32[12,36,256]{2,1,0:T(8,128)} %get-tuple-element.205) | copy-start | bytes 1327108
  215.3 2.6 %collective-permute-start.8 = (f32[2,32,256]{2,1,0:T(8,128)S(1)}, f32[2,32,256]{2,1,0:T(8,128)S(1)}, u32[]{:S(2)}, u32[]{:S(2)}) collective-permute-start(f32[2,32,256]{2,1,0:T(8,128)S(1)} %get-tuple-element.215), channel_id=1, source_target_pairs={{0,2},{2,4},{4,6},{6,8},{8,10},{10,12},{12,14},{14,16},{16,18},{18... | collective-permute-start | bytes 196616 | tf_op jit(solution)/shard_map/ppermute | solution.py:21
  216.6 5.4 %collective-permute-start.9 = (f32[2,32,256]{2,1,0:T(8,128)S(1)}, f32[2,32,256]{2,1,0:T(8,128)S(1)}, u32[]{:S(2)}, u32[]{:S(2)}) collective-permute-start(f32[2,32,256]{2,1,0:T(8,128)S(1)} %get-tuple-element.216), channel_id=1, source_target_pairs={{2,0},{4,2},{6,4},{8,6},{10,8},{12,10},{14,12},{16,14},{18,16},{20... | collective-permute-start | bytes 196616 | tf_op jit(solution)/shard_map/ppermute | solution.py:24
  221.9 5.4 %collective-permute-start.10 = (f32[12,2,256]{2,1,0:T(2,128)S(1)}, f32[12,2,256]{2,1,0:T(2,128)S(1)}, u32[]{:S(2)}, u32[]{:S(2)}) collective-permute-start(f32[12,2,256]{2,1,0:T(2,128)S(1)} %get-tuple-element.211), channel_id=1, source_target_pairs={{0,1},{2,3},{4,5},{6,7},{8,9},{10,11},{12,13},{14,15},{16,17},{18,... | collective-permute-start | bytes 73736 | tf_op jit(solution)/shard_map/ppermute | solution.py:21
  225.8 5.7 %collective-permute-start.11 = (f32[12,2,256]{2,1,0:T(2,128)S(1)}, f32[12,2,256]{2,1,0:T(2,128)S(1)}, u32[]{:S(2)}, u32[]{:S(2)}) collective-permute-start(f32[12,2,256]{2,1,0:T(2,128)S(1)} %get-tuple-element.212), channel_id=1, source_target_pairs={{1,0},{3,2},{5,4},{7,6},{9,8},{11,10},{13,12},{15,14},{17,16},{19,... | collective-permute-start | bytes 73736 | tf_op jit(solution)/shard_map/ppermute | solution.py:24
where the time goes:
time: 236 us; the launch traced here: 234 us
  local copies, waits for them, and re-layouts  64.1 us (27%)
  other arithmetic  44.6 us (19%)
  blocking collectives  42.8 us (18%)
  starting transfers between devices  34.5 us (15%)
  loops' own time  23.5 us (10%)
  waiting for transfers between devices  19.4 us (8%)
  between operations  3.59 us (2%)
    unnamed x1, blocking collectives  42.8 us
    another operation x1, loops' own time, coarse_solve(): return lax.fori_loop(0, COARSE_ITERS, sweep, start)[0]  23.5 us
    reshape x1, local copies, waits for them, and re-layouts, block_mean(): fine.reshape(rows_here // 2, 2, cols_here // 2, 2, layers // 2, 2)  18.1 us
    reshape x1, local copies, waits for them, and re-layouts, body(): residual.reshape(half_x, 2, half_y, 2, half_z, 2).sum(axis=(1, 3, 5))  18.1 us
    ppermute x6, waiting for transfers between devices, with_halo(): lax.ppermute(lax.slice_in_dim(block, 0, width, axis=dim), axis, backward)  16.4 us
    ppermute x6, starting transfers between devices, with_halo(): lax.ppermute(lax.slice_in_dim(block, block.shape[dim] - width, None, axis...  16.2 us
    reshape x1, local copies, waits for them, and re-layouts, body(): fine_fix = jnp.broadcast_to(correction[:, None, :, None, :, None], (half_...  12.7 us
    reduce_sum x12, other arithmetic, sweep(): alpha = norm_now / jnp.sum(search * image)  8.53 us
  transfers between devices with their start and end apart: 15, of which 7 were waited for; matrix products, arithmetic and copies ran while one was open for 36% of the time, Pallas kernels for 0%

commit v1 on v0

v1 whole, which is shorter than its diff:
```python
import functools

import jax
import jax.numpy as jnp
from jax import lax
from jax.experimental import pallas as pl
from jax.experimental.pallas import tpu as pltpu
from jax.sharding import PartitionSpec as P

BLOCK_SWEEPS = 4
COARSE_ITERS = 12
OMEGA = 0.8
KEEP = 1.0 - OMEGA
SNOW_FACTOR = 3.0

DEPTH = 4
STRIP = 8
FLOAT = jnp.float32
VMEM_BYTES = 48 * 1024 * 1024


def partners(count, odd):
    found = []
    for i in range(count):
        j = ((i + 1) ^ 1) - 1 if odd else i ^ 1
        found.append(j if 0 <= j < count else i)
    return found


def pairings(count):
    return [k for k in (False, True) if any(j != i for i, j in enumerate(partners(count, k)))]


def pairs_of(count_down, count_cross, down_kind, cross_kind):
    rows = list(range(count_down)) if down_kind is None else partners(count_down, down_kind)
    cols = list(range(count_cross)) if cross_kind is None else partners(count_cross, cross_kind)
    return [
        (i * count_cross + j, rows[i] * count_cross + cols[j])
        for i in range(count_down)
        for j in range(count_cross)
    ]


def facing(index, count, kind):
    ahead = (index % 2 == 0) != kind
    return ahead, jnp.where(ahead, index < count - 1, index > 0)


def roll(x, amount, axis):
    return pltpu.roll(x, amount % x.shape[axis], axis)


def iota(shape, axis):
    return lax.broadcasted_iota(jnp.int32, shape, axis)


def gather(field, rows, wx, wx_at, wy, wz):
    low, here, high = rows
    value = field[here]
    total = wx[wx_at] * field[high] + wx[wx_at - 1] * field[low]
    total = total + wy * roll(value, -1, 0) + roll(wy * value, 1, 0)
    return total + wz * roll(value, -1, 1) + roll(wz * value, 1, 1)


def pack_kernel(nd, nc, rhs, kappa, mask, conduct, *messages):
    rows, cols, _ = rhs.shape
    messages = iter(messages)
    down, cross = lax.axis_index("down"), lax.axis_index("cross")
    for x in range(rows):
        conduct[x] = kappa[x] / (1.0 + SNOW_FACTOR * mask[x].astype(FLOAT))
    for kind in pairings(nd):
        ahead, _ = facing(down, nd, kind)
        out = next(messages)
        out[:DEPTH] = conduct[pl.ds(jnp.where(ahead, rows - DEPTH, 0), DEPTH)]
        out[DEPTH:] = rhs[pl.ds(jnp.where(ahead, rows - DEPTH + 1, 0), DEPTH - 1)]
    for cross_kind in pairings(nc):
        right, _ = facing(cross, nc, cross_kind)
        strip = pl.ds(pl.multiple_of(jnp.where(right, cols - STRIP, 0), STRIP), STRIP)
        out = next(messages)
        out[:rows] = conduct[:, strip, :]
        out[rows:] = rhs[:, strip, :]
        for kind in pairings(nd):
            ahead, _ = facing(down, nd, kind)
            out = next(messages)
            out[: DEPTH - 1] = conduct[pl.ds(jnp.where(ahead, rows - DEPTH + 1, 0), DEPTH - 1), strip, :]
            out[DEPTH - 1 :] = rhs[pl.ds(jnp.where(ahead, rows - DEPTH + 2, 0), DEPTH - 2), strip, :]


def pair_sum(x, axis):
    even = iota(x.shape, axis) % 2 == 0
    return x + jnp.where(even, roll(x, -1, axis), roll(x, 1, axis))


def total_of(x):
    return jnp.sum(jnp.sum(x, axis=0, keepdims=True), axis=1, keepdims=True)


def fold_lanes(x):
    return sum(x[:, i : i + 128] for i in range(0, x.shape[1], 128))


def main_kernel(nd, nc, rhs, conduct, route, *refs):
    rows, cols, layers = rhs.shape
    tiles = route.shape[1]
    tile_w = cols // tiles
    n_messages = len(pairings(nd)) + len(pairings(nc)) * (1 + len(pairings(nd)))
    messages = iter(refs[:n_messages])
    src, gain, wx, wy, wz, state, chunks, q, first, pres = refs[n_messages:]
    down, cross = lax.axis_index("down"), lax.axis_index("cross")
    wide = cols + 2 * STRIP
    own = slice(STRIP, STRIP + cols)

    zero_strip = jnp.zeros((q.shape[0], STRIP, layers), FLOAT)
    for ref in (q, src):
        ref[:, :STRIP, :] = zero_strip[: ref.shape[0]]
        ref[:, STRIP + cols :, :] = zero_strip[: ref.shape[0]]
    if len(pairings(nd)) < 2:
        q[...] = jnp.zeros(q.shape, FLOAT)
        src[...] = jnp.zeros(src.shape, FLOAT)
    q[DEPTH : DEPTH + rows, own, :] = conduct[...]
    src[DEPTH - 1 : DEPTH - 1 + rows, own, :] = rhs[...]
    for kind in pairings(nd):
        ahead, valid = facing(down, nd, kind)
        got = next(messages)
        q[pl.ds(jnp.where(ahead, DEPTH + rows, 0), DEPTH), own, :] = jnp.where(valid, got[:DEPTH], 0.0)
        src[pl.ds(jnp.where(ahead, DEPTH - 1 + rows, 0), DEPTH - 1), own, :] = jnp.where(
            valid, got[DEPTH:], 0.0
        )
    for cross_kind in pairings(nc):
        right, cross_valid = facing(cross, nc, cross_kind)
        strip = pl.ds(pl.multiple_of(jnp.where(right, STRIP + cols, 0), STRIP), STRIP)
        got = next(messages)
        q[DEPTH : DEPTH + rows, strip, :] = jnp.where(cross_valid, got[:rows], 0.0)
        src[DEPTH - 1 : DEPTH - 1 + rows, strip, :] = jnp.where(cross_valid, got[rows:], 0.0)
        for kind in pairings(nd):
            ahead, valid = facing(down, nd, kind)
            valid = valid & cross_valid
            got = next(messages)
            q[pl.ds(jnp.where(ahead, DEPTH + rows, 1), DEPTH - 1), strip, :] = jnp.where(
                valid, got[: DEPTH - 1], 0.0
            )
            src[pl.ds(jnp.where(ahead, DEPTH - 1 + rows, 1), DEPTH - 2), strip, :] = jnp.where(
                valid, got[DEPTH - 1 :], 0.0
            )

    lane = iota((wide, layers), 1)
    col = iota((wide, layers), 0)
    col_ok = (col >= jnp.where(cross > 0, 0, STRIP)) & (
        col < jnp.where(cross < nc - 1, wide, STRIP + cols)
    )

    for i in range(rows + 2 * (DEPTH - 1)):
        x = i - (DEPTH - 1)
        here = q[i + 1]
        ahead = q[i + 2]
        above = jnp.where(lane == layers - 1, 0.0, roll(here, -1, 1))
        below = jnp.where(lane == 0, 0.0, roll(here, 1, 1))
        right = roll(here, -1, 0)
        doubled = 6.0 * here + (q[i] + ahead) + (right + roll(here, 1, 0)) + (above + below)
        ok = col_ok & (doubled > 0.0)
        if x < 0:
            ok = ok & (down > 0)
        if x >= rows:
            ok = ok & (down < nd - 1)
        gain_here = jnp.where(ok, (2.0 * OMEGA) / doubled, 0.0)
        gain[i] = gain_here
        first[i] = gain_here * src[i]
        if i < wx.shape[0]:
            wx[i] = 0.5 * (here + ahead)
        if -2 <= x < rows + 2:
            wy[x + 2] = 0.5 * (here + right)
            wz[x + 2] = jnp.where(lane == layers - 1, 0.0, 0.5 * (here + above))

    for i in range(rows + 4):
        spread = gather(first, (i, i + 1, i + 2), wx, i + 1, wy[i], wz[i])
        pres[i] = KEEP * first[i + 1] + gain[i + 1] * (src[i + 1] + spread)

    tile_shape = (tiles, tile_w, layers)
    res_sum = jnp.zeros((cols, layers), FLOAT)
    coarse_res, coarse_con = [], []
    for k in range(rows // 2):
        res_pair = None
        for x in (2 * k, 2 * k + 1):
            i = x + 2
            value = pres[i]
            here = q[x + DEPTH]
            spread = gather(pres, (i - 1, i, i + 1), wx, i + 1, wy[i], wz[i])
            diag = wx[i + 1] + wx[i] + wy[i] + roll(wy[i], 1, 0)
            vertical = wz[i] + roll(wz[i], 1, 1)
            vertical = vertical + jnp.where((lane == 0) | (lane == layers - 1), 0.5 * here, 0.0)
            res = (src[x + DEPTH - 1] - (diag + vertical) * value + spread)[own]
            res_pair = res if res_pair is None else res_pair + res
        res_sum = res_sum + res_pair
        con_pair = q[2 * k + DEPTH, own, :] + q[2 * k + 1 + DEPTH, own, :]
        coarse_res.append(pair_sum(pair_sum(res_pair, 1), 0).reshape(tile_shape))
        coarse_con.append((0.125 * pair_sum(pair_sum(con_pair, 1), 0)).reshape(tile_shape))

    strip_col = iota((STRIP, layers), 0)
    own_lane = iota((cols, layers), 1)

    def rows_sum(start):
        return total_of(sum(q[DEPTH + start + r, own, :] for r in range(4)))

    def cols_sum(start):
        acc = jnp.zeros((STRIP, layers), FLOAT)
        for x in range(rows):
            left = q[x + DEPTH, start - STRIP : start, :]
            right = q[x + DEPTH, start : start + STRIP, :]
            acc = acc + jnp.where(strip_col >= STRIP - 2, left, 0.0) + jnp.where(strip_col < 2, right, 0.0)
        return total_of(acc)

    plane = sum(q[x + DEPTH, own, :] for x in range(rows))
    ends = total_of(jnp.where((own_lane < 2) | (own_lane >= layers - 2), plane, 0.0))
    link_down = 0.25 * rows_sum(rows - 2)
    link_up = 0.25 * rows_sum(-2)
    link_cross = 0.25 * cols_sum(STRIP + cols)
    link_back = 0.25 * cols_sum(STRIP)
    outflow = link_down + link_up + link_cross + link_back + 0.25 * ends
    total = total_of(res_sum)
    line = iota((8, 128), 0)
    summary = jnp.where(line == 0, total, jnp.where(line == 1, link_down, jnp.where(line == 2, link_cross, outflow)))

    tile_col = iota(tile_shape, 1)
    tile_lane = iota(tile_shape, 2)
    half_rows = len(coarse_con)
    link_x = [2.0 * (coarse_con[k] + coarse_con[k + 1]) for k in range(half_rows - 1)]
    link_y, link_z, tile_gain = [], [], []
    for k in range(half_rows):
        con = coarse_con[k]
        y_high = jnp.where(tile_col < tile_w - 2, roll(con, -2, 1), 0.0)
        y_low = jnp.where(tile_col >= 2, roll(con, 2, 1), 0.0)
        z_high = jnp.where(tile_lane < layers - 2, roll(con, -2, 2), 0.0)
        z_low = jnp.where(tile_lane >= 2, roll(con, 2, 2), 0.0)
        diag = 6.0 * con + (y_high + y_low) + (z_high + z_low)
        if k > 0:
            diag = diag + coarse_con[k - 1]
        if k < half_rows - 1:
            diag = diag + coarse_con[k + 1]
        diag = 2.0 * diag
        tile_gain.append(OMEGA / jnp.where(diag > 0.0, diag, 1.0))
        link_y.append(jnp.where(tile_col < tile_w - 2, 2.0 * (con + y_high), 0.0))
        link_z.append(jnp.where(tile_lane < layers - 2, 2.0 * (con + z_high), 0.0))
    fix = [tile_gain[k] * coarse_res[k] for k in range(half_rows)]
    for _ in range(BLOCK_SWEEPS - 1):
        updated = []
        for k in range(half_rows):
            value = fix[k]
            acc = coarse_res[k] + link_y[k] * roll(value, -2, 1) + roll(link_y[k] * value, 2, 1)
            acc = acc + link_z[k] * roll(value, -2, 2) + roll(link_z[k] * value, 2, 2)
            if k > 0:
                acc = acc + link_x[k - 1] * fix[k - 1]
            if k < half_rows - 1:
                acc = acc + link_x[k] * fix[k + 1]
            updated.append(KEEP * value + tile_gain[k] * acc)
        fix = updated
    touched = [jnp.where(route[0, t] >= 0, 1.0, 0.0) for t in range(tiles)]
    fix = [jnp.stack([f[t] * touched[t] for t in range(tiles)]) for f in fix]

    for i in range(rows + 4):
        if 2 <= i < rows + 2:
            state[i, :STRIP, :] = pres[i, :STRIP, :]
            state[i, own, :] = pres[i, own, :] + fix[(i - 2) // 2].reshape(cols, layers)
            state[i, STRIP + cols :, :] = pres[i, STRIP + cols :, :]
        else:
            state[i] = pres[i]

    half = layers // 2
    body_rows = 2 * tile_w
    count = nd * nc
    zero_chunk = jnp.zeros((body_rows, 128), FLOAT)

    def fill(b, carry):
        chunks[b, :body_rows, :] = zero_chunk
        chunks[b, body_rows:, :] = summary
        return carry

    lax.fori_loop(0, count, fill, 0)
    parity_col = iota((tile_w, layers), 0) % 2
    parity_lane = iota((tile_w, layers), 1) % 2

    def put(index, packed):
        chunks[index, :tile_w, :] = packed[:, :half]
        chunks[index, tile_w:body_rows, :] = packed[:, half:]

    def pack_row(f):
        top = jnp.where(parity_lane == 0, f[0], f[1])
        bottom = jnp.where(parity_lane == 0, f[2], f[3])
        return jnp.where(parity_col == 0, top, bottom)

    pair_col = iota((tile_w, layers), 0) // 2

    def pack_edge(tile, column):
        out = jnp.broadcast_to(fix[0][tile, column : column + 1], (tile_w, layers))
        for k in range(1, half_rows):
            line = jnp.broadcast_to(fix[k][tile, column : column + 1], (tile_w, layers))
            out = jnp.where(pair_col == k, line, out)
        return out

    me = down * nc + cross
    edges = {-1: (0, 0), 1: (tiles - 1, tile_w - 1)}
    for dx in (-1, 0, 1):
        for dy in (-1, 0, 1):
            if (dx, dy) == (0, 0):
                continue
            there = jnp.bool_(True)
            if dx:
                there = there & ((down > 0) if dx < 0 else (down < nd - 1))
            if dy:
                there = there & ((cross > 0) if dy < 0 else (cross < nc - 1))

            @pl.when(there)
            def _(dx=dx, dy=dy):
                k = 0 if dx < 0 else half_rows - 1
                if dy == 0:
                    packed = pack_row(fix[k])
                elif dx == 0:
                    packed = pack_edge(*edges[dy])
                else:
                    tile, column = edges[dy]
                    packed = jnp.broadcast_to(fix[k][tile, column : column + 1], (tile_w, layers))
                put(me + dx * nc + dy, packed)


def coarse_solve(totals, outflow, link_down, link_up, link_cross):
    nc = len(totals)

    def operate(v):
        out = []
        for c in range(nc):
            image = outflow[c] * v[c] - link_down[c] * roll(v[c], -1, 0) - link_up[c] * roll(v[c], 1, 0)
            if c < nc - 1:
                image = image - link_cross[c] * v[c + 1]
            if c > 0:
                image = image - link_cross[c - 1] * v[c - 1]
            out.append(image)
        return out

    def dot(a, b):
        return jnp.sum(sum(x * y for x, y in zip(a, b)), axis=0, keepdims=True)

    answer = [jnp.zeros_like(t) for t in totals]
    resid = search = totals
    norm = dot(totals, totals)
    for step in range(COARSE_ITERS):
        image = operate(search)
        alpha = norm / dot(search, image)
        answer = [a + alpha * s for a, s in zip(answer, search)]
        if step == COARSE_ITERS - 1:
            break
        resid = [r - alpha * m for r, m in zip(resid, image)]
        norm_next = dot(resid, resid)
        beta = norm_next / norm
        search = [r + beta * s for r, s in zip(resid, search)]
        norm = norm_next
    return answer


def last_kernel(nd, nc, tiles, got, src, gain, wx, wy, wz, state, out, bricks, pres, third):
    rows, cols, layers = out.shape
    tile_w = cols // tiles
    body_rows = 2 * tile_w
    down, cross = lax.axis_index("down"), lax.axis_index("cross")
    own = slice(STRIP, STRIP + cols)

    last = iota((nd, 128), 0) == nd - 1
    totals = [got[:, c, body_rows, :] for c in range(nc)]
    link_down = [jnp.where(last, 0.0, got[:, c, body_rows + 1, :]) for c in range(nc)]
    link_up = [roll(link, 1, 0) for link in link_down]
    link_cross = [got[:, c, body_rows + 2, :] for c in range(nc)]
    outflow = [got[:, c, body_rows + 3, :] for c in range(nc)]
    answer = coarse_solve(totals, outflow, link_down, link_up, link_cross)
    for c in range(nc):
        bricks[c] = answer[c]

    lanes = iota((tile_w, layers), 1) % 2
    sublanes = iota((tile_w, layers), 0) % 2

    def neighbour(dx, dy):
        there = jnp.bool_(True)
        if dx:
            there = there & ((down > 0) if dx < 0 else (down < nd - 1))
        if dy:
            there = there & ((cross > 0) if dy < 0 else (cross < nc - 1))
        row = jnp.clip(down + dx, 0, nd - 1)
        col = jnp.clip(cross + dy, 0, nc - 1)
        line = bricks[col, pl.ds(row, 1), :]
        brick = jnp.concatenate([line] * (layers // 128), axis=1)
        packed = jnp.concatenate(
            [got[row, col, :tile_w, :], got[row, col, tile_w:body_rows, :]], axis=1
        )
        return there, brick, packed

    def unpack_row(packed):
        parts = []
        for sub in (0, 1):
            tall = jnp.where(sublanes == sub, packed, roll(packed, 1 if sub == 0 else -1, 0))
            for lan in (0, 1):
                parts.append(jnp.where(lanes == lan, tall, roll(tall, 1 if lan == 0 else -1, 1)))
        return jnp.concatenate(parts, axis=0)

    mine = jnp.concatenate([bricks[cross, pl.ds(down, 1), :]] * (layers // 128), axis=1)
    for i in range(2, rows + 2):
        pres[i, own, :] = state[i, own, :] + mine
    for dx, at in ((-1, 0), (1, rows + 2)):
        there, brick, packed = neighbour(dx, 0)
        extra = jnp.where(there, unpack_row(packed) + brick, 0.0)
        for i in (at, at + 1):
            pres[i, own, :] = state[i, own, :] + extra
    for dy, start in ((-1, 0), (1, STRIP + cols)):
        strip = slice(start, start + STRIP)
        there, brick, packed = neighbour(0, dy)
        for k in range(rows // 2):
            line = packed[2 * k : 2 * k + 1] + brick
            extra = jnp.where(there, jnp.broadcast_to(line, (STRIP, layers)), 0.0)
            for i in (2 * k + 2, 2 * k + 3):
                pres[i, strip, :] = state[i, strip, :] + extra
        for dx, at in ((-1, 0), (1, rows + 2)):
            there, brick, packed = neighbour(dx, dy)
            extra = jnp.where(there, jnp.broadcast_to(packed[0:1] + brick, (STRIP, layers)), 0.0)
            for i in (at, at + 1):
                pres[i, strip, :] = state[i, strip, :] + extra

    for i in range(rows + 2):
        spread = gather(pres, (i, i + 1, i + 2), wx, i + 2, wy[i + 1], wz[i + 1])
        third[i] = KEEP * pres[i + 1] + gain[i + 2] * (src[i + 2] + spread)
    for x in range(rows):
        spread = gather(third, (x, x + 1, x + 2), wx, x + 3, wy[x + 2], wz[x + 2])
        new = KEEP * third[x + 1] + gain[x + 3] * (src[x + 3] + spread)
        out[x] = new[own]


def whole(shape):
    return jax.ShapeDtypeStruct(shape, FLOAT)


def call(kernel, out_shape, n_in, scratch=(), smem=()):
    return pl.pallas_call(
        kernel,
        out_shape=out_shape,
        in_specs=[
            pl.BlockSpec(memory_space=pltpu.SMEM if i in smem else pltpu.VMEM) for i in range(n_in)
        ],
        out_specs=jax.tree.map(lambda _: pl.BlockSpec(memory_space=pltpu.VMEM), out_shape),
        scratch_shapes=list(scratch),
        compiler_params=pltpu.CompilerParams(vmem_limit_bytes=VMEM_BYTES),
    )


def body(nd, nc, right_side, kappa, band_mask, tile_route):
    rows, cols, layers = right_side.shape
    tiles = tile_route.shape[1]
    axes = ("down", "cross")
    wide = cols + 2 * STRIP

    shapes, perms = [], []
    for kind in pairings(nd):
        shapes.append((2 * DEPTH - 1, cols, layers))
        perms.append(pairs_of(nd, nc, kind, None))
    for cross_kind in pairings(nc):
        shapes.append((2 * rows, STRIP, layers))
        perms.append(pairs_of(nd, nc, None, cross_kind))
        for kind in pairings(nd):
            shapes.append((2 * DEPTH - 3, STRIP, layers))
            perms.append(pairs_of(nd, nc, kind, cross_kind))
    conduct, *messages = call(
        functools.partial(pack_kernel, nd, nc),
        [whole((rows, cols, layers))] + [whole(s) for s in shapes],
        3,
    )(right_side, kappa, band_mask)
    received = [lax.ppermute(m, axes, p) for m, p in zip(messages, perms)]

    body_rows = 2 * (cols // tiles)
    heights = (rows + 6, rows + 6, rows + 5, rows + 4, rows + 4, rows + 4)
    *kept, chunks = call(
        functools.partial(main_kernel, nd, nc),
        [whole((h, wide, layers)) for h in heights] + [whole((nd * nc, body_rows + 8, 128))],
        3 + len(received),
        scratch=[
            pltpu.VMEM((h, wide, layers), FLOAT) for h in (rows + 8, rows + 6, rows + 4)
        ],
        smem=(2,),
    )(right_side, conduct, tile_route, *received)
    arrived = lax.all_to_all(chunks, axes, 0, 0, tiled=True).reshape(nd, nc, body_rows + 8, 128)
    return call(
        functools.partial(last_kernel, nd, nc, tiles),
        whole((rows, cols, layers)),
        1 + len(kept),
        scratch=[
            pltpu.VMEM((nc, nd, 128), FLOAT),
            pltpu.VMEM((rows + 4, wide, layers), FLOAT),
            pltpu.VMEM((rows + 2, wide, layers), FLOAT),
        ],
    )(arrived, *kept)


def solution(mesh):
    return jax.shard_map(
        functools.partial(body, mesh.shape["down"], mesh.shape["cross"]),
        mesh=mesh,
        in_specs=(
            P("down", "cross", None),
            P("down", "cross", None),
            P("down", "cross", None),
            P("down", "cross"),
        ),
        out_specs=P("down", "cross", None),
        check_vma=False,
    )
```

time: 236 us -> 38.5 us (0.16)
  local copies, waits for them, and re-layouts: 64.1 us -> 2.85 us
  other arithmetic: 44.6 us -> 0 us
  starting transfers between devices: 34.5 us -> 7.97 us
  blocking collectives: 42.8 us -> 19.2 us
  loops' own time: 23.5 us -> 0 us
  waiting for transfers between devices: 19.4 us -> 2.67 us
  Pallas kernels: 0 us -> 5.31 us
  between operations: 3.59 us -> 0.04 us
    reshape x6 -> x0, local copies, waits for them, and re-layouts: 50.3 us -> none  [the longest x1 18.1 us: block_mean(): fine.reshape(rows_here // 2, 2, cols_here // 2, 2, layers // 2, 2)]
    unnamed x1 -> x0, blocking collectives: 42.8 us -> none
    reduce_sum x38 -> x0, other arithmetic: 35.4 us -> none  [the longest x12 8.53 us: sweep(): alpha = norm_now / jnp.sum(search * image)]
    another operation x1 -> x0, loops' own time: 23.5 us -> none  [coarse_solve(): return lax.fori_loop(0, COARSE_ITERS, sweep, start)[0]]
    all_to_all x0 -> x1, blocking collectives: none -> 19.2 us  [body(): lax.all_to_all(chunks, axes, 0, 0, tiled=True)]
    ppermute x12 -> x5, starting transfers between devices: 24.1 us -> 7.97 us  [body(): received = [lax.ppermute(m, axes, p) for m, p in zip(messages, perms)]]
    ppermute x12 -> x5, waiting for transfers between devices: 16.6 us -> 2.67 us  [body(): received = [lax.ppermute(m, axes, p) for m, p in zip(messages, perms)]]
    all_to_all x3 -> x0, starting transfers between devices: 10.4 us -> none  [the longest x1 3.59 us: body(): lax.all_to_all(send_con, 'cross', split_axis=0, concat_axis=0, tiled=True)]
  transfers between devices with their start and end apart: 15 -> 5, of which waited for: 7 -> 2; matrix products, arithmetic and copies ran while one was open for 36% -> 0% of each run, Pallas kernels for 0% -> 0%
where the time goes in v1:
time: 38.5 us; the launch traced here: 38 us
  blocking collectives  19.2 us (50%)
  starting transfers between devices  7.97 us (21%)
  Pallas kernels  5.31 us (14%)
  local copies, waits for them, and re-layouts  2.85 us (7%)
  waiting for transfers between devices  2.67 us (7%)
    all_to_all x1, blocking collectives, body(): lax.all_to_all(chunks, axes, 0, 0, tiled=True)  19.2 us
    ppermute x5, starting transfers between devices, body(): received = [lax.ppermute(m, axes, p) for m, p in zip(messages, perms)]  7.97 us
    pallas_call x1, Pallas kernels, body(): call(functools.partial(main_kernel, nd, nc), [whole((h, wide, layers)) fo...  3.26 us
    unnamed x8, local copies, waits for them, and re-layouts  2.85 us
    ppermute x5, waiting for transfers between devices, body(): received = [lax.ppermute(m, axes, p) for m, p in zip(messages, perms)]  2.67 us
    pallas_call x1, Pallas kernels, body(): call(functools.partial(last_kernel, nd, nc, tiles), whole((rows, cols, la...  1.93 us
  transfers between devices with their start and end apart: 5, of which 2 were waited for; matrix products, arithmetic and copies ran while one was open for 0% of the time, Pallas kernels for 0%

profile of v1, /device:TPU:0, one launch (start us, length us, event | category | flops | bytes accessed | tf_op | source)
XLA Modules:
  0.0 38.0 jit_solution(15937387811038739167)
XLA Ops:
  0.0 0.0 copy-start
  0.0 0.9 %copy-done = f32[8,32,256]{2,1,0:T(8,128)S(1)} copy-done((f32[8,32,256]{2,1,0:T(8,128)S(1)}, f32[8,32,256]{2,1,0:T(8,128)}, u32[]{:S(2)}) %copy-start) | copy-done | bytes 262168
  1.0 0.0 copy-start.1
  1.0 0.9 %copy-done.1 = f32[8,32,256]{2,1,0:T(8,128)S(1)} copy-done((f32[8,32,256]{2,1,0:T(8,128)S(1)}, f32[8,32,256]{2,1,0:T(8,128)}, u32[]{:S(2)}) %copy-start.1) | copy-done | bytes 262168
  1.9 0.0 copy-start.2
  1.9 0.9 %copy-done.2 = s32[8,32,256]{2,1,0:T(8,128)S(1)} copy-done((s32[8,32,256]{2,1,0:T(8,128)S(1)}, s32[8,32,256]{2,1,0:T(8,128)}, u32[]{:S(2)}) %copy-start.2) | copy-done | bytes 262168
  2.9 0.1 shard_map.46
  3.0 0.5 %collective-permute-start = (f32[7,32,256]{2,1,0:T(8,128)S(1)}, f32[7,32,256]{2,1,0:T(8,128)S(1)}, u32[]{:S(2)}, u32[]{:S(2)}) collective-permute-start(f32[7,32,256]{2,1,0:T(8,128)S(1)} %get-tuple-element.19), channel_id=1, source_target_pairs={{0,2},{1,3},{2,0},{3,1},{4,6},{5,7},{6,4},{7,5},{8,10},{9,11},{10,... | collective-permute-start | bytes 688136 | tf_op jit(solution)/shard_map/ppermute | solution.py:470
  3.5 0.7 %collective-permute-start.1 = (f32[7,32,256]{2,1,0:T(8,128)S(1)}, f32[7,32,256]{2,1,0:T(8,128)S(1)}, u32[]{:S(2)}, u32[]{:S(2)}) collective-permute-start(f32[7,32,256]{2,1,0:T(8,128)S(1)} %get-tuple-element.20), channel_id=1, source_target_pairs={{0,0},{1,1},{2,4},{3,5},{4,2},{5,3},{6,8},{7,9},{8,6},{9,7},{10,12... | collective-permute-start | bytes 688136 | tf_op jit(solution)/shard_map/ppermute | solution.py:470
  4.2 2.6 %collective-permute-start.2 = (f32[16,8,256]{2,1,0:T(8,128)S(1)}, f32[16,8,256]{2,1,0:T(8,128)S(1)}, u32[]{:S(2)}, u32[]{:S(2)}) collective-permute-start(f32[16,8,256]{2,1,0:T(8,128)S(1)} %get-tuple-element.21), channel_id=1, source_target_pairs={{0,1},{1,0},{2,3},{3,2},{4,5},{5,4},{6,7},{7,6},{8,9},{9,8},{10,11... | collective-permute-start | bytes 393224 | tf_op jit(solution)/shard_map/ppermute | solution.py:470
  6.7 2.7 %collective-permute-start.3 = (f32[5,8,256]{2,1,0:T(8,128)S(1)}, f32[5,8,256]{2,1,0:T(8,128)S(1)}, u32[]{:S(2)}, u32[]{:S(2)}) collective-permute-start(f32[5,8,256]{2,1,0:T(8,128)S(1)} %get-tuple-element.22), channel_id=1, source_target_pairs={{0,3},{1,2},{2,1},{3,0},{4,7},{5,6},{6,5},{7,4},{8,11},{9,10},{10,... | collective-permute-start | bytes 122888 | tf_op jit(solution)/shard_map/ppermute | solution.py:470
  9.5 0.0 copy-start.3
  9.5 1.5 %collective-permute-start.4 = (f32[5,8,256]{2,1,0:T(8,128)S(1)}, f32[5,8,256]{2,1,0:T(8,128)S(1)}, u32[]{:S(2)}, u32[]{:S(2)}) collective-permute-start(f32[5,8,256]{2,1,0:T(8,128)S(1)} %get-tuple-element.23), channel_id=1, source_target_pairs={{0,1},{1,0},{2,5},{3,4},{4,3},{5,2},{6,9},{7,8},{8,7},{9,6},{10,13... | collective-permute-start | bytes 122888 | tf_op jit(solution)/shard_map/ppermute | solution.py:470
  10.9 1.6 %collective-permute-done.3.refs_3_ = f32[5,8,256]{2,1,0:T(8,128)S(1)} collective-permute-done((f32[5,8,256]{2,1,0:T(8,128)S(1)}, f32[5,8,256]{2,1,0:T(8,128)S(1)}, u32[]{:S(2)}, u32[]{:S(2)}) %collective-permute-start.3) | collective-permute-done | bytes 40992 | tf_op jit(solution)/shard_map/ppermute | solution.py:470
  12.5 1.1 %collective-permute-done.4.refs_4_ = f32[5,8,256]{2,1,0:T(8,128)S(1)} collective-permute-done((f32[5,8,256]{2,1,0:T(8,128)S(1)}, f32[5,8,256]{2,1,0:T(8,128)S(1)}, u32[]{:S(2)}, u32[]{:S(2)}) %collective-permute-start.4) | collective-permute-done | bytes 40992 | tf_op jit(solution)/shard_map/ppermute | solution.py:470
  13.6 0.0 collective-permute-done.2.refs_2_
  13.6 0.0 collective-permute-done.refs_0_
  13.6 0.0 collective-permute-done.1.refs_1_
  13.6 0.0 copy-done.3
  13.6 3.3 %shard_map.47 = (f32[14,48,256]{2,1,0:T(8,128)S(1)}, f32[14,48,256]{2,1,0:T(8,128)S(1)}, f32[13,48,256]{2,1,0:T(8,128)S(1)}, f32[12,48,256]{2,1,0:T(8,128)S(1)},...) custom-call(f32[8,32,256]{2,1,0:T(8,128)S(1)} %copy-done, ...), custom_call_target="tpu_custom_call" | custom-call | tf_op jit(solution)/shard_map/pallas_call | solution.py:474
  16.9 19.2 %all_to_all.5 = f32[32,24,128]{2,1,0:T(8,128)S(1)} all-to-all(f32[32,24,128]{2,1,0:T(8,128)S(1)} %get-tuple-element.24), channel_id=1, replica_groups=mesh['down'=16,'cross'=2] {'down','cross'}, dimensions={0} | all-to-all | bytes 786432 | tf_op jit(solution)/shard_map/all_to_all | solution.py:483
  36.1 1.9 %shard_map.48 = f32[8,32,256]{2,1,0:T(8,128)} custom-call(f32[16,2,24,128]{3,2,1,0:T(8,128)S(1)} %bitcast.1, f32[14,48,256]{2,1,0:T(8,128)S(1)} %get-tuple-element.25.src, f32[14,48,256]{2,1,0:T(8,128)S(1)} %get-tuple-element.26.gain, f32[13,48,256]{2,1,0:T(8,128)S(1)} %get-tuple-element.27.wx, f32[12,48,256]{2,1,0:T(8,128)S(1)} %get-tuple-element.28.wy, ...), custom_call_target="tpu_custom_call" | custom-call | tf_op jit(solution)/shard_map/pallas_call | solution.py:484
Async XLA Ops:
  0.0 0.9 %copy-start = (f32[8,32,256]{2,1,0:T(8,128)S(1)}, f32[8,32,256]{2,1,0:T(8,128)}, u32[]{:S(2)}) copy-start(f32[8,32,256]{2,1,0:T(8,128)} %rhs.3) | copy-start | bytes 786436
  1.0 0.9 %copy-start.1 = (f32[8,32,256]{2,1,0:T(8,128)S(1)}, f32[8,32,256]{2,1,0:T(8,128)}, u32[]{:S(2)}) copy-start(f32[8,32,256]{2,1,0:T(8,128)} %kappa.1) | copy-start | bytes 786436
  1.9 0.9 %copy-start.2 = (s32[8,32,256]{2,1,0:T(8,128)S(1)}, s32[8,32,256]{2,1,0:T(8,128)}, u32[]{:S(2)}) copy-start(s32[8,32,256]{2,1,0:T(8,128)} %mask.1) | copy-start | bytes 786436
  3.0 10.6 %collective-permute-start = (f32[7,32,256]{2,1,0:T(8,128)S(1)}, f32[7,32,256]{2,1,0:T(8,128)S(1)}, u32[]{:S(2)}, u32[]{:S(2)}) collective-permute-start(f32[7,32,256]{2,1,0:T(8,128)S(1)} %get-tuple-element.19), channel_id=1, source_target_pairs={{0,2},{1,3},{2,0},{3,1},{4,6},{5,7},{6,4},{7,5},{8,10},{9,11},{10,... | collective-permute-start | bytes 688136 | tf_op jit(solution)/shard_map/ppermute | solution.py:470
  3.5 10.1 %collective-permute-start.1 = (f32[7,32,256]{2,1,0:T(8,128)S(1)}, f32[7,32,256]{2,1,0:T(8,128)S(1)}, u32[]{:S(2)}, u32[]{:S(2)}) collective-permute-start(f32[7,32,256]{2,1,0:T(8,128)S(1)} %get-tuple-element.20), channel_id=1, source_target_pairs={{0,0},{1,1},{2,4},{3,5},{4,2},{5,3},{6,8},{7,9},{8,6},{9,7},{10,12... | collective-permute-start | bytes 688136 | tf_op jit(solution)/shard_map/ppermute | solution.py:470
  4.2 9.5 %collective-permute-start.2 = (f32[16,8,256]{2,1,0:T(8,128)S(1)}, f32[16,8,256]{2,1,0:T(8,128)S(1)}, u32[]{:S(2)}, u32[]{:S(2)}) collective-permute-start(f32[16,8,256]{2,1,0:T(8,128)S(1)} %get-tuple-element.21), channel_id=1, source_target_pairs={{0,1},{1,0},{2,3},{3,2},{4,5},{5,4},{6,7},{7,6},{8,9},{9,8},{10,11... | collective-permute-start | bytes 393224 | tf_op jit(solution)/shard_map/ppermute | solution.py:470
  6.7 5.8 %collective-permute-start.3 = (f32[5,8,256]{2,1,0:T(8,128)S(1)}, f32[5,8,256]{2,1,0:T(8,128)S(1)}, u32[]{:S(2)}, u32[]{:S(2)}) collective-permute-start(f32[5,8,256]{2,1,0:T(8,128)S(1)} %get-tuple-element.22), channel_id=1, source_target_pairs={{0,3},{1,2},{2,1},{3,0},{4,7},{5,6},{6,5},{7,4},{8,11},{9,10},{10,... | collective-permute-start | bytes 122888 | tf_op jit(solution)/shard_map/ppermute | solution.py:470
  9.5 4.2 %copy-start.3 = (s32[1,4]{1,0:T(1,128)S(1)}, s32[1,4]{1,0:T(1,128)}, u32[]{:S(2)}) copy-start(s32[1,4]{1,0:T(1,128)} %route.1) | copy-start | bytes 52
  9.5 4.1 %collective-permute-start.4 = (f32[5,8,256]{2,1,0:T(8,128)S(1)}, f32[5,8,256]{2,1,0:T(8,128)S(1)}, u32[]{:S(2)}, u32[]{:S(2)}) collective-permute-start(f32[5,8,256]{2,1,0:T(8,128)S(1)} %get-tuple-element.23), channel_id=1, source_target_pairs={{0,1},{1,0},{2,5},{3,4},{4,3},{5,2},{6,9},{7,8},{8,7},{9,6},{10,13... | collective-permute-start | bytes 122888 | tf_op jit(solution)/shard_map/ppermute | solution.py:470

commit v2 on v1

v2 whole, which is shorter than its diff:
```python
import functools

import jax
import jax.numpy as jnp
from jax import lax
from jax.experimental import pallas as pl
from jax.experimental.pallas import tpu as pltpu
from jax.sharding import PartitionSpec as P

BLOCK_SWEEPS = 4
COARSE_ITERS = 12
OMEGA = 0.8
KEEP = 1.0 - OMEGA
SNOW_FACTOR = 3.0

DEPTH = 4
CORNER = 2 * DEPTH - 3
STRIP = 8
LANES = 128
HALF = 8
CHUNK = HALF + 1
FLOAT = jnp.float32
VMEM_BYTES = 48 * 1024 * 1024


def partners(count, odd):
    found = []
    for i in range(count):
        j = ((i + 1) ^ 1) - 1 if odd else i ^ 1
        found.append(j if 0 <= j < count else i)
    return found


def pairings(count):
    return [k for k in (False, True) if any(j != i for i, j in enumerate(partners(count, k)))]


def pairs_of(count_down, count_cross, down_kind, cross_kind):
    rows = list(range(count_down)) if down_kind is None else partners(count_down, down_kind)
    cols = list(range(count_cross)) if cross_kind is None else partners(count_cross, cross_kind)
    return [
        (i * count_cross + j, rows[i] * count_cross + cols[j])
        for i in range(count_down)
        for j in range(count_cross)
    ]


def facing(index, count, kind):
    ahead = (index % 2 == 0) != kind
    return ahead, jnp.where(ahead, index < count - 1, index > 0)


def beside(index, count, step):
    return (index + step >= 0) & (index + step < count)


def roll(x, amount, axis):
    return pltpu.roll(x, amount % x.shape[axis], axis)


def iota(shape, axis):
    return lax.broadcasted_iota(jnp.int32, shape, axis)


def gather(field, here, wx, wx_at, wy, wz):
    value = field[here]
    total = wx[wx_at] * field[here + 1] + wx[wx_at - 1] * field[here - 1]
    total = total + wy * roll(value, -1, 0) + roll(wy * value, 1, 0)
    return total + wz * roll(value, -1, 1) + roll(wz * value, 1, 1)


def edge_rows(ahead, rows, depth):
    return pl.ds(jnp.where(ahead, rows - depth, 0), depth)


def edge_strip(right, cols):
    return pl.ds(pl.multiple_of(jnp.where(right, cols - STRIP, 0), STRIP), STRIP)


def pack_kernel(nd, nc, rhs_hbm, kappa_hbm, mask_hbm, conduct, *refs):
    *messages, rhs, kappa, mask, sems = refs
    rows, cols, _ = rhs.shape
    messages = iter(messages)
    down, cross = lax.axis_index("down"), lax.axis_index("cross")
    copies = [
        pltpu.make_async_copy(src, dst, sems.at[i])
        for i, (src, dst) in enumerate(((kappa_hbm, kappa), (mask_hbm, mask), (rhs_hbm, rhs)))
    ]
    for copy in copies:
        copy.start()
    copies[0].wait()
    copies[1].wait()
    for x in range(rows):
        conduct[x] = kappa[x] / (1.0 + SNOW_FACTOR * mask[x].astype(FLOAT))
    copies[2].wait()
    for kind in pairings(nd):
        ahead, _ = facing(down, nd, kind)
        out = next(messages)
        out[:DEPTH] = conduct[edge_rows(ahead, rows, DEPTH)]
        out[DEPTH:] = rhs[edge_rows(ahead, rows, DEPTH - 1)]
        if kind:
            for cross_kind in pairings(nc):
                right, _ = facing(cross, nc, cross_kind)
                strip = edge_strip(right, cols)
                out = next(messages)
                out[: DEPTH - 1] = conduct[edge_rows(ahead, rows, DEPTH - 1), strip, :]
                out[DEPTH - 1 :] = rhs[edge_rows(ahead, rows, DEPTH - 2), strip, :]
    for cross_kind in pairings(nc):
        right, _ = facing(cross, nc, cross_kind)
        strip = edge_strip(right, cols)
        out = next(messages)
        out[:rows] = conduct[:, strip, :]
        out[rows:] = rhs[:, strip, :]


def strip_kernel(nd, nc, even, *refs):
    cols = even.shape[1]
    count = len(pairings(nc))
    ahead, _ = facing(lax.axis_index("down"), nd, False)
    for cross_kind, own, out in zip(pairings(nc), refs[:count], refs[count:]):
        right, _ = facing(lax.axis_index("cross"), nc, cross_kind)
        strip = edge_strip(right, cols)
        rows = own.shape[0] // 2
        out[: 2 * rows] = own[...]
        out[2 * rows : 2 * rows + DEPTH - 1] = even[pl.ds(jnp.where(ahead, 0, 1), DEPTH - 1), strip, :]
        out[2 * rows + DEPTH - 1 :] = even[
            pl.ds(jnp.where(ahead, DEPTH, DEPTH + 1), DEPTH - 2), strip, :
        ]


def fold(x):
    x = sum(x[:, i : i + LANES] for i in range(0, x.shape[1], LANES))
    return jnp.sum(x, axis=0, keepdims=True)


def swap_pairs(x, axis):
    return jnp.where(iota(x.shape, axis) % 2 == 0, roll(x, -1, axis), roll(x, 1, axis))


def pack_pairs(a, b, axis):
    even = iota(a.shape, axis) % 2 == 0
    return jnp.where(even, a, b) + swap_pairs(jnp.where(even, b, a), axis)


def unpack_pairs(x, axis):
    even = iota(x.shape, axis) % 2 == 0
    return jnp.where(even, x, roll(x, 1, axis)), jnp.where(even, roll(x, -1, axis), x)


def main_kernel(nd, nc, rhs, conduct, route, *refs):
    rows, cols, layers = rhs.shape
    tiles = route.shape[1]
    tile_w = cols // tiles
    n_down, n_cross = len(pairings(nd)), len(pairings(nc))
    n_messages = n_down + n_cross * n_down
    vertical = refs[:n_down]
    corners = refs[n_down : n_down + n_cross * (n_down - 1)]
    strips = refs[n_down + n_cross * (n_down - 1) : n_messages]
    src, gain, wx, wy, wz, state, swapped, chunks, q, first, pres, diag = refs[n_messages:]
    down, cross = lax.axis_index("down"), lax.axis_index("cross")
    wide = cols + STRIP
    own, halo = slice(0, cols), slice(cols, wide)

    if n_down < 2:
        q[...] = jnp.zeros(q.shape, FLOAT)
        src[...] = jnp.zeros(src.shape, FLOAT)
    else:
        for ref in (q, src):
            for i in (0, ref.shape[0] - 1):
                ref[i, halo, :] = jnp.zeros((STRIP, layers), FLOAT)
    q[DEPTH : DEPTH + rows, own, :] = conduct[...]
    src[DEPTH - 1 : DEPTH - 1 + rows, own, :] = rhs[...]
    halo_col = iota((STRIP, layers), 0)
    sides = []
    for cross_kind in pairings(nc):
        right, valid = facing(cross, nc, cross_kind)
        start = jnp.where(right, 0, STRIP // 2)
        stop = jnp.where(valid, start + STRIP // 2, 0)
        sides.append((halo_col >= start) & (halo_col < stop))

    def merged(parts, valid=None):
        total = jnp.zeros((STRIP, layers), FLOAT)
        for side, part in zip(sides, parts):
            total = jnp.where(side if valid is None else side & valid, part, total)
        return total

    for x in range(rows):
        q[DEPTH + x, halo, :] = merged([s[x] for s in strips])
        src[DEPTH - 1 + x, halo, :] = merged([s[rows + x] for s in strips])
    for at, kind in enumerate(pairings(nd)):
        ahead, valid = facing(down, nd, kind)
        got = vertical[at]
        q_at = jnp.where(ahead, DEPTH + rows, 0)
        src_at = jnp.where(ahead, DEPTH - 1 + rows, 0)
        q[pl.ds(q_at, DEPTH), own, :] = jnp.where(valid, got[:DEPTH], 0.0)
        src[pl.ds(src_at, DEPTH - 1), own, :] = jnp.where(valid, got[DEPTH:], 0.0)
        nearer = jnp.where(ahead, 0, 1)
        parts, start = (corners, 0) if kind else (strips, 2 * rows)
        for i in range(DEPTH - 1):
            q[q_at + nearer + i, halo, :] = merged([p[start + i] for p in parts], valid)
        for i in range(DEPTH - 2):
            src[src_at + nearer + i, halo, :] = merged([p[start + DEPTH - 1 + i] for p in parts], valid)

    lane = iota((wide, layers), 1)
    col = iota((wide, layers), 0)
    last_lane = lane == layers - 1
    middle_col = cols + STRIP // 2
    col_ok = (col < jnp.where(cross < nc - 1, middle_col, cols)) | (
        col >= jnp.where(cross > 0, middle_col, wide)
    )

    for i in range(rows + 2 * (DEPTH - 1)):
        x = i - (DEPTH - 1)
        here = q[i + 1]
        ahead = q[i + 2]
        above = jnp.where(last_lane, 0.0, roll(here, -1, 1))
        below = jnp.where(lane == 0, 0.0, roll(here, 1, 1))
        right = roll(here, -1, 0)
        doubled = 6.0 * here + (q[i] + ahead) + (right + roll(here, 1, 0)) + (above + below)
        ok = col_ok & (doubled > 0.0)
        if x < 0:
            ok = ok & (down > 0)
        if x >= rows:
            ok = ok & (down < nd - 1)
        gain_here = jnp.where(ok, (2.0 * OMEGA) / doubled, 0.0)
        gain[i] = gain_here
        first[i] = gain_here * src[i]
        if 0 <= x < rows:
            diag[x] = 0.5 * doubled
        if i < wx.shape[0]:
            wx[i] = 0.5 * (here + ahead)
        if -2 <= x < rows + 2:
            wy[x + 2] = 0.5 * (here + right)
            wz[x + 2] = jnp.where(last_lane, 0.0, 0.5 * (here + above))

    for i in range(rows + 4):
        spread = gather(first, i + 1, wx, i + 1, wy[i], wz[i])
        pres[i] = KEEP * first[i + 1] + gain[i + 1] * (src[i + 1] + spread)

    res_rows, con_rows = [], []
    for k in range(rows // 2):
        pair = None
        for x in (2 * k, 2 * k + 1):
            i = x + 2
            spread = gather(pres, i, wx, i + 1, wy[i], wz[i])
            res = (src[x + DEPTH - 1] - diag[x] * pres[i] + spread)[own]
            pair = res if pair is None else pair + res
        res_rows.append(pair)
        con_rows.append(0.125 * (q[2 * k + DEPTH, own, :] + q[2 * k + 1 + DEPTH, own, :]))

    strip_col = iota((STRIP, layers), 0)
    plane = sum(q[x + DEPTH, own, :] for x in range(rows))
    beyond = sum(q[x + DEPTH, halo, :] for x in range(rows))
    own_lane = iota((cols, layers), 1)
    low, high = strip_col < 2, strip_col >= STRIP - 2
    ends = fold(jnp.where((own_lane < 2) | (own_lane >= layers - 2), plane, 0.0))
    link_back = fold(jnp.where(low, plane[:STRIP], 0.0) + jnp.where(high, beyond, 0.0))
    link_cross = fold(jnp.where(high, plane[cols - STRIP :], 0.0) + jnp.where(low, beyond, 0.0))
    link_up = fold(sum(q[DEPTH + x, own, :] for x in range(-2, 2)))
    link_down = fold(sum(q[DEPTH + x, own, :] for x in range(rows - 2, rows + 2)))
    outflow = link_down + link_up + link_cross + link_back + ends
    sums = jnp.concatenate([fold(sum(res_rows)), 0.25 * link_down, 0.25 * link_cross, 0.25 * outflow])
    sums = jnp.sum(sums, axis=1, keepdims=True)
    line = iota((1, LANES), 1)
    summary = jnp.where(
        line == 0, sums[0:1], jnp.where(line == 1, sums[1:2], jnp.where(line == 2, sums[2:3], sums[3:4]))
    )

    packs = rows // 4
    couples = tiles // 2
    shape = (couples, tile_w, layers)

    def coarse(lists):
        by_row = []
        for x in lists:
            t = x.reshape(couples, 2, tile_w, layers)
            by_row.append(pack_pairs(t[:, 0], t[:, 1], 2))
        return [pack_pairs(by_row[k], by_row[k + packs], 1) for k in range(packs)]

    res, con = coarse(res_rows), coarse(con_rows)
    tile_col, tile_lane = iota(shape, 1), iota(shape, 2)
    even_col = tile_col % 2 == 0
    y_end, y_start = tile_col >= tile_w - 2, tile_col < 2
    z_end, z_start = tile_lane >= layers - 2, tile_lane < 2
    link_x = [2.0 * (con[k] + con[k + 1]) for k in range(packs - 1)]
    middle = 2.0 * (con[packs - 1] + roll(con[0], -1, 1))
    middle_low = jnp.where(even_col, middle, 0.0)
    middle_high = jnp.where(even_col, 0.0, roll(middle, 1, 1))
    link_y, link_z, tile_gain = [], [], []
    for k in range(packs):
        c = con[k]
        y_high = jnp.where(y_end, 0.0, roll(c, -2, 1))
        z_high = jnp.where(z_end, 0.0, roll(c, -2, 2))
        y_low = jnp.where(y_start, 0.0, roll(c, 2, 1))
        z_low = jnp.where(z_start, 0.0, roll(c, 2, 2))
        total = 6.0 * c + (y_high + y_low) + (z_high + z_low)
        if k > 0:
            total = total + con[k - 1]
        else:
            total = total + jnp.where(even_col, 0.0, roll(con[packs - 1], 1, 1))
        if k < packs - 1:
            total = total + con[k + 1]
        else:
            total = total + jnp.where(even_col, roll(con[0], -1, 1), 0.0)
        total = 2.0 * total
        tile_gain.append(OMEGA / jnp.where(total > 0.0, total, 1.0))
        link_y.append(jnp.where(y_end, 0.0, 2.0 * (c + y_high)))
        link_z.append(jnp.where(z_end, 0.0, 2.0 * (c + z_high)))
    fix = [tile_gain[k] * res[k] for k in range(packs)]
    for _ in range(BLOCK_SWEEPS - 1):
        updated = []
        for k in range(packs):
            value = fix[k]
            acc = res[k] + link_y[k] * roll(value, -2, 1) + roll(link_y[k] * value, 2, 1)
            acc = acc + link_z[k] * roll(value, -2, 2) + roll(link_z[k] * value, 2, 2)
            if k > 0:
                acc = acc + link_x[k - 1] * fix[k - 1]
            else:
                acc = acc + middle_high * roll(fix[packs - 1], 1, 1)
            if k < packs - 1:
                acc = acc + link_x[k] * fix[k + 1]
            else:
                acc = acc + middle_low * roll(fix[0], -1, 1)
            updated.append(KEEP * value + tile_gain[k] * acc)
        fix = updated
    flat_lane = iota((tile_w, layers), 1) % 2 == 0
    touched = jnp.stack(
        [
            jnp.where(flat_lane, route[0, 2 * t], route[0, 2 * t + 1]) >= 0
            for t in range(couples)
        ]
    )
    fix = [jnp.where(touched, f, 0.0) for f in fix]

    fine = [None] * (rows // 2)
    for k in range(packs):
        for j, part in enumerate(unpack_pairs(fix[k], 1)):
            both = unpack_pairs(part, 2)
            fine[k + j * packs] = jnp.stack(both, axis=1).reshape(cols, layers)

    for i in range(rows + 4):
        if 2 <= i < rows + 2:
            state[i, own, :] = pres[i, own, :] + fine[(i - 2) // 2]
            state[i, halo, :] = pres[i, halo, :]
        else:
            state[i] = pres[i]

    pair_col = iota((tile_w, layers), 0)
    rim_shape = (tile_w, layers)

    def rim(row):
        f = fine[row].reshape(couples, 2, tile_w, layers)
        by_lane = [jnp.where(flat_lane, f[t, 0], f[t, 1]) for t in range(couples)]
        out = by_lane[0]
        for t in range(1, couples):
            out = jnp.where(pair_col % couples == t, by_lane[t], out)
        return out[:, :LANES], out[:, LANES:]

    rims = [rim(0), rim(rows // 2 - 1)]
    even_ahead, _ = facing(down, nd, False)
    even_rim = [jnp.where(even_ahead, b, a) for a, b in zip(*rims)]
    odd_rim = [jnp.where(even_ahead, a, b) for a, b in zip(*rims)]
    swapped[:HALF] = even_rim[0]
    swapped[HALF : 2 * HALF] = even_rim[1]
    swapped[2 * HALF :] = odd_rim[1]

    blank = jnp.zeros((HALF, LANES), FLOAT)

    def fill(b, carry):
        at = b * CHUNK
        chunks[pl.ds(at, HALF), :] = blank
        chunks[pl.ds(at + HALF, 1), :] = summary
        return carry

    lax.fori_loop(0, nd * nc, fill, 0)
    me = down * nc + cross
    if n_down > 1:
        step = jnp.where(even_ahead, -1, 1)

        @pl.when(beside(down, nd, step))
        def _():
            chunks[pl.ds((me + step * nc) * CHUNK, HALF), :] = odd_rim[0]

    for dy in (-1, 1):
        column = 0 if dy < 0 else cols - 1

        @pl.when(beside(cross, nc, dy))
        def _(dy=dy, column=column):
            lines = []
            for k in range(rows // 2):
                f = fine[k][column : column + 1]
                lines += [f[:, :LANES], f[:, LANES:]]
            at = (me + dy) * CHUNK
            for i, f in enumerate(lines):
                chunks[pl.ds(at + i, 1), :] = f
            for dx in (-1, 1):

                @pl.when(beside(down, nd, dx))
                def _(dx=dx):
                    at = (me + dy + dx * nc) * CHUNK
                    pair = lines[:2] if dx < 0 else lines[-2:]
                    chunks[pl.ds(at, 1), :] = pair[0]
                    chunks[pl.ds(at + 1, 1), :] = pair[1]


def relay_kernel(nd, nc, chunks_in, swapped, chunks):
    chunks[...] = chunks_in[...]
    down, cross = lax.axis_index("down"), lax.axis_index("cross")
    step = jnp.where(down % 2 == 0, 2, -2)

    @pl.when(beside(down, nd, step))
    def _():
        at = ((down + step) * nc + cross) * CHUNK
        chunks[pl.ds(at, HALF), :] = swapped[2 * HALF :]


def coarse_solve(totals, outflow, link_down, link_up, link_cross):
    nc = len(totals)

    def operate(v):
        out = []
        for c in range(nc):
            image = outflow[c] * v[c] - link_down[c] * roll(v[c], -1, 0) - link_up[c] * roll(v[c], 1, 0)
            if c < nc - 1:
                image = image - link_cross[c] * v[c + 1]
            if c > 0:
                image = image - link_cross[c - 1] * v[c - 1]
            out.append(image)
        return out

    def dot(a, b):
        return jnp.sum(sum(x * y for x, y in zip(a, b)), axis=0, keepdims=True)

    answer = [jnp.zeros_like(t) for t in totals]
    resid = search = totals
    norm = dot(totals, totals)
    for step in range(COARSE_ITERS):
        image = operate(search)
        alpha = norm / dot(search, image)
        answer = [a + alpha * s for a, s in zip(answer, search)]
        if step == COARSE_ITERS - 1:
            break
        resid = [r - alpha * m for r, m in zip(resid, image)]
        norm_next = dot(resid, resid)
        beta = norm_next / norm
        search = [r + beta * s for r, s in zip(resid, search)]
        norm = norm_next
    return answer


def last_kernel(nd, nc, tiles, got, swapped, src, gain, wx, wy, wz, state, out, bricks, pres, third):
    rows, cols, layers = out.shape
    tile_w = cols // tiles
    couples = tiles // 2
    down, cross = lax.axis_index("down"), lax.axis_index("cross")
    own, halo = slice(0, cols), slice(cols, cols + STRIP)

    tables = [got[pl.ds(c * CHUNK + HALF, nd, stride=nc * CHUNK), :] for c in range(nc)]

    def spread_lane(table, at):
        return jnp.broadcast_to(table[:, at : at + 1], (nd, LANES))

    last = iota((nd, LANES), 0) == nd - 1
    totals = [spread_lane(t, 0) for t in tables]
    link_down = [jnp.where(last, 0.0, spread_lane(t, 1)) for t in tables]
    link_up = [roll(link, 1, 0) for link in link_down]
    link_cross = [spread_lane(t, 2) for t in tables]
    outflow = [spread_lane(t, 3) for t in tables]
    answer = coarse_solve(totals, outflow, link_down, link_up, link_cross)
    for c in range(nc):
        bricks[c] = answer[c]

    def brick(dx, dy):
        line = bricks[jnp.clip(cross + dy, 0, nc - 1), pl.ds(jnp.clip(down + dx, 0, nd - 1), 1), :]
        return jnp.concatenate([line] * (layers // LANES), axis=1)

    def lines(dx, dy, start, count):
        row, col = jnp.clip(down + dx, 0, nd - 1), jnp.clip(cross + dy, 0, nc - 1)
        return got[pl.ds((row * nc + col) * CHUNK + start, count), :]

    def unpack(packed):
        sub = iota((tile_w, layers), 0) % couples
        parts = []
        for t in range(couples):
            tall = jnp.where(sub == t, packed, 0.0)
            for shift in range(1, couples):
                tall = tall + jnp.where(
                    sub == (t + shift) % couples, roll(packed, shift if t + shift < couples else shift - couples, 0), 0.0
                )
            parts += unpack_pairs(tall, 1)
        return jnp.concatenate(parts, axis=0)

    mine = brick(0, 0)
    for i in range(2, rows + 2):
        pres[i, own, :] = state[i, own, :] + mine
    even_ahead = down % 2 == 0
    even_rim = jnp.concatenate([swapped[:HALF], swapped[HALF : 2 * HALF]], axis=1)
    odd_step = jnp.where(even_ahead, -1, 1)
    odd_rim = jnp.concatenate([lines(odd_step, 0, 0, HALF), lines(2 * odd_step, 0, 0, HALF)], axis=1)
    for dx, at in ((-1, 0), (1, rows + 2)):
        rim = jnp.where(even_ahead == (dx > 0), even_rim, odd_rim)
        extra = jnp.where(beside(down, nd, dx), unpack(rim) + brick(dx, 0), 0.0)
        for i in (at, at + 1):
            pres[i, own, :] = state[i, own, :] + extra

    right = iota((STRIP, layers), 0) < STRIP // 2
    there = (iota((STRIP, layers), 0) < jnp.where(cross < nc - 1, STRIP // 2, 0)) | (
        iota((STRIP, layers), 0) >= jnp.where(cross > 0, STRIP // 2, STRIP)
    )
    b_right, b_left = brick(0, 1), brick(0, -1)
    e_right, e_left = lines(0, 1, 0, HALF), lines(0, -1, 0, HALF)

    def line_pair(block, k):
        return jnp.concatenate([block[2 * k : 2 * k + 1], block[2 * k + 1 : 2 * k + 2]], axis=1)

    for k in range(rows // 2):
        extra = jnp.where(right, line_pair(e_right, k) + b_right, line_pair(e_left, k) + b_left)
        extra = jnp.where(there, extra, 0.0)
        for i in (2 * k + 2, 2 * k + 3):
            pres[i, halo, :] = state[i, halo, :] + extra
    for dx, at in ((-1, 0), (1, rows + 2)):
        extra = jnp.where(
            right,
            line_pair(lines(dx, 1, 0, 2), 0) + brick(dx, 1),
            line_pair(lines(dx, -1, 0, 2), 0) + brick(dx, -1),
        )
        extra = jnp.where(there & beside(down, nd, dx), extra, 0.0)
        for i in (at, at + 1):
            pres[i, halo, :] = state[i, halo, :] + extra

    for i in range(rows + 2):
        spread = gather(pres, i + 1, wx, i + 2, wy[i + 1], wz[i + 1])
        third[i] = KEEP * pres[i + 1] + gain[i + 2] * (src[i + 2] + spread)
    for x in range(rows):
        spread = gather(third, x + 1, wx, x + 3, wy[x + 2], wz[x + 2])
        new = KEEP * third[x + 1] + gain[x + 3] * (src[x + 3] + spread)
        out[x] = new[own]


def whole(*shape):
    return jax.ShapeDtypeStruct(shape, FLOAT)


def call(kernel, out_shape, spaces, scratch=(), vmem_bytes=VMEM_BYTES):
    return pl.pallas_call(
        kernel,
        out_shape=out_shape,
        in_specs=[pl.BlockSpec(memory_space=s) for s in spaces],
        out_specs=jax.tree.map(lambda _: pl.BlockSpec(memory_space=pltpu.VMEM), out_shape),
        scratch_shapes=list(scratch),
        compiler_params=pltpu.CompilerParams(vmem_limit_bytes=vmem_bytes),
    )


def body(nd, nc, right_side, kappa, band_mask, tile_route):
    rows, cols, layers = right_side.shape
    tiles = tile_route.shape[1]
    axes = ("down", "cross")
    wide = cols + STRIP
    block = whole(rows, cols, layers)
    vmem, smem = pltpu.VMEM, pltpu.SMEM

    shapes, perms = [], []
    for kind in pairings(nd):
        shapes.append(whole(2 * DEPTH - 1, cols, layers))
        perms.append(pairs_of(nd, nc, kind, None))
        if kind:
            for cross_kind in pairings(nc):
                shapes.append(whole(CORNER, STRIP, layers))
                perms.append(pairs_of(nd, nc, kind, cross_kind))
    strip = [whole(2 * rows, STRIP, layers) for _ in pairings(nc)]
    conduct, *messages = call(
        functools.partial(pack_kernel, nd, nc),
        [block] + shapes + strip,
        [pltpu.HBM] * 3,
        scratch=[
            pltpu.VMEM((rows, cols, layers), FLOAT),
            pltpu.VMEM((rows, cols, layers), FLOAT),
            pltpu.VMEM((rows, cols, layers), band_mask.dtype),
            pltpu.SemaphoreType.DMA((3,)),
        ],
        vmem_bytes=53 * 1024 * 1024,
    )(right_side, kappa, band_mask)
    received = [lax.ppermute(m, axes, p) for m, p in zip(messages, perms)]
    if pairings(nc):
        strips = call(
            functools.partial(strip_kernel, nd, nc),
            [whole(2 * rows + CORNER, STRIP, layers) for _ in pairings(nc)],
            [vmem] * (1 + len(strip)),
        )(received[0], *messages[len(perms) :])
        received += [
            lax.ppermute(m, axes, pairs_of(nd, nc, None, cross_kind))
            for m, cross_kind in zip(strips, pairings(nc))
        ]

    heights = (rows + 6, rows + 6, rows + 5, rows + 4, rows + 4, rows + 4)
    *kept, swapped, chunks = call(
        functools.partial(main_kernel, nd, nc),
        [whole(h, wide, layers) for h in heights]
        + [whole(3 * HALF, LANES), whole(nd * nc * CHUNK, LANES)],
        [vmem, vmem, smem] + [vmem] * len(received),
        scratch=[
            pltpu.VMEM((h, wide, layers), FLOAT) for h in (rows + 8, rows + 6, rows + 4, rows)
        ],
    )(right_side, conduct, tile_route, *received)
    swapped = lax.ppermute(swapped, axes, pairs_of(nd, nc, False, None))
    chunks = call(
        functools.partial(relay_kernel, nd, nc),
        whole(nd * nc * CHUNK, LANES),
        [vmem, vmem],
    )(chunks, swapped)
    chunks = chunks.reshape(nd * nc, CHUNK, 1, LANES)
    arrived = lax.all_to_all(chunks, axes, 0, 0, tiled=True).reshape(nd * nc * CHUNK, LANES)
    return call(
        functools.partial(last_kernel, nd, nc, tiles),
        block,
        [vmem] * (2 + len(kept)),
        scratch=[
            pltpu.VMEM((nc, nd, LANES), FLOAT),
            pltpu.VMEM((rows + 4, wide, layers), FLOAT),
            pltpu.VMEM((rows + 2, wide, layers), FLOAT),
        ],
    )(arrived, swapped, *kept)


def solution(mesh):
    return jax.shard_map(
        functools.partial(body, mesh.shape["down"], mesh.shape["cross"]),
        mesh=mesh,
        in_specs=(
            P("down", "cross", None),
            P("down", "cross", None),
            P("down", "cross", None),
            P("down", "cross"),
        ),
        out_specs=P("down", "cross", None),
        check_vma=False,
    )
```

time: 38.5 us -> 33.3 us (0.86)
  blocking collectives: 19.2 us -> 14.4 us
  waiting for transfers between devices: 2.67 us -> 5.69 us
  local copies, waits for them, and re-layouts: 2.85 us -> 0.01 us
  starting transfers between devices: 7.97 us -> 7.17 us
  Pallas kernels: 5.31 us -> 5.8 us
    ppermute x5 -> x3, starting transfers between devices: 7.97 us -> 1.27 us  [body(): received = [lax.ppermute(m, axes, p) for m, p in zip(messages, perms)]]
    ppermute x0 -> x2, starting transfers between devices: none -> 5.9 us  [the longest x1 2.98 us: body(): swapped = lax.ppermute(swapped, axes, pairs_of(nd, nc, False, None))]
    all_to_all x1, blocking collectives: 19.2 us -> 14.4 us  [body(): lax.all_to_all(chunks, axes, 0, 0, tiled=True)]
    unnamed x8 -> x4, local copies, waits for them, and re-layouts: 2.85 us -> 0.01 us
    ppermute x5 -> x3, waiting for transfers between devices: 2.67 us -> 4.85 us  [body(): received = [lax.ppermute(m, axes, p) for m, p in zip(messages, perms)]]
    ppermute x0 -> x2, waiting for transfers between devices: none -> 0.84 us  [the longest x1 0.83 us: body(): swapped = lax.ppermute(swapped, axes, pairs_of(nd, nc, False, None))]
    pallas_call x3 -> x5, Pallas kernels: 5.31 us -> 5.8 us  [the longest x1 2.66 us: body(): call(functools.partial(main_kernel, nd, nc), [whole(h, wide, layers) for...]
  transfers between devices with their start and end apart: 5 -> 5, of which waited for: 2 -> 3; matrix products, arithmetic and copies ran while one was open for 0% -> 0% of each run, Pallas kernels for 0% -> 0%
where the time goes in v2:
time: 33.3 us; the launch traced here: 33.1 us
  blocking collectives  14.4 us (43%)
  starting transfers between devices  7.17 us (22%)
  Pallas kernels  5.8 us (17%)
  waiting for transfers between devices  5.69 us (17%)
    all_to_all x1, blocking collectives, body(): lax.all_to_all(chunks, axes, 0, 0, tiled=True)  14.4 us
    ppermute x3, waiting for transfers between devices, body(): received = [lax.ppermute(m, axes, p) for m, p in zip(messages, perms)]  4.85 us
    ppermute x1, starting transfers between devices, body(): swapped = lax.ppermute(swapped, axes, pairs_of(nd, nc, False, None))  2.98 us
    ppermute x1, starting transfers between devices, body(): lax.ppermute(m, axes, pairs_of(nd, nc, None, cross_kind))  2.92 us
    pallas_call x1, Pallas kernels, body(): call(functools.partial(main_kernel, nd, nc), [whole(h, wide, layers) for...  2.66 us
    pallas_call x1, Pallas kernels, body(): call(functools.partial(last_kernel, nd, nc, tiles), block, [vmem] * (2 +...  1.93 us
    ppermute x3, starting transfers between devices, body(): received = [lax.ppermute(m, axes, p) for m, p in zip(messages, perms)]  1.27 us
    pallas_call x1, Pallas kernels, body(): call(functools.partial(pack_kernel, nd, nc), [block] + shapes + strip, [p...  1.17 us
  transfers between devices with their start and end apart: 5, of which 3 were waited for; matrix products, arithmetic and copies ran while one was open for 0% of the time, Pallas kernels for 0%

profile of v2, /device:TPU:0, one launch (start us, length us, event | category | flops | bytes accessed | tf_op | source)
XLA Modules:
  0.0 33.1 jit_solution(13969493859563040266)
XLA Ops:
  0.0 1.2 %shard_map.46 = (f32[8,32,256]{2,1,0:T(8,128)S(1)}, f32[7,32,256]{2,1,0:T(8,128)S(1)}, f32[7,32,256]{2,1,0:T(8,128)S(1)}, f32[5,8,256]{2,1,0:T(8,128)S(1)}, f32[16,8,256]{2,1,0:T(8,128)S(1)}) custom-call(f32[8,32,256]{2,1,0:T(8,128)} %rhs.1, f32[8,32,256]{2,1,0:T(8,128)} %kappa_hbm.1, s32[8,32,256]{2,1,0:T(8,128)} %mask_hbm.1), custom_call_target="tpu_custom_call" | custom-call | tf_op jit(solution)/shard_map/pallas_call | solution.py:572
  1.2 0.5 %collective-permute-start = (f32[7,32,256]{2,1,0:T(8,128)S(1)}, f32[7,32,256]{2,1,0:T(8,128)S(1)}, u32[]{:S(2)}, u32[]{:S(2)}) collective-permute-start(f32[7,32,256]{2,1,0:T(8,128)S(1)} %get-tuple-element.19), channel_id=1, source_target_pairs={{0,2},{1,3},{2,0},{3,1},{4,6},{5,7},{6,4},{7,5},{8,10},{9,11},{10,... | collective-permute-start | bytes 688136 | tf_op jit(solution)/shard_map/ppermute | solution.py:584
  1.7 0.7 %collective-permute-start.1 = (f32[7,32,256]{2,1,0:T(8,128)S(1)}, f32[7,32,256]{2,1,0:T(8,128)S(1)}, u32[]{:S(2)}, u32[]{:S(2)}) collective-permute-start(f32[7,32,256]{2,1,0:T(8,128)S(1)} %get-tuple-element.20), channel_id=1, source_target_pairs={{0,0},{1,1},{2,4},{3,5},{4,2},{5,3},{6,8},{7,9},{8,6},{9,7},{10,12... | collective-permute-start | bytes 688136 | tf_op jit(solution)/shard_map/ppermute | solution.py:584
  2.4 0.4 %collective-permute-done.even.refs_0_ = f32[7,32,256]{2,1,0:T(8,128)S(1)} collective-permute-done((f32[7,32,256]{2,1,0:T(8,128)S(1)}, f32[7,32,256]{2,1,0:T(8,128)S(1)}, u32[]{:S(2)}, u32[]{:S(2)}) %collective-permute-start) | collective-permute-done | bytes 229408 | tf_op jit(solution)/shard_map/ppermute | solution.py:584
  2.8 0.0 copy-start
  2.8 2.9 %collective-permute-start.3 = (f32[21,8,256]{2,1,0:T(8,128)S(1)}, f32[21,8,256]{2,1,0:T(8,128)S(1)}, u32[]{:S(2)}, u32[]{:S(2)}) collective-permute-start(f32[21,8,256]{2,1,0:T(8,128)S(1)} %shard_map.47), channel_id=1, source_target_pairs={{0,1},{1,0},{2,3},{3,2},{4,5},{5,4},{6,7},{7,6},{8,9},{9,8},{10,11... | collective-permute-start | bytes 516104 | tf_op jit(solution)/shard_map/ppermute | solution.py:592
  5.8 0.0 copy-start.1
  5.8 0.1 collective-permute-start.2
  5.9 4.4 %collective-permute-done.2.refs_2_ = f32[5,8,256]{2,1,0:T(8,128)S(1)} collective-permute-done((f32[5,8,256]{2,1,0:T(8,128)S(1)}, f32[5,8,256]{2,1,0:T(8,128)S(1)}, u32[]{:S(2)}, u32[]{:S(2)}) %collective-permute-start.2) | collective-permute-done | bytes 40992 | tf_op jit(solution)/shard_map/ppermute | solution.py:584
  10.3 0.0 collective-permute-done.1.refs_1_
  10.3 0.0 collective-permute-done.3.refs_3_
  10.3 0.0 copy-done
  10.3 0.0 copy-done.1
  10.3 2.7 %shard_map.48 = (f32[14,40,256]{2,1,0:T(8,128)S(1)}, f32[14,40,256]{2,1,0:T(8,128)S(1)}, f32[13,40,256]{2,1,0:T(8,128)S(1)}, f32[12,40,256]{2,1,0:T(8,128)S(1)},...) custom-call(f32[8,32,256]{2,1,0:T(8,128)S(1)} %copy-done, ...), custom_call_target="tpu_custom_call" | custom-call | tf_op jit(solution)/shard_map/pallas_call | solution.py:597
  13.0 3.0 %collective-permute-start.4 = (f32[24,128]{1,0:T(8,128)S(1)}, f32[24,128]{1,0:T(8,128)S(1)}, u32[]{:S(2)}, u32[]{:S(2)}) collective-permute-start(f32[24,128]{1,0:T(8,128)S(1)} %get-tuple-element.24), channel_id=1, source_target_pairs={{0,2},{1,3},{2,0},{3,1},{4,6},{5,7},{6,4},{7,5},{8,10},{9,11},{10,... | collective-permute-start | bytes 36872 | tf_op jit(solution)/shard_map/ppermute | solution.py:606
  15.9 0.8 %collective-permute-done.4.swapped = f32[24,128]{1,0:T(8,128)S(1)} collective-permute-done((f32[24,128]{1,0:T(8,128)S(1)}, f32[24,128]{1,0:T(8,128)S(1)}, u32[]{:S(2)}, u32[]{:S(2)}) %collective-permute-start.4) | collective-permute-done | bytes 12320 | tf_op jit(solution)/shard_map/ppermute | solution.py:606
  16.8 14.4 %all_to_all.5 = f32[32,9,1,128]{3,2,1,0:T(1,128)S(1)} all-to-all(f32[32,9,1,128]{3,2,1,0:T(1,128)S(1)} %bitcast.3), channel_id=1, replica_groups=mesh['down'=16,'cross'=2] {'down','cross'}, dimensions={0} | all-to-all | bytes 294912 | tf_op jit(solution)/shard_map/all_to_all | solution.py:613
  31.2 1.9 %shard_map.50 = f32[8,32,256]{2,1,0:T(8,128)} custom-call(f32[288,128]{1,0:T(8,128)S(1)} %bitcast.2, f32[24,128]{1,0:T(8,128)S(1)} %collective-permute-done.4.swapped, f32[14,40,256]{2,1,0:T(8,128)S(1)} %get-tuple-element.25.src, f32[14,40,256]{2,1,0:T(8,128)S(1)} %get-tuple-element.26.gain, f32[13,40,256]{2,1,0:T(8,128)S(1)} %get-tuple-element.27.wx, ...), custom_call_target="tpu_custom_call" | custom-call | tf_op jit(solution)/shard_map/pallas_call | solution.py:614
  (2 shorter events, 0.0 us)
Async XLA Ops:
  1.2 1.6 %collective-permute-start = (f32[7,32,256]{2,1,0:T(8,128)S(1)}, f32[7,32,256]{2,1,0:T(8,128)S(1)}, u32[]{:S(2)}, u32[]{:S(2)}) collective-permute-start(f32[7,32,256]{2,1,0:T(8,128)S(1)} %get-tuple-element.19), channel_id=1, source_target_pairs={{0,2},{1,3},{2,0},{3,1},{4,6},{5,7},{6,4},{7,5},{8,10},{9,11},{10,... | collective-permute-start | bytes 688136 | tf_op jit(solution)/shard_map/ppermute | solution.py:584
  1.7 8.6 %collective-permute-start.1 = (f32[7,32,256]{2,1,0:T(8,128)S(1)}, f32[7,32,256]{2,1,0:T(8,128)S(1)}, u32[]{:S(2)}, u32[]{:S(2)}) collective-permute-start(f32[7,32,256]{2,1,0:T(8,128)S(1)} %get-tuple-element.20), channel_id=1, source_target_pairs={{0,0},{1,1},{2,4},{3,5},{4,2},{5,3},{6,8},{7,9},{8,6},{9,7},{10,12... | collective-permute-start | bytes 688136 | tf_op jit(solution)/shard_map/ppermute | solution.py:584
  2.8 7.5 %copy-start = (f32[8,32,256]{2,1,0:T(8,128)S(1)}, f32[8,32,256]{2,1,0:T(8,128)}, u32[]{:S(2)}) copy-start(f32[8,32,256]{2,1,0:T(8,128)} %rhs.1) | copy-start | bytes 786436
  2.8 7.4 %collective-permute-start.3 = (f32[21,8,256]{2,1,0:T(8,128)S(1)}, f32[21,8,256]{2,1,0:T(8,128)S(1)}, u32[]{:S(2)}, u32[]{:S(2)}) collective-permute-start(f32[21,8,256]{2,1,0:T(8,128)S(1)} %shard_map.47), channel_id=1, source_target_pairs={{0,1},{1,0},{2,3},{3,2},{4,5},{5,4},{6,7},{7,6},{8,9},{9,8},{10,11... | collective-permute-start | bytes 516104 | tf_op jit(solution)/shard_map/ppermute | solution.py:592
  5.8 4.5 %copy-start.1 = (s32[1,4]{1,0:T(1,128)S(1)}, s32[1,4]{1,0:T(1,128)}, u32[]{:S(2)}) copy-start(s32[1,4]{1,0:T(1,128)} %route.1) | copy-start | bytes 52
  5.8 4.5 %collective-permute-start.2 = (f32[5,8,256]{2,1,0:T(8,128)S(1)}, f32[5,8,256]{2,1,0:T(8,128)S(1)}, u32[]{:S(2)}, u32[]{:S(2)}) collective-permute-start(f32[5,8,256]{2,1,0:T(8,128)S(1)} %get-tuple-element.21), channel_id=1, source_target_pairs={{0,1},{1,0},{2,5},{3,4},{4,3},{5,2},{6,9},{7,8},{8,7},{9,6},{10,13... | collective-permute-start | bytes 122888 | tf_op jit(solution)/shard_map/ppermute | solution.py:584
  13.0 3.8 %collective-permute-start.4 = (f32[24,128]{1,0:T(8,128)S(1)}, f32[24,128]{1,0:T(8,128)S(1)}, u32[]{:S(2)}, u32[]{:S(2)}) collective-permute-start(f32[24,128]{1,0:T(8,128)S(1)} %get-tuple-element.24), channel_id=1, source_target_pairs={{0,2},{1,3},{2,0},{3,1},{4,6},{5,7},{6,4},{7,5},{8,10},{9,11},{10,... | collective-permute-start | bytes 36872 | tf_op jit(solution)/shard_map/ppermute | solution.py:606

commit v3 on v2

v3 whole, which is shorter than its diff:
```python
import functools

import jax
import jax.numpy as jnp
from jax import lax
from jax.experimental import pallas as pl
from jax.experimental.pallas import tpu as pltpu
from jax.sharding import PartitionSpec as P

BLOCK_SWEEPS = 4
COARSE_ITERS = 12
OMEGA = 0.8
KEEP = 1.0 - OMEGA
SNOW_FACTOR = 3.0

DEPTH = 4
CORNER = DEPTH - 1
STRIP = 8
LANES = 128
HALF = 8
CHUNK = HALF + 1
FLOAT = jnp.float32
VMEM_BYTES = 48 * 1024 * 1024


def partners(count, odd):
    found = []
    for i in range(count):
        j = ((i + 1) ^ 1) - 1 if odd else i ^ 1
        found.append(j if 0 <= j < count else i)
    return found


def pairings(count):
    return [k for k in (False, True) if any(j != i for i, j in enumerate(partners(count, k)))]


def pairs_of(count_down, count_cross, down_kind, cross_kind):
    rows = list(range(count_down)) if down_kind is None else partners(count_down, down_kind)
    cols = list(range(count_cross)) if cross_kind is None else partners(count_cross, cross_kind)
    return [
        (i * count_cross + j, rows[i] * count_cross + cols[j])
        for i in range(count_down)
        for j in range(count_cross)
    ]


def facing(index, count, kind):
    ahead = (index % 2 == 0) != kind
    return ahead, jnp.where(ahead, index < count - 1, index > 0)


def beside(index, count, step):
    return (index + step >= 0) & (index + step < count)


def roll(x, amount, axis):
    return pltpu.roll(x, amount % x.shape[axis], axis)


def iota(shape, axis):
    return lax.broadcasted_iota(jnp.int32, shape, axis)


def gather(value, low, high, wx_low, wx_high, wy, wz):
    total = wx_high * high + wx_low * low
    total = total + wy * roll(value, -1, 0) + roll(wy * value, 1, 0)
    return total + wz * roll(value, -1, 1) + roll(wz * value, 1, 1)


class Rows:
    def __init__(self, *parts):
        self.parts = parts

    def place(self, x):
        for ref, first, count in self.parts:
            if first <= x < first + count:
                return ref, x - first
        raise IndexError(x)

    def __getitem__(self, x):
        ref, i = self.place(x)
        return ref[i]

    def __setitem__(self, x, value):
        ref, i = self.place(x)
        ref[i] = value


def smooth(field, gain, src, wx, wy, wz, x):
    spread = gather(field[x], field[x - 1], field[x + 1], wx[x - 1], wx[x], wy[x], wz[x])
    return KEEP * field[x] + gain[x] * (src[x] + spread)


def counted(x, rows):
    return jnp.where(lax.axis_index("down") % 2 == 0, x, rows - 1 - x)


def edge_strip(right, cols):
    return pl.ds(pl.multiple_of(jnp.where(right, cols - STRIP, 0), STRIP), STRIP)


def pack_rows(out, start, tiles, right):
    for i in range(0, len(tiles), 2):
        a, b = tiles[i], tiles[min(i + 1, len(tiles) - 1)]
        upper = iota(a.shape, 0) < STRIP // 2
        a, b = jnp.where(right, roll(a, STRIP // 2, 0), a), jnp.where(right, b, roll(b, STRIP // 2, 0))
        out[start + i // 2] = jnp.where(upper, a, b)


def unpack_row(message, start, i, right):
    tile = message[start + i // 2]
    return jnp.where(right == (i % 2 == 0), tile, roll(tile, STRIP // 2, 0))


def pack_kernel(nd, nc, rhs_hbm, kappa_hbm, mask_hbm, conduct, *refs):
    *messages, rhs, kappa, mask, sems = refs
    rows, cols, _ = rhs.shape
    messages = iter(messages)
    cross = lax.axis_index("cross")
    copies = [
        pltpu.make_async_copy(src, dst, sems.at[i])
        for i, (src, dst) in enumerate(((kappa_hbm, kappa), (mask_hbm, mask), (rhs_hbm, rhs)))
    ]
    for copy in copies:
        copy.start()
    copies[0].wait()
    copies[1].wait()
    for x in range(rows):
        at = counted(x, rows)
        conduct[x] = kappa[at] / (1.0 + SNOW_FACTOR * mask[at].astype(FLOAT))
    copies[2].wait()
    for kind in pairings(nd):
        near = [i if kind else rows - 1 - i for i in range(DEPTH)]
        out = next(messages)
        for i, x in enumerate(near):
            out[i] = conduct[x]
        for i, x in enumerate(near[:-1]):
            out[DEPTH + i] = rhs[counted(x, rows)]
        if kind:
            for cross_kind in pairings(nc):
                right, _ = facing(cross, nc, cross_kind)
                strip = edge_strip(right, cols)
                tiles = [conduct[x, strip, :] for x in near[: DEPTH - 1]]
                tiles += [rhs[counted(x, rows), strip, :] for x in near[: DEPTH - 2]]
                pack_rows(next(messages), 0, tiles, right)
    for cross_kind in pairings(nc):
        right, _ = facing(cross, nc, cross_kind)
        strip = edge_strip(right, cols)
        tiles = [conduct[x, strip, :] for x in range(rows)]
        tiles += [rhs[counted(x, rows), strip, :] for x in range(rows)]
        pack_rows(next(messages), 0, tiles, right)


def strip_kernel(nd, nc, even, *refs):
    cols = even.shape[1]
    count = len(pairings(nc))
    for cross_kind, own, out in zip(pairings(nc), refs[:count], refs[count:]):
        right, _ = facing(lax.axis_index("cross"), nc, cross_kind)
        strip = edge_strip(right, cols)
        rows = own.shape[0]
        out[:rows] = own[...]
        tiles = [even[i, strip, :] for i in range(DEPTH - 1)]
        tiles += [even[DEPTH + i, strip, :] for i in range(DEPTH - 2)]
        pack_rows(out, rows, tiles, right)


def fold(x):
    x = sum(x[:, i : i + LANES] for i in range(0, x.shape[1], LANES))
    return jnp.sum(x, axis=0, keepdims=True)


def swap_pairs(x, axis):
    return jnp.where(iota(x.shape, axis) % 2 == 0, roll(x, -1, axis), roll(x, 1, axis))


def pack_pairs(a, b, axis):
    even = iota(a.shape, axis) % 2 == 0
    return jnp.where(even, a, b) + swap_pairs(jnp.where(even, b, a), axis)


def unpack_pairs(x, axis):
    even = iota(x.shape, axis) % 2 == 0
    return jnp.where(even, x, roll(x, 1, axis)), jnp.where(even, roll(x, -1, axis), x)


class Frame:
    def __init__(self, nd, nc, cols, layers):
        self.cols, self.layers, self.wide = cols, layers, cols + STRIP
        self.own, self.halo = slice(0, cols), slice(cols, cols + STRIP)
        cross = lax.axis_index("cross")
        half = STRIP // 2
        self.lane = iota((self.wide, layers), 1)
        self.last_lane = self.lane == layers - 1
        col = iota((self.wide, layers), 0)
        self.col_ok = (col < jnp.where(cross < nc - 1, cols + half, cols)) | (
            col >= jnp.where(cross > 0, cols + half, self.wide)
        )
        halo_col = iota((STRIP, layers), 0)
        self.sides, self.rights = [], []
        for cross_kind in pairings(nc):
            right, valid = facing(cross, nc, cross_kind)
            start = jnp.where(right, 0, half)
            stop = jnp.where(valid, start + half, 0)
            self.sides.append((halo_col >= start) & (halo_col < stop))
            self.rights.append(right)

    def merged(self, messages, start, i):
        total = jnp.zeros((STRIP, self.layers), FLOAT)
        for side, right, message in zip(self.sides, self.rights, messages):
            total = jnp.where(side, unpack_row(message, start, i, right), total)
        return total

    def row(self, own, halo):
        return jnp.concatenate([own, halo], axis=0)

    def weights(self, q, gain, src, first, diag, wx, wy, wz, x, valid=None):
        here = q[x]
        above = jnp.where(self.last_lane, 0.0, roll(here, -1, 1))
        below = jnp.where(self.lane == 0, 0.0, roll(here, 1, 1))
        right = roll(here, -1, 0)
        doubled = 6.0 * here + (q[x - 1] + q[x + 1]) + (right + roll(here, 1, 0)) + (above + below)
        ok = self.col_ok & (doubled > 0.0)
        if valid is not None:
            ok = ok & valid
        gain_here = jnp.where(ok, (2.0 * OMEGA) / doubled, 0.0)
        gain[x] = gain_here
        first[x] = gain_here * src[x]
        if diag is not None:
            diag[x] = 0.5 * doubled
        if wx is not None:
            wx[x] = 0.5 * (here + q[x + 1])
        if wy is not None:
            self.plane_weights(wy, wz, x, here, right, above)

    def plane_weights(self, wy, wz, x, here, right, above):
        wy[x] = 0.5 * (here + right)
        wz[x] = jnp.where(self.last_lane, 0.0, 0.5 * (here + above))


def residual(frame, src, diag, pres, wx, wy, wz, x):
    spread = gather(pres[x], pres[x - 1], pres[x + 1], wx[x - 1], wx[x], wy[x], wz[x])
    return (src[x] - diag[x] * pres[x] + spread)[frame.own]


def spans(rows):
    far = rows + DEPTH
    early = dict(
        q=(0, far), src=(0, far - 1), gain=(1, far - 1), first=(1, far - 1), diag=(1, rows),
        wx=(0, far - 2), wy=(0, rows + 2), wz=(0, rows + 2), pres=(2, rows + 2),
    )
    late = dict(
        q=(-DEPTH, 0), src=(1 - DEPTH, 0), gain=(1 - DEPTH, 1), first=(1 - DEPTH, 1), diag=(0, 1),
        wx=(1 - DEPTH, 0), wy=(-2, 0), wz=(-2, 0), pres=(-2, 2),
    )
    return early, late


EARLY = ("q", "src", "gain", "first", "diag", "wx", "wy", "wz", "pres")
LATE_KEPT = ("src", "gain", "wx", "wy", "wz", "pres")
LATE_SCRATCH = ("q", "first", "diag")


def span_shape(span, wide, layers):
    return (span[1] - span[0], wide, layers)


def joined(rows, name, early_ref, late_ref):
    early, late = (d[name] for d in spans(rows))
    return Rows((early_ref, early[0], early[1] - early[0]), (late_ref, late[0], late[1] - late[0]))


def coarse_rows(pair, couples, tile_w):
    t = pair.reshape(couples, 2, tile_w, pair.shape[1])
    return pack_pairs(t[:, 0], t[:, 1], 2)


def early_kernel(nd, nc, tiles, rhs, conduct, route, even, *refs):
    rows, cols, layers = conduct.shape
    tile_w = cols // tiles
    couples = tiles // 2
    n_cross = len(pairings(nc))
    strips = refs[:n_cross]
    *arrays, res_coarse, res_row, coef, sums, touched = refs[n_cross:]
    early, _ = spans(rows)
    at = {n: Rows((r, early[n][0], r.shape[0])) for n, r in zip(EARLY, arrays)}
    q, src, gain, first, diag, wx, wy, wz, pres = (at[n] for n in EARLY)
    frame = Frame(nd, nc, cols, layers)
    own, halo = frame.own, frame.halo

    for x in range(rows):
        q[x] = frame.row(conduct[x], frame.merged(strips, 0, x))
        src[x] = frame.row(rhs[counted(x, rows)], frame.merged(strips, 0, rows + x))
    _, valid = facing(lax.axis_index("down"), nd, False)
    blank = jnp.zeros((STRIP, layers), FLOAT)
    for i in range(DEPTH):
        corner = frame.merged(strips, rows, i) if i < DEPTH - 1 else blank
        q[rows + i] = jnp.where(valid, frame.row(even[i], corner), 0.0)
    for i in range(DEPTH - 1):
        corner = frame.merged(strips, rows, DEPTH - 1 + i) if i < DEPTH - 2 else blank
        src[rows + i] = jnp.where(valid, frame.row(even[DEPTH + i], corner), 0.0)

    here = q[0]
    above = jnp.where(frame.last_lane, 0.0, roll(here, -1, 1))
    frame.plane_weights(wy, wz, 0, here, roll(here, -1, 0), above)
    wx[0] = 0.5 * (here + q[1])
    for x in range(*early["gain"]):
        frame.weights(
            q, gain, src, first,
            diag if x < rows else None,
            wx if x < early["wx"][1] else None,
            wy if x < early["wy"][1] else None,
            wz, x, valid if x >= rows else None,
        )
    for x in range(*early["pres"]):
        pres[x] = smooth(first, gain, src, wx, wy, wz, x)

    res = {x: residual(frame, src, diag, pres, wx, wy, wz, x) for x in range(3, rows)}
    res_row[...] = res[3]
    for k in range(2, rows // 2):
        res_coarse[k - 2] = coarse_rows(res[2 * k] + res[2 * k + 1], couples, tile_w)

    even_lane = iota((tile_w, layers), 1) % 2 == 0
    for t in range(couples):
        numbers = [jnp.broadcast_to(route[0:1, i : i + 1], (tile_w, layers)) for i in (2 * t, 2 * t + 1)]
        touched[t] = jnp.where(jnp.where(even_lane, *numbers) >= 0, 1.0, 0.0)

    strip_col = iota((STRIP, layers), 0)
    plane = sum(q[x][own] for x in range(rows))
    beyond = sum(q[x][halo] for x in range(rows))
    own_lane = iota((cols, layers), 1)
    low, high = strip_col < 2, strip_col >= STRIP - 2
    sums[0:1] = fold(sum(res.values()))
    sums[1:2] = fold(sum(q[x][own] for x in range(rows - 2, rows + 2)))
    sums[2:3] = fold(jnp.where(high, plane[cols - STRIP :], 0.0) + jnp.where(low, beyond, 0.0))
    sums[3:4] = fold(jnp.where(low, plane[:STRIP], 0.0) + jnp.where(high, beyond, 0.0))
    sums[4:5] = fold(jnp.where((own_lane < 2) | (own_lane >= layers - 2), plane, 0.0))

    packs = rows // 4
    by_row = [
        coarse_rows(0.125 * (q[2 * k][own] + q[2 * k + 1][own]), couples, tile_w)
        for k in range(rows // 2)
    ]
    con = [pack_pairs(by_row[k], by_row[k + packs], 1) for k in range(packs)]
    shape = (couples, tile_w, layers)
    tile_col, tile_lane = iota(shape, 1), iota(shape, 2)
    even_col = tile_col % 2 == 0
    y_end, y_start = tile_col >= tile_w - 2, tile_col < 2
    z_end, z_start = tile_lane >= layers - 2, tile_lane < 2
    for k in range(packs - 1):
        coef[3 * packs + 2 + k] = 2.0 * (con[k] + con[k + 1])
    middle = 2.0 * (con[packs - 1] + roll(con[0], -1, 1))
    coef[3 * packs] = jnp.where(even_col, middle, 0.0)
    coef[3 * packs + 1] = jnp.where(even_col, 0.0, roll(middle, 1, 1))
    for k in range(packs):
        c = con[k]
        y_high = jnp.where(y_end, 0.0, roll(c, -2, 1))
        z_high = jnp.where(z_end, 0.0, roll(c, -2, 2))
        y_low = jnp.where(y_start, 0.0, roll(c, 2, 1))
        z_low = jnp.where(z_start, 0.0, roll(c, 2, 2))
        total = 6.0 * c + (y_high + y_low) + (z_high + z_low)
        if k > 0:
            total = total + con[k - 1]
        else:
            total = total + jnp.where(even_col, 0.0, roll(con[packs - 1], 1, 1))
        if k < packs - 1:
            total = total + con[k + 1]
        else:
            total = total + jnp.where(even_col, roll(con[0], -1, 1), 0.0)
        total = 2.0 * total
        coef[k] = OMEGA / jnp.where(total > 0.0, total, 1.0)
        coef[packs + k] = jnp.where(y_end, 0.0, 2.0 * (c + y_high))
        coef[2 * packs + k] = jnp.where(z_end, 0.0, 2.0 * (c + z_high))


def late_kernel(nd, nc, tiles, rows, odd, *refs):
    n_cross = len(pairings(nc)) if len(pairings(nd)) > 1 else 0
    corners = refs[:n_cross]
    n_in = n_cross + len(EARLY) + 5
    early_refs = dict(zip(EARLY, refs[n_cross:]))
    res_coarse, res_row, coef, sums, touched = refs[n_in - 5 : n_in]
    names = LATE_KEPT + ("swapped", "fix", "summary") + LATE_SCRATCH
    late_refs = dict(zip(names, refs[n_in:]))
    swapped, fix_out, summary = (late_refs[n] for n in ("swapped", "fix", "summary"))
    wide, layers = early_refs["q"].shape[1:]
    cols = wide - STRIP
    tile_w = cols // tiles
    couples = tiles // 2
    down = lax.axis_index("down")
    even = down % 2 == 0
    q, src, gain, first, diag, wx, wy, wz, pres = (
        joined(rows, n, early_refs[n], late_refs[n]) for n in EARLY
    )
    frame = Frame(nd, nc, cols, layers)
    _, late = spans(rows)

    valid = beside(down, nd, jnp.where(even, -1, 1))
    blank = jnp.zeros((STRIP, layers), FLOAT)
    for i in range(DEPTH):
        corner = frame.merged(corners, 0, i) if i < DEPTH - 1 else blank
        q[-1 - i] = jnp.where(valid, frame.row(odd[i], corner), 0.0)
    for i in range(DEPTH - 1):
        corner = frame.merged(corners, 0, DEPTH - 1 + i) if i < DEPTH - 2 else blank
        src[-1 - i] = jnp.where(valid, frame.row(odd[DEPTH + i], corner), 0.0)
    for x in range(*late["gain"]):
        frame.weights(
            q, gain, src, first,
            diag if x == 0 else None,
            wx if x < 0 else None,
            wy if -2 <= x < 0 else None,
            wz, x, valid if x < 0 else None,
        )
    for x in range(*late["pres"]):
        pres[x] = smooth(first, gain, src, wx, wy, wz, x)
    res = [residual(frame, src, diag, pres, wx, wy, wz, x) for x in range(3)]
    res.append(res_row[...])

    res_total = sums[0:1] + fold(res[0] + res[1] + res[2])
    link_odd = fold(sum(q[x][frame.own] for x in range(-2, 2)))
    link_even, link_cross, link_back, ends = (sums[i : i + 1] for i in range(1, 5))
    outflow = link_even + link_odd + link_cross + link_back + ends
    link_down = jnp.where(even, link_even, link_odd)
    lines = jnp.concatenate([res_total, 0.25 * link_down, 0.25 * link_cross, 0.25 * outflow])
    lines = jnp.sum(lines, axis=1, keepdims=True)
    line = iota((1, LANES), 1)
    summary[...] = jnp.where(
        line == 0, lines[0:1], jnp.where(line == 1, lines[1:2], jnp.where(line == 2, lines[2:3], lines[3:4]))
    )

    packs = rows // 4
    by_row = [coarse_rows(res[2 * k] + res[2 * k + 1], couples, tile_w) for k in range(2)]
    by_row += [res_coarse[k] for k in range(rows // 2 - 2)]
    r = [pack_pairs(by_row[k], by_row[k + packs], 1) for k in range(packs)]
    middle_low, middle_high = coef[3 * packs], coef[3 * packs + 1]
    fix = [coef[k] * r[k] for k in range(packs)]
    for _ in range(BLOCK_SWEEPS - 1):
        updated = []
        for k in range(packs):
            value, link_y, link_z = fix[k], coef[packs + k], coef[2 * packs + k]
            acc = r[k] + link_y * roll(value, -2, 1) + roll(link_y * value, 2, 1)
            acc = acc + link_z * roll(value, -2, 2) + roll(link_z * value, 2, 2)
            if k > 0:
                acc = acc + coef[3 * packs + 1 + k] * fix[k - 1]
            else:
                acc = acc + middle_high * roll(fix[packs - 1], 1, 1)
            if k < packs - 1:
                acc = acc + coef[3 * packs + 2 + k] * fix[k + 1]
            else:
                acc = acc + middle_low * roll(fix[0], -1, 1)
            updated.append(KEEP * value + coef[k] * acc)
        fix = updated
    fix = [jnp.where(touched[...] > 0.0, f, 0.0) for f in fix]
    for k in range(packs):
        fix_out[k] = fix[k]

    def rim(k, j):
        part = unpack_pairs(fix[k], 1)[j]
        sub = iota((tile_w, layers), 0) % couples
        packed = part[0]
        for t in range(1, couples):
            packed = jnp.where(sub == t, part[t], packed)
        return packed[:, :LANES], packed[:, LANES:]

    even_rim, odd_rim = rim(packs - 1, 1), rim(0, 0)
    swapped[:HALF] = even_rim[0]
    swapped[HALF : 2 * HALF] = even_rim[1]
    swapped[2 * HALF : 3 * HALF] = odd_rim[1]
    swapped[3 * HALF :] = odd_rim[0]


def spread_kernel(nd, nc, tiles, fix, swapped, summary, pres_early, pres_late, state, chunks):
    packs, couples, tile_w, layers = fix.shape
    rows = 4 * packs
    cols = tiles * tile_w
    own, halo = slice(0, cols), slice(cols, cols + STRIP)
    down, cross = lax.axis_index("down"), lax.axis_index("cross")
    pres = joined(rows, "pres", pres_early, pres_late)

    fine = [None] * (rows // 2)
    for k in range(packs):
        for j, part in enumerate(unpack_pairs(fix[k], 1)):
            both = unpack_pairs(part, 2)
            fine[k + j * packs] = jnp.stack(both, axis=1).reshape(cols, layers)

    for x in range(-2, rows + 2):
        value = pres[x]
        if 0 <= x < rows:
            state[x + 2, own, :] = value[own] + fine[x // 2]
            state[x + 2, halo, :] = value[halo]
        else:
            state[x + 2] = value

    blank = jnp.zeros((HALF, LANES), FLOAT)
    sums = summary[...]

    def fill(b, carry):
        at = b * CHUNK
        chunks[pl.ds(at, HALF), :] = blank
        chunks[pl.ds(at + HALF, 1), :] = sums
        return carry

    lax.fori_loop(0, nd * nc, fill, 0)
    me = down * nc + cross
    odd_step = jnp.where(down % 2 == 0, -1, 1)

    @pl.when(beside(down, nd, odd_step))
    def _():
        chunks[pl.ds((me + odd_step * nc) * CHUNK, HALF), :] = swapped[3 * HALF :]

    for dy in (-1, 1):
        column = 0 if dy < 0 else cols - 1

        @pl.when(beside(cross, nc, dy))
        def _(dy=dy, column=column):
            lines = []
            for k in range(rows // 2):
                f = fine[k][column : column + 1]
                lines += [f[:, :LANES], f[:, LANES:]]
            at = (me + dy) * CHUNK
            for i, f in enumerate(lines):
                chunks[pl.ds(at + i, 1), :] = f
            for side in (0, 1):
                dx = -odd_step if side else odd_step

                @pl.when(beside(down, nd, dx))
                def _(side=side, dx=dx):
                    at = (me + dy + dx * nc) * CHUNK
                    pair = lines[-2:] if side else lines[:2]
                    chunks[pl.ds(at, 1), :] = pair[0]
                    chunks[pl.ds(at + 1, 1), :] = pair[1]


def relay_kernel(nd, nc, chunks_in, swapped, chunks):
    chunks[...] = chunks_in[...]
    down, cross = lax.axis_index("down"), lax.axis_index("cross")
    step = jnp.where(down % 2 == 0, 2, -2)

    @pl.when(beside(down, nd, step))
    def _():
        at = ((down + step) * nc + cross) * CHUNK
        chunks[pl.ds(at, HALF), :] = swapped[2 * HALF : 3 * HALF]


def coarse_solve(totals, outflow, link_down, link_up, link_cross):
    nc = len(totals)

    def operate(v):
        out = []
        for c in range(nc):
            image = outflow[c] * v[c] - link_down[c] * roll(v[c], -1, 0) - link_up[c] * roll(v[c], 1, 0)
            if c < nc - 1:
                image = image - link_cross[c] * v[c + 1]
            if c > 0:
                image = image - link_cross[c - 1] * v[c - 1]
            out.append(image)
        return out

    def dot(a, b):
        return jnp.sum(sum(x * y for x, y in zip(a, b)), axis=0, keepdims=True)

    answer = [jnp.zeros_like(t) for t in totals]
    resid = search = totals
    norm = dot(totals, totals)
    for step in range(COARSE_ITERS):
        image = operate(search)
        alpha = norm / dot(search, image)
        answer = [a + alpha * s for a, s in zip(answer, search)]
        if step == COARSE_ITERS - 1:
            break
        resid = [r - alpha * m for r, m in zip(resid, image)]
        norm_next = dot(resid, resid)
        beta = norm_next / norm
        search = [r + beta * s for r, s in zip(resid, search)]
        norm = norm_next
    return answer


KEPT = ("src", "gain", "wx", "wy", "wz")


def last_kernel(nd, nc, tiles, got, swapped, state, *refs):
    early = dict(zip(KEPT, refs))
    late = dict(zip(KEPT, refs[len(KEPT) :]))
    out, bricks, pres_ref, third_ref = refs[2 * len(KEPT) :]
    rows, cols, layers = out.shape
    src, gain, wx, wy, wz = (joined(rows, n, early[n], late[n]) for n in KEPT)
    tile_w = cols // tiles
    couples = tiles // 2
    down, cross = lax.axis_index("down"), lax.axis_index("cross")
    own, halo = slice(0, cols), slice(cols, cols + STRIP)

    tables = [got[pl.ds(c * CHUNK + HALF, nd, stride=nc * CHUNK), :] for c in range(nc)]

    def spread_lane(table, at):
        return jnp.broadcast_to(table[:, at : at + 1], (nd, LANES))

    last = iota((nd, LANES), 0) == nd - 1
    totals = [spread_lane(t, 0) for t in tables]
    link_down = [jnp.where(last, 0.0, spread_lane(t, 1)) for t in tables]
    link_up = [roll(link, 1, 0) for link in link_down]
    link_cross = [spread_lane(t, 2) for t in tables]
    outflow = [spread_lane(t, 3) for t in tables]
    answer = coarse_solve(totals, outflow, link_down, link_up, link_cross)
    for c in range(nc):
        bricks[c] = answer[c]

    def brick(dx, dy):
        line = bricks[jnp.clip(cross + dy, 0, nc - 1), pl.ds(jnp.clip(down + dx, 0, nd - 1), 1), :]
        return jnp.concatenate([line] * (layers // LANES), axis=1)

    def lines(dx, dy, count):
        row, col = jnp.clip(down + dx, 0, nd - 1), jnp.clip(cross + dy, 0, nc - 1)
        return got[pl.ds((row * nc + col) * CHUNK, count), :]

    def line_pair(block, k):
        return jnp.concatenate([block[2 * k : 2 * k + 1], block[2 * k + 1 : 2 * k + 2]], axis=1)

    def unpack(packed):
        sub = iota((tile_w, layers), 0) % couples
        parts = []
        for t in range(couples):
            tall = jnp.where(sub == t, packed, 0.0)
            for s in range(couples):
                if s != t:
                    tall = tall + jnp.where(sub == s, roll(packed, s - t, 0), 0.0)
            parts += unpack_pairs(tall, 1)
        return jnp.concatenate(parts, axis=0)

    odd_step = jnp.where(down % 2 == 0, -1, 1)
    even_rim = jnp.concatenate([swapped[:HALF], swapped[HALF : 2 * HALF]], axis=1)
    odd_rim = jnp.concatenate([lines(odd_step, 0, HALF), lines(2 * odd_step, 0, HALF)], axis=1)
    right = iota((STRIP, layers), 0) < STRIP // 2
    there = (iota((STRIP, layers), 0) < jnp.where(cross < nc - 1, STRIP // 2, 0)) | (
        iota((STRIP, layers), 0) >= jnp.where(cross > 0, STRIP // 2, STRIP)
    )

    pres = Rows((pres_ref, -2, rows + 4))
    third = Rows((third_ref, -1, rows + 2))
    mine = brick(0, 0)
    side_bricks = brick(0, 1), brick(0, -1)
    side_lines = lines(0, 1, HALF), lines(0, -1, HALF)
    for k in range(rows // 2):
        extra = jnp.where(right, *(line_pair(f, k) + b for f, b in zip(side_lines, side_bricks)))
        extra = jnp.where(there, extra, 0.0)
        for x in (2 * k, 2 * k + 1):
            pres_ref[x + 2, own, :] = state[x + 2, own, :] + mine
            pres_ref[x + 2, halo, :] = state[x + 2, halo, :] + extra
    for step, rim, at in ((odd_step, odd_rim, 0), (-odd_step, even_rim, rows + 2)):
        valid = beside(down, nd, step)
        row = jnp.where(valid, unpack(rim) + brick(step, 0), 0.0)
        corner = jnp.where(
            right, *(line_pair(lines(step, dy, 2), 0) + brick(step, dy) for dy in (1, -1))
        )
        corner = jnp.where(there & valid, corner, 0.0)
        for i in (at, at + 1):
            pres_ref[i, own, :] = state[i, own, :] + row
            pres_ref[i, halo, :] = state[i, halo, :] + corner

    for x in range(-1, rows + 1):
        third[x] = smooth(pres, gain, src, wx, wy, wz, x)
    for x in range(rows):
        out[counted(x, rows)] = smooth(third, gain, src, wx, wy, wz, x)[own]


def whole(*shape):
    return jax.ShapeDtypeStruct(shape, FLOAT)


def call(kernel, out_shape, spaces, scratch=(), vmem_bytes=VMEM_BYTES):
    return pl.pallas_call(
        kernel,
        out_shape=out_shape,
        in_specs=[pl.BlockSpec(memory_space=s) for s in spaces],
        out_specs=jax.tree.map(lambda _: pl.BlockSpec(memory_space=pltpu.VMEM), out_shape),
        scratch_shapes=list(scratch),
        compiler_params=pltpu.CompilerParams(vmem_limit_bytes=vmem_bytes),
    )


def body(nd, nc, right_side, kappa, band_mask, tile_route):
    rows, cols, layers = right_side.shape
    tiles = tile_route.shape[1]
    axes = ("down", "cross")
    wide = cols + STRIP
    block = whole(rows, cols, layers)
    vmem = pltpu.VMEM
    early, late = spans(rows)

    shapes, perms = [], []
    for kind in pairings(nd):
        shapes.append(whole(2 * DEPTH - 1, cols, layers))
        perms.append(pairs_of(nd, nc, kind, None))
        if kind:
            for cross_kind in pairings(nc):
                shapes.append(whole(CORNER, STRIP, layers))
                perms.append(pairs_of(nd, nc, kind, cross_kind))
    strips = [whole(rows, STRIP, layers) for _ in pairings(nc)]
    packs, couples, tile_w = rows // 4, tiles // 2, cols // tiles
    tile_shape = (couples, tile_w, layers)
    conduct, *messages = call(
        functools.partial(pack_kernel, nd, nc),
        [block] + shapes + strips,
        [pltpu.HBM] * 3,
        scratch=[
            pltpu.VMEM((rows, cols, layers), FLOAT),
            pltpu.VMEM((rows, cols, layers), FLOAT),
            pltpu.VMEM((rows, cols, layers), band_mask.dtype),
            pltpu.SemaphoreType.DMA((3,)),
        ],
        vmem_bytes=53 * 1024 * 1024,
    )(right_side, kappa, band_mask)

    received = [lax.ppermute(m, axes, p) for m, p in zip(messages, perms)]
    even, odd = received[0], received[1:]
    if strips:
        strips = call(
            functools.partial(strip_kernel, nd, nc),
            [whole(rows + CORNER, STRIP, layers) for _ in strips],
            [vmem] * (1 + len(strips)),
        )(even, *messages[len(perms) :])
        strips = [
            lax.ppermute(m, axes, pairs_of(nd, nc, None, cross_kind))
            for m, cross_kind in zip(strips, pairings(nc))
        ]
    if not odd:
        odd = [jnp.zeros((2 * DEPTH - 1, cols, layers), FLOAT)]

    first_part = call(
        functools.partial(early_kernel, nd, nc, tiles),
        [whole(*span_shape(early[n], wide, layers)) for n in EARLY]
        + [
            whole(rows // 2 - 2, *tile_shape),
            whole(cols, layers),
            whole(4 * packs + 1, *tile_shape),
            whole(5, LANES),
            whole(*tile_shape),
        ],
        [vmem] * (4 + len(strips)),
    )(right_side, conduct, tile_route, even, *strips)
    *late_arrays, swapped, fix, summary = call(
        functools.partial(late_kernel, nd, nc, tiles, rows),
        [whole(*span_shape(late[n], wide, layers)) for n in LATE_KEPT]
        + [whole(4 * HALF, LANES), whole(packs, *tile_shape), whole(1, LANES)],
        [vmem] * (len(odd) + len(first_part)),
        scratch=[pltpu.VMEM(span_shape(late[n], wide, layers), FLOAT) for n in LATE_SCRATCH],
    )(*odd, *first_part)
    early_arrays = dict(zip(EARLY, first_part))
    late_arrays = dict(zip(LATE_KEPT, late_arrays))

    partner = lax.ppermute(swapped, axes, pairs_of(nd, nc, False, None))
    state, chunks = call(
        functools.partial(spread_kernel, nd, nc, tiles),
        [whole(rows + 4, wide, layers), whole(nd * nc * CHUNK, LANES)],
        [vmem] * 5,
    )(fix, swapped, summary, early_arrays["pres"], late_arrays["pres"])
    chunks = call(
        functools.partial(relay_kernel, nd, nc),
        whole(nd * nc * CHUNK, LANES),
        [vmem, vmem],
    )(chunks, partner)
    chunks = chunks.reshape(nd * nc, CHUNK, 1, LANES)
    arrived = lax.all_to_all(chunks, axes, 0, 0, tiled=True).reshape(nd * nc * CHUNK, LANES)
    return call(
        functools.partial(last_kernel, nd, nc, tiles),
        block,
        [vmem] * (3 + 2 * len(KEPT)),
        scratch=[
            pltpu.VMEM((nc, nd, LANES), FLOAT),
            pltpu.VMEM((rows + 4, wide, layers), FLOAT),
            pltpu.VMEM((rows + 2, wide, layers), FLOAT),
        ],
    )(arrived, partner, state, *(early_arrays[n] for n in KEPT), *(late_arrays[n] for n in KEPT))


def solution(mesh):
    return jax.shard_map(
        functools.partial(body, mesh.shape["down"], mesh.shape["cross"]),
        mesh=mesh,
        in_specs=(
            P("down", "cross", None),
            P("down", "cross", None),
            P("down", "cross", None),
            P("down", "cross"),
        ),
        out_specs=P("down", "cross", None),
        check_vma=False,
    )
```

time: 33.3 us -> 30.9 us (0.928)
  waiting for transfers between devices: 5.69 us -> 3.76 us
  blocking collectives: 14.4 us -> 15.2 us
  starting transfers between devices: 7.17 us -> 6.43 us
  Pallas kernels: 5.8 us -> 5.26 us
    ppermute x3, waiting for transfers between devices: 4.85 us -> 0.83 us  [body(): received = [lax.ppermute(m, axes, p) for m, p in zip(messages, perms)]]
    ppermute x1, waiting for transfers between devices: 0.01 us -> 2.42 us  [body(): lax.ppermute(m, axes, pairs_of(nd, nc, None, cross_kind))]
    all_to_all x1, blocking collectives: 14.4 us -> 15.2 us  [body(): lax.all_to_all(chunks, axes, 0, 0, tiled=True)]
    ppermute x1, starting transfers between devices: 2.98 us -> 2.23 us  [body(): partner = lax.ppermute(swapped, axes, pairs_of(nd, nc, False, None))]
    pallas_call x4 -> x6, Pallas kernels: 5.78 us -> 5.24 us  [the longest x1 1.9 us: body(): call(functools.partial(last_kernel, nd, nc, tiles), block, [vmem] * (3 +...]
  transfers between devices with their start and end apart: 5 -> 5, of which waited for: 3 -> 4; matrix products, arithmetic and copies ran while one was open for 0% -> 0% of each run, Pallas kernels for 0% -> 5%
where the time goes in v3:
time: 30.9 us; the launch traced here: 30.7 us
  blocking collectives  15.2 us (49%)
  starting transfers between devices  6.43 us (21%)
  Pallas kernels  5.26 us (17%)
  waiting for transfers between devices  3.76 us (12%)
    all_to_all x1, blocking collectives, body(): lax.all_to_all(chunks, axes, 0, 0, tiled=True)  15.2 us
    ppermute x1, starting transfers between devices, body(): lax.ppermute(m, axes, pairs_of(nd, nc, None, cross_kind))  2.92 us
    ppermute x1, waiting for transfers between devices, body(): lax.ppermute(m, axes, pairs_of(nd, nc, None, cross_kind))  2.42 us
    ppermute x1, starting transfers between devices, body(): partner = lax.ppermute(swapped, axes, pairs_of(nd, nc, False, None))  2.23 us
    pallas_call x1, Pallas kernels, body(): call(functools.partial(last_kernel, nd, nc, tiles), block, [vmem] * (3 +...  1.9 us
    ppermute x3, starting transfers between devices, body(): received = [lax.ppermute(m, axes, p) for m, p in zip(messages, perms)]  1.27 us
    pallas_call x1, Pallas kernels, body(): call(functools.partial(pack_kernel, nd, nc), [block] + shapes + strips, [...  1.18 us
    pallas_call x1, Pallas kernels, body(): call(functools.partial(early_kernel, nd, nc, tiles), [whole(*span_shape(e...  1.09 us
  transfers between devices with their start and end apart: 5, of which 4 were waited for; matrix products, arithmetic and copies ran while one was open for 0% of the time, Pallas kernels for 5%

profile of v3, /device:TPU:0, one launch (start us, length us, event | category | flops | bytes accessed | tf_op | source)
XLA Modules:
  0.0 30.7 jit_solution(12273511955465002735)
XLA Ops:
  0.0 1.2 %shard_map.46 = (f32[8,32,256]{2,1,0:T(8,128)S(1)}, f32[7,32,256]{2,1,0:T(8,128)S(1)}, f32[7,32,256]{2,1,0:T(8,128)S(1)}, f32[3,8,256]{2,1,0:T(8,128)S(1)}, f32[8,8,256]{2,1,0:T(8,128)S(1)}) custom-call(f32[8,32,256]{2,1,0:T(8,128)} %rhs.1, f32[8,32,256]{2,1,0:T(8,128)} %kappa_hbm.1, s32[8,32,256]{2,1,0:T(8,128)} %mask_hbm.1), custom_call_target="tpu_custom_call" | custom-call | tf_op jit(solution)/shard_map/pallas_call | solution.py:700
  1.2 0.0 copy-start
  1.2 0.5 %collective-permute-start.2 = (f32[7,32,256]{2,1,0:T(8,128)S(1)}, f32[7,32,256]{2,1,0:T(8,128)S(1)}, u32[]{:S(2)}, u32[]{:S(2)}) collective-permute-start(f32[7,32,256]{2,1,0:T(8,128)S(1)} %get-tuple-element.38), channel_id=1, source_target_pairs={{0,2},{1,3},{2,0},{3,1},{4,6},{5,7},{6,4},{7,5},{8,10},{9,11},{10,... | collective-permute-start | bytes 688136 | tf_op jit(solution)/shard_map/ppermute | solution.py:713
  1.7 0.7 %collective-permute-start = (f32[7,32,256]{2,1,0:T(8,128)S(1)}, f32[7,32,256]{2,1,0:T(8,128)S(1)}, u32[]{:S(2)}, u32[]{:S(2)}) collective-permute-start(f32[7,32,256]{2,1,0:T(8,128)S(1)} %get-tuple-element.35), channel_id=1, source_target_pairs={{0,0},{1,1},{2,4},{3,5},{4,2},{5,3},{6,8},{7,9},{8,6},{9,7},{10,12... | collective-permute-start | bytes 688136 | tf_op jit(solution)/shard_map/ppermute | solution.py:713
  2.4 0.4 %collective-permute-done.2.even = f32[7,32,256]{2,1,0:T(8,128)S(1)} collective-permute-done((f32[7,32,256]{2,1,0:T(8,128)S(1)}, f32[7,32,256]{2,1,0:T(8,128)S(1)}, u32[]{:S(2)}, u32[]{:S(2)}) %collective-permute-start.2) | collective-permute-done | bytes 229408 | tf_op jit(solution)/shard_map/ppermute | solution.py:713
  2.8 2.9 %collective-permute-start.3 = (f32[11,8,256]{2,1,0:T(8,128)S(1)}, f32[11,8,256]{2,1,0:T(8,128)S(1)}, u32[]{:S(2)}, u32[]{:S(2)}) collective-permute-start(f32[11,8,256]{2,1,0:T(8,128)S(1)} %shard_map.47), channel_id=1, source_target_pairs={{0,1},{1,0},{2,3},{3,2},{4,5},{5,4},{6,7},{7,6},{8,9},{9,8},{10,11... | collective-permute-start | bytes 270344 | tf_op jit(solution)/shard_map/ppermute | solution.py:722
  5.8 0.0 copy-start.1
  5.8 0.1 collective-permute-start.1
  5.9 2.4 %collective-permute-done.3.refs_0_ = f32[11,8,256]{2,1,0:T(8,128)S(1)} collective-permute-done((f32[11,8,256]{2,1,0:T(8,128)S(1)}, f32[11,8,256]{2,1,0:T(8,128)S(1)}, u32[]{:S(2)}, u32[]{:S(2)}) %collective-permute-start.3) | collective-permute-done | bytes 90144 | tf_op jit(solution)/shard_map/ppermute | solution.py:722
  8.3 0.0 copy-done
  8.3 0.0 copy-done.1
  8.3 1.1 %shard_map.48 = (f32[12,40,256]{2,1,0:T(8,128)S(1)}, f32[11,40,256]{2,1,0:T(8,128)S(1)}, f32[10,40,256]{2,1,0:T(8,128)S(1)}, f32[10,40,256]{2,1,0:T(8,128)S(1)},...) custom-call(f32[8,32,256]{2,1,0:T(8,128)S(1)} %copy-done, ...), custom_call_target="tpu_custom_call" | custom-call | tf_op jit(solution)/shard_map/pallas_call | solution.py:728
  9.4 0.4 %collective-permute-done.1.refs_0_ = f32[3,8,256]{2,1,0:T(8,128)S(1)} collective-permute-done((f32[3,8,256]{2,1,0:T(8,128)S(1)}, f32[3,8,256]{2,1,0:T(8,128)S(1)}, u32[]{:S(2)}, u32[]{:S(2)}) %collective-permute-start.1) | collective-permute-done | bytes 24608 | tf_op jit(solution)/shard_map/ppermute | solution.py:713
  9.8 0.0 collective-permute-done.odd
  9.8 0.7 %shard_map.49 = (f32[3,40,256]{2,1,0:T(8,128)S(1)}, f32[4,40,256]{2,1,0:T(8,128)S(1)}, f32[3,40,256]{2,1,0:T(8,128)S(1)}, f32[2,40,256]{2,1,0:T(8,128)S(1)}, f32...) custom-call(f32[7,32,256]{2,1,0:T(8,128)S(1)} %collective-permute-do, ...), custom_call_target="tpu_custom_call" | custom-call | tf_op jit(solution)/shard_map/pallas_call | solution.py:740
  10.5 2.2 %collective-permute-start.4 = (f32[32,128]{1,0:T(8,128)S(1)}, f32[32,128]{1,0:T(8,128)S(1)}, u32[]{:S(2)}, u32[]{:S(2)}) collective-permute-start(f32[32,128]{1,0:T(8,128)S(1)} %get-tuple-element.55.swapped), channel_id=1, source_target_pairs={{0,2},{1,3},{2,0},{3,1},{4,6},{5,7},{6,4},{7,5},{8,10},{9,11},{10,... | collective-permute-start | bytes 49160 | tf_op jit(solution)/shard_map/ppermute | solution.py:750
  12.8 0.3 %shard_map.50 = (f32[12,40,256]{2,1,0:T(8,128)S(1)}, f32[288,128]{1,0:T(8,128)S(1)}) custom-call(f32[2,2,8,256]{3,2,1,0:T(8,128)S(1)} %get-tuple-element.54.fix, f32[32,128]{1,0:T(8,128)S(1)} %get-tuple-element.55.swapped, f32[1,128]{1,0:T(1,128)S(1)} %get-tuple-element.56.summary, f32[8,40,256]{2,1,0:T(8,128)S(1)} %get-tuple-element.48.refs_9_.pres_early, ...), custom_call_target="tpu_custom_call" | custom-call | tf_op jit(solution)/shard_map/pallas_call | solution.py:751
  13.1 0.5 %collective-permute-done.4.swapped = f32[32,128]{1,0:T(8,128)S(1)} collective-permute-done((f32[32,128]{1,0:T(8,128)S(1)}, f32[32,128]{1,0:T(8,128)S(1)}, u32[]{:S(2)}, u32[]{:S(2)}) %collective-permute-start.4) | collective-permute-done | bytes 16416 | tf_op jit(solution)/shard_map/ppermute | solution.py:750
  13.6 15.2 %all_to_all.5 = f32[32,9,1,128]{3,2,1,0:T(1,128)S(1)} all-to-all(f32[32,9,1,128]{3,2,1,0:T(1,128)S(1)} %bitcast.3), channel_id=1, replica_groups=mesh['down'=16,'cross'=2] {'down','cross'}, dimensions={0} | all-to-all | bytes 294912 | tf_op jit(solution)/shard_map/all_to_all | solution.py:762
  28.8 1.9 %shard_map.52 = f32[8,32,256]{2,1,0:T(8,128)} custom-call(f32[288,128]{1,0:T(8,128)S(1)} %bitcast.2, f32[32,128]{1,0:T(8,128)S(1)} %collective-permute-done.4.swapped, f32[12,40,256]{2,1,0:T(8,128)S(1)} %get-tuple-element.59.state, f32[11,40,256]{2,1,0:T(8,128)S(1)} %get-tuple-element.41.refs_2_.refs_0_, ...), custom_call_target="tpu_custom_call" | custom-call | tf_op jit(solution)/shard_map/pallas_call | solution.py:763
  (2 shorter events, 0.0 us)
Async XLA Ops:
  1.2 7.1 %copy-start = (f32[8,32,256]{2,1,0:T(8,128)S(1)}, f32[8,32,256]{2,1,0:T(8,128)}, u32[]{:S(2)}) copy-start(f32[8,32,256]{2,1,0:T(8,128)} %rhs.1) | copy-start | bytes 786436
  1.2 1.6 %collective-permute-start.2 = (f32[7,32,256]{2,1,0:T(8,128)S(1)}, f32[7,32,256]{2,1,0:T(8,128)S(1)}, u32[]{:S(2)}, u32[]{:S(2)}) collective-permute-start(f32[7,32,256]{2,1,0:T(8,128)S(1)} %get-tuple-element.38), channel_id=1, source_target_pairs={{0,2},{1,3},{2,0},{3,1},{4,6},{5,7},{6,4},{7,5},{8,10},{9,11},{10,... | collective-permute-start | bytes 688136 | tf_op jit(solution)/shard_map/ppermute | solution.py:713
  1.7 8.1 %collective-permute-start = (f32[7,32,256]{2,1,0:T(8,128)S(1)}, f32[7,32,256]{2,1,0:T(8,128)S(1)}, u32[]{:S(2)}, u32[]{:S(2)}) collective-permute-start(f32[7,32,256]{2,1,0:T(8,128)S(1)} %get-tuple-element.35), channel_id=1, source_target_pairs={{0,0},{1,1},{2,4},{3,5},{4,2},{5,3},{6,8},{7,9},{8,6},{9,7},{10,12... | collective-permute-start | bytes 688136 | tf_op jit(solution)/shard_map/ppermute | solution.py:713
  2.8 5.4 %collective-permute-start.3 = (f32[11,8,256]{2,1,0:T(8,128)S(1)}, f32[11,8,256]{2,1,0:T(8,128)S(1)}, u32[]{:S(2)}, u32[]{:S(2)}) collective-permute-start(f32[11,8,256]{2,1,0:T(8,128)S(1)} %shard_map.47), channel_id=1, source_target_pairs={{0,1},{1,0},{2,3},{3,2},{4,5},{5,4},{6,7},{7,6},{8,9},{9,8},{10,11... | collective-permute-start | bytes 270344 | tf_op jit(solution)/shard_map/ppermute | solution.py:722
  5.8 2.5 %copy-start.1 = (s32[1,4]{1,0:T(1,128)S(1)}, s32[1,4]{1,0:T(1,128)}, u32[]{:S(2)}) copy-start(s32[1,4]{1,0:T(1,128)} %route.1) | copy-start | bytes 52
  5.8 4.0 %collective-permute-start.1 = (f32[3,8,256]{2,1,0:T(8,128)S(1)}, f32[3,8,256]{2,1,0:T(8,128)S(1)}, u32[]{:S(2)}, u32[]{:S(2)}) collective-permute-start(f32[3,8,256]{2,1,0:T(8,128)S(1)} %get-tuple-element.36), channel_id=1, source_target_pairs={{0,1},{1,0},{2,5},{3,4},{4,3},{5,2},{6,9},{7,8},{8,7},{9,6},{10,13... | collective-permute-start | bytes 73736 | tf_op jit(solution)/shard_map/ppermute | solution.py:713
  10.5 3.1 %collective-permute-start.4 = (f32[32,128]{1,0:T(8,128)S(1)}, f32[32,128]{1,0:T(8,128)S(1)}, u32[]{:S(2)}, u32[]{:S(2)}) collective-permute-start(f32[32,128]{1,0:T(8,128)S(1)} %get-tuple-element.55.swapped), channel_id=1, source_target_pairs={{0,2},{1,3},{2,0},{3,1},{4,6},{5,7},{6,4},{7,5},{8,10},{9,11},{10,... | collective-permute-start | bytes 49160 | tf_op jit(solution)/shard_map/ppermute | solution.py:750

commit v4 on v3

--- a/solution.py
+++ b/solution.py
@@ -17,10 +17,10 @@
 CORNER = DEPTH - 1
 STRIP = 8
 LANES = 128
-HALF = 8
-CHUNK = HALF + 1
+LINES = 4
+CHUNK = LINES + 1
 FLOAT = jnp.float32
-VMEM_BYTES = 48 * 1024 * 1024
+VMEM_BYTES = 24 * 1024 * 1024
 
 
 def partners(count, odd):
@@ -113,7 +113,7 @@
     return jnp.where(right == (i % 2 == 0), tile, roll(tile, STRIP // 2, 0))
 
 
-def pack_kernel(nd, nc, rhs_hbm, kappa_hbm, mask_hbm, conduct, *refs):
+def pack_kernel(nd, nc, rhs_hbm, kappa_hbm, mask_hbm, conduct, more, *refs):
     *messages, rhs, kappa, mask, sems = refs
     rows, cols, _ = rhs.shape
     messages = iter(messages)
@@ -130,13 +130,15 @@
         at = counted(x, rows)
         conduct[x] = kappa[at] / (1.0 + SNOW_FACTOR * mask[at].astype(FLOAT))
     copies[2].wait()
+    more[0], more[1] = conduct[DEPTH - 1], rhs[counted(DEPTH - 2, rows)]
     for kind in pairings(nd):
         near = [i if kind else rows - 1 - i for i in range(DEPTH)]
+        depth = DEPTH - 1 if kind else DEPTH
         out = next(messages)
-        for i, x in enumerate(near):
+        for i, x in enumerate(near[:depth]):
             out[i] = conduct[x]
-        for i, x in enumerate(near[:-1]):
-            out[DEPTH + i] = rhs[counted(x, rows)]
+        for i, x in enumerate(near[: depth - 1]):
+            out[depth + i] = rhs[counted(x, rows)]
         if kind:
             for cross_kind in pairings(nc):
                 right, _ = facing(cross, nc, cross_kind)
@@ -214,16 +216,19 @@
     def row(self, own, halo):
         return jnp.concatenate([own, halo], axis=0)
 
-    def weights(self, q, gain, src, first, diag, wx, wy, wz, x, valid=None):
-        here = q[x]
+    def diagonal(self, low, here, high, valid=None):
         above = jnp.where(self.last_lane, 0.0, roll(here, -1, 1))
         below = jnp.where(self.lane == 0, 0.0, roll(here, 1, 1))
         right = roll(here, -1, 0)
-        doubled = 6.0 * here + (q[x - 1] + q[x + 1]) + (right + roll(here, 1, 0)) + (above + below)
+        doubled = 6.0 * here + (low + high) + (right + roll(here, 1, 0)) + (above + below)
         ok = self.col_ok & (doubled > 0.0)
         if valid is not None:
             ok = ok & valid
-        gain_here = jnp.where(ok, (2.0 * OMEGA) / doubled, 0.0)
+        return doubled, jnp.where(ok, (2.0 * OMEGA) / doubled, 0.0), right, above
+
+    def weights(self, q, gain, src, first, diag, wx, wy, wz, x, valid=None):
+        here = q[x]
+        doubled, gain_here, right, above = self.diagonal(q[x - 1], here, q[x + 1], valid)
         gain[x] = gain_here
         first[x] = gain_here * src[x]
         if diag is not None:
@@ -250,15 +255,15 @@
         wx=(0, far - 2), wy=(0, rows + 2), wz=(0, rows + 2), pres=(2, rows + 2),
     )
     late = dict(
-        q=(-DEPTH, 0), src=(1 - DEPTH, 0), gain=(1 - DEPTH, 1), first=(1 - DEPTH, 1), diag=(0, 1),
-        wx=(1 - DEPTH, 0), wy=(-2, 0), wz=(-2, 0), pres=(-2, 2),
+        q=(1 - DEPTH, 0), src=(2 - DEPTH, 0), gain=(2 - DEPTH, 1), first=(2 - DEPTH, 1), diag=(0, 1),
+        wx=(2 - DEPTH, 0), wy=(-1, 0), wz=(-1, 0), pres=(-1, 2),
     )
     return early, late
 
 
 EARLY = ("q", "src", "gain", "first", "diag", "wx", "wy", "wz", "pres")
-LATE_KEPT = ("src", "gain", "wx", "wy", "wz", "pres")
-LATE_SCRATCH = ("q", "first", "diag")
+LATE_KEPT = ("src", "gain", "wx", "wy", "wz", "pres", "q", "first")
+LATE_SCRATCH = ("diag",)
 
 
 def span_shape(span, wide, layers):
@@ -373,15 +378,15 @@
         coef[2 * packs + k] = jnp.where(z_end, 0.0, 2.0 * (c + z_high))
 
 
-def late_kernel(nd, nc, tiles, rows, odd, *refs):
+def late_kernel(nd, nc, tiles, rows, more, odd, *refs):
     n_cross = len(pairings(nc)) if len(pairings(nd)) > 1 else 0
     corners = refs[:n_cross]
     n_in = n_cross + len(EARLY) + 5
     early_refs = dict(zip(EARLY, refs[n_cross:]))
     res_coarse, res_row, coef, sums, touched = refs[n_in - 5 : n_in]
-    names = LATE_KEPT + ("swapped", "fix", "summary") + LATE_SCRATCH
+    names = LATE_KEPT + ("fix", "near", "far", "chunks") + LATE_SCRATCH
     late_refs = dict(zip(names, refs[n_in:]))
-    swapped, fix_out, summary = (late_refs[n] for n in ("swapped", "fix", "summary"))
+    fix_out, near_out, far_out, chunks = (late_refs[n] for n in ("fix", "near", "far", "chunks"))
     wide, layers = early_refs["q"].shape[1:]
     cols = wide - STRIP
     tile_w = cols // tiles
@@ -395,19 +400,17 @@
     _, late = spans(rows)
 
     valid = beside(down, nd, jnp.where(even, -1, 1))
-    blank = jnp.zeros((STRIP, layers), FLOAT)
-    for i in range(DEPTH):
-        corner = frame.merged(corners, 0, i) if i < DEPTH - 1 else blank
-        q[-1 - i] = jnp.where(valid, frame.row(odd[i], corner), 0.0)
     for i in range(DEPTH - 1):
-        corner = frame.merged(corners, 0, DEPTH - 1 + i) if i < DEPTH - 2 else blank
-        src[-1 - i] = jnp.where(valid, frame.row(odd[DEPTH + i], corner), 0.0)
+        q[-1 - i] = jnp.where(valid, frame.row(odd[i], frame.merged(corners, 0, i)), 0.0)
+    for i in range(DEPTH - 2):
+        corner = frame.merged(corners, 0, DEPTH - 1 + i)
+        src[-1 - i] = jnp.where(valid, frame.row(odd[DEPTH - 1 + i], corner), 0.0)
     for x in range(*late["gain"]):
         frame.weights(
             q, gain, src, first,
             diag if x == 0 else None,
             wx if x < 0 else None,
-            wy if -2 <= x < 0 else None,
+            wy if x == -1 else None,
             wz, x, valid if x < 0 else None,
         )
     for x in range(*late["pres"]):
@@ -423,7 +426,7 @@
     lines = jnp.concatenate([res_total, 0.25 * link_down, 0.25 * link_cross, 0.25 * outflow])
     lines = jnp.sum(lines, axis=1, keepdims=True)
     line = iota((1, LANES), 1)
-    summary[...] = jnp.where(
+    summary = jnp.where(
         line == 0, lines[0:1], jnp.where(line == 1, lines[1:2], jnp.where(line == 2, lines[2:3], lines[3:4]))
     )
 
@@ -453,92 +456,44 @@
     for k in range(packs):
         fix_out[k] = fix[k]
 
-    def rim(k, j):
-        part = unpack_pairs(fix[k], 1)[j]
-        sub = iota((tile_w, layers), 0) % couples
-        packed = part[0]
+    parts = [unpack_pairs(fix[k % packs], 1)[k // packs] for k in range(rows // 2)]
+    sub = iota((tile_w, layers), 0) % couples
+
+    def rim(row):
+        packed = parts[row][0]
         for t in range(1, couples):
-            packed = jnp.where(sub == t, part[t], packed)
-        return packed[:, :LANES], packed[:, LANES:]
-
-    even_rim, odd_rim = rim(packs - 1, 1), rim(0, 0)
-    swapped[:HALF] = even_rim[0]
-    swapped[HALF : 2 * HALF] = even_rim[1]
-    swapped[2 * HALF : 3 * HALF] = odd_rim[1]
-    swapped[3 * HALF :] = odd_rim[0]
-
-
-def spread_kernel(nd, nc, tiles, fix, swapped, summary, pres_early, pres_late, state, chunks):
-    packs, couples, tile_w, layers = fix.shape
-    rows = 4 * packs
-    cols = tiles * tile_w
-    own, halo = slice(0, cols), slice(cols, cols + STRIP)
-    down, cross = lax.axis_index("down"), lax.axis_index("cross")
-    pres = joined(rows, "pres", pres_early, pres_late)
-
-    fine = [None] * (rows // 2)
-    for k in range(packs):
-        for j, part in enumerate(unpack_pairs(fix[k], 1)):
-            both = unpack_pairs(part, 2)
-            fine[k + j * packs] = jnp.stack(both, axis=1).reshape(cols, layers)
-
-    for x in range(-2, rows + 2):
-        value = pres[x]
-        if 0 <= x < rows:
-            state[x + 2, own, :] = value[own] + fine[x // 2]
-            state[x + 2, halo, :] = value[halo]
-        else:
-            state[x + 2] = value
-
-    blank = jnp.zeros((HALF, LANES), FLOAT)
-    sums = summary[...]
-
-    def fill(b, carry):
-        at = b * CHUNK
-        chunks[pl.ds(at, HALF), :] = blank
-        chunks[pl.ds(at + HALF, 1), :] = sums
-        return carry
-
-    lax.fori_loop(0, nd * nc, fill, 0)
+            packed = jnp.where(sub == t, parts[row][t], packed)
+        return packed
+
+    near_out[...] = rim(rows // 2 - 1)
+    far_out[2 * cols :] = rim(0)
+    far_out[:cols], far_out[cols : 2 * cols] = more[0], more[1]
+
+    chunks[pl.ds(LINES, nd * nc, stride=CHUNK), :] = jnp.broadcast_to(summary, (nd * nc, LANES))
+    cross = lax.axis_index("cross")
     me = down * nc + cross
-    odd_step = jnp.where(down % 2 == 0, -1, 1)
-
-    @pl.when(beside(down, nd, odd_step))
-    def _():
-        chunks[pl.ds((me + odd_step * nc) * CHUNK, HALF), :] = swapped[3 * HALF :]
-
+    odd_step = jnp.where(even, -1, 1)
     for dy in (-1, 1):
-        column = 0 if dy < 0 else cols - 1
+        at_couple, at_col = (0, 0) if dy < 0 else (couples - 1, tile_w - 1)
+        edge = jnp.concatenate([p[at_couple][at_col : at_col + 1] for p in parts])
+        edge = unpack_pairs(edge, 1)[0 if dy < 0 else 1]
+        even_lane = iota((1, layers), 1) % 2 == 0
+        pairs = [jnp.where(even_lane, edge[k : k + 1], edge[k + 1 : k + 2]) for k in range(0, rows // 2, 2)]
+
+        def put(step, lines):
+            at = (me + dy + step * nc) * CHUNK
+            for i, line in enumerate(lines):
+                chunks[pl.ds(at + 2 * i, 1), :] = line[:, :LANES]
+                chunks[pl.ds(at + 2 * i + 1, 1), :] = line[:, LANES:]
 
         @pl.when(beside(cross, nc, dy))
-        def _(dy=dy, column=column):
-            lines = []
-            for k in range(rows // 2):
-                f = fine[k][column : column + 1]
-                lines += [f[:, :LANES], f[:, LANES:]]
-            at = (me + dy) * CHUNK
-            for i, f in enumerate(lines):
-                chunks[pl.ds(at + i, 1), :] = f
-            for side in (0, 1):
-                dx = -odd_step if side else odd_step
-
-                @pl.when(beside(down, nd, dx))
-                def _(side=side, dx=dx):
-                    at = (me + dy + dx * nc) * CHUNK
-                    pair = lines[-2:] if side else lines[:2]
-                    chunks[pl.ds(at, 1), :] = pair[0]
-                    chunks[pl.ds(at + 1, 1), :] = pair[1]
-
-
-def relay_kernel(nd, nc, chunks_in, swapped, chunks):
-    chunks[...] = chunks_in[...]
-    down, cross = lax.axis_index("down"), lax.axis_index("cross")
-    step = jnp.where(down % 2 == 0, 2, -2)
-
-    @pl.when(beside(down, nd, step))
-    def _():
-        at = ((down + step) * nc + cross) * CHUNK
-        chunks[pl.ds(at, HALF), :] = swapped[2 * HALF : 3 * HALF]
+        def _(put=put, edge=edge, pairs=pairs):
+            put(0, pairs)
+            for k, step in ((0, odd_step), (rows // 2 - 1, -odd_step)):
+
+                @pl.when(beside(down, nd, step))
+                def _(k=k, step=step):
+                    put(step, [edge[k : k + 1]])
 
 
 def coarse_solve(totals, outflow, link_down, link_up, link_cross):
@@ -578,18 +533,37 @@
 KEPT = ("src", "gain", "wx", "wy", "wz")
 
 
-def last_kernel(nd, nc, tiles, got, swapped, state, *refs):
+def around(nd, nc, step, dy):
+    row = jnp.clip(lax.axis_index("down") + step, 0, nd - 1)
+    return row, jnp.clip(lax.axis_index("cross") + dy, 0, nc - 1)
+
+
+def second_row(nd, nc, frame, more, q_ref, first_ref, src, gain, wx):
+    valid = beside(lax.axis_index("down"), nd, jnp.where(lax.axis_index("down") % 2 == 0, -1, 1))
+    q, first = Rows((q_ref, 1 - DEPTH, DEPTH - 1)), Rows((first_ref, 2 - DEPTH, DEPTH - 1))
+    blank = jnp.zeros((STRIP, frame.layers), FLOAT)
+    q_far = jnp.where(valid, frame.row(more[0], blank), 0.0)
+    src_far = jnp.where(valid, frame.row(more[1], blank), 0.0)
+    _, gain_far, _, _ = frame.diagonal(q_far, q[-3], q[-2], valid)
+    here = q[-2]
+    above = jnp.where(frame.last_lane, 0.0, roll(here, -1, 1))
+    wy, wz = 0.5 * (here + roll(here, -1, 0)), jnp.where(frame.last_lane, 0.0, 0.5 * (here + above))
+    spread = gather(first[-2], gain_far * src_far, first[-1], 0.5 * (q[-3] + here), wx[-2], wy, wz)
+    return KEEP * first[-2] + gain[-2] * (src[-2] + spread)
+
+
+def middle_kernel(nd, nc, tiles, got, fix, pres_early, pres_late, *refs):
     early = dict(zip(KEPT, refs))
     late = dict(zip(KEPT, refs[len(KEPT) :]))
-    out, bricks, pres_ref, third_ref = refs[2 * len(KEPT) :]
-    rows, cols, layers = out.shape
+    pres_ref, third_ref, out, bricks = refs[2 * len(KEPT) :]
+    packs, couples, tile_w, layers = fix.shape
+    rows, cols = 4 * packs, tiles * tile_w
     src, gain, wx, wy, wz = (joined(rows, n, early[n], late[n]) for n in KEPT)
-    tile_w = cols // tiles
-    couples = tiles // 2
+    start = joined(rows, "pres", pres_early, pres_late)
     down, cross = lax.axis_index("down"), lax.axis_index("cross")
     own, halo = slice(0, cols), slice(cols, cols + STRIP)
 
-    tables = [got[pl.ds(c * CHUNK + HALF, nd, stride=nc * CHUNK), :] for c in range(nc)]
+    tables = [got[pl.ds(c * CHUNK + LINES, nd, stride=nc * CHUNK), :] for c in range(nc)]
 
     def spread_lane(table, at):
         return jnp.broadcast_to(table[:, at : at + 1], (nd, LANES))
@@ -604,16 +578,75 @@
     for c in range(nc):
         bricks[c] = answer[c]
 
-    def brick(dx, dy):
-        line = bricks[jnp.clip(cross + dy, 0, nc - 1), pl.ds(jnp.clip(down + dx, 0, nd - 1), 1), :]
-        return jnp.concatenate([line] * (layers // LANES), axis=1)
-
-    def lines(dx, dy, count):
-        row, col = jnp.clip(down + dx, 0, nd - 1), jnp.clip(cross + dy, 0, nc - 1)
-        return got[pl.ds((row * nc + col) * CHUNK, count), :]
-
-    def line_pair(block, k):
-        return jnp.concatenate([block[2 * k : 2 * k + 1], block[2 * k + 1 : 2 * k + 2]], axis=1)
+    def brick(step, dy):
+        row, col = around(nd, nc, step, dy)
+        return jnp.concatenate([bricks[col, pl.ds(row, 1), :]] * (layers // LANES), axis=1)
+
+    def lines(step, dy, count):
+        row, col = around(nd, nc, step, dy)
+        at = (row * nc + col) * CHUNK
+        return [
+            jnp.concatenate([got[pl.ds(at + i, 1), :], got[pl.ds(at + i + 1, 1), :]], axis=1)
+            for i in range(0, count, 2)
+        ]
+
+    fine = [None] * (rows // 2)
+    for k in range(packs):
+        for j, part in enumerate(unpack_pairs(fix[k], 1)):
+            both = unpack_pairs(part, 2)
+            fine[k + j * packs] = jnp.stack(both, axis=1).reshape(cols, layers)
+
+    half = STRIP // 2
+    halo_col = iota((STRIP, layers), 0)
+    right = halo_col < half
+    there = (halo_col < jnp.where(cross < nc - 1, half, 0)) | (
+        halo_col >= jnp.where(cross > 0, half, STRIP)
+    )
+    pres = Rows((pres_ref, -2, rows + 4))
+    third = Rows((third_ref, 1, rows - 2))
+    mine = brick(0, 0)
+    side_bricks = brick(0, 1), brick(0, -1)
+    side_lines = [
+        [line for pair in lines(0, dy, LINES) for line in unpack_pairs(pair, 1)] for dy in (1, -1)
+    ]
+    for k in range(rows // 2):
+        extra = jnp.where(right, *(f[k] + b for f, b in zip(side_lines, side_bricks)))
+        extra = jnp.where(there, extra, 0.0)
+        for x in (2 * k, 2 * k + 1):
+            value = start[x]
+            pres_ref[x + 2, own, :] = value[own] + (fine[k] + mine)
+            pres_ref[x + 2, halo, :] = value[halo] + extra
+    odd_step = jnp.where(down % 2 == 0, -1, 1)
+    for step, xs in ((odd_step, (-2, -1)), (-odd_step, (rows, rows + 1))):
+        valid = beside(down, nd, step)
+        row = jnp.where(valid, brick(step, 0), 0.0)
+        corner = jnp.where(
+            right, *(lines(step, dy, 2)[0] + brick(step, dy) for dy in (1, -1))
+        )
+        corner = jnp.where(there & valid, corner, 0.0)
+        for x in xs:
+            value = start[x] if x > -2 else jnp.zeros((cols + STRIP, layers), FLOAT)
+            pres_ref[x + 2, own, :] = value[own] + row
+            pres_ref[x + 2, halo, :] = value[halo] + corner
+
+    for x in range(1, rows - 1):
+        third[x] = smooth(pres, gain, src, wx, wy, wz, x)
+    for x in range(2, rows - 2):
+        out[counted(x, rows) - 2] = smooth(third, gain, src, wx, wy, wz, x)[own]
+
+
+def last_kernel(nd, nc, tiles, near, far, q_late, first_late, pres_mid, third_mid, out_mid, *refs):
+    early = dict(zip(KEPT, refs))
+    late = dict(zip(KEPT, refs[len(KEPT) :]))
+    out, pres_edge, third_edge, out_edge, sems = refs[2 * len(KEPT) :]
+    rows, cols, layers = out.shape
+    src, gain, wx, wy, wz = (joined(rows, n, early[n], late[n]) for n in KEPT)
+    tile_w = cols // tiles
+    couples = tiles // 2
+    down = lax.axis_index("down")
+    own, halo = slice(0, cols), slice(cols, cols + STRIP)
+    copy_mid = pltpu.make_async_copy(out_mid, out.at[pl.ds(2, rows - 4)], sems.at[0])
+    copy_mid.start()
 
     def unpack(packed):
         sub = iota((tile_w, layers), 0) % couples
@@ -627,51 +660,44 @@
         return jnp.concatenate(parts, axis=0)
 
     odd_step = jnp.where(down % 2 == 0, -1, 1)
-    even_rim = jnp.concatenate([swapped[:HALF], swapped[HALF : 2 * HALF]], axis=1)
-    odd_rim = jnp.concatenate([lines(odd_step, 0, HALF), lines(2 * odd_step, 0, HALF)], axis=1)
-    right = iota((STRIP, layers), 0) < STRIP // 2
-    there = (iota((STRIP, layers), 0) < jnp.where(cross < nc - 1, STRIP // 2, 0)) | (
-        iota((STRIP, layers), 0) >= jnp.where(cross > 0, STRIP // 2, STRIP)
-    )
-
-    pres = Rows((pres_ref, -2, rows + 4))
-    third = Rows((third_ref, -1, rows + 2))
-    mine = brick(0, 0)
-    side_bricks = brick(0, 1), brick(0, -1)
-    side_lines = lines(0, 1, HALF), lines(0, -1, HALF)
-    for k in range(rows // 2):
-        extra = jnp.where(right, *(line_pair(f, k) + b for f, b in zip(side_lines, side_bricks)))
-        extra = jnp.where(there, extra, 0.0)
-        for x in (2 * k, 2 * k + 1):
-            pres_ref[x + 2, own, :] = state[x + 2, own, :] + mine
-            pres_ref[x + 2, halo, :] = state[x + 2, halo, :] + extra
-    for step, rim, at in ((odd_step, odd_rim, 0), (-odd_step, even_rim, rows + 2)):
-        valid = beside(down, nd, step)
-        row = jnp.where(valid, unpack(rim) + brick(step, 0), 0.0)
-        corner = jnp.where(
-            right, *(line_pair(lines(step, dy, 2), 0) + brick(step, dy) for dy in (1, -1))
-        )
-        corner = jnp.where(there & valid, corner, 0.0)
-        for i in (at, at + 1):
-            pres_ref[i, own, :] = state[i, own, :] + row
-            pres_ref[i, halo, :] = state[i, halo, :] + corner
-
-    for x in range(-1, rows + 1):
+    more = far[:cols], far[cols : 2 * cols]
+    even_rim, odd_rim = near[...], far[2 * cols :]
+    pres = Rows((pres_edge, -2, 2), (pres_mid.at[pl.ds(2, rows)], 0, rows), (pres_edge.at[pl.ds(2, 2)], rows, 2))
+    third = Rows((third_edge, -1, 2), (third_mid, 1, rows - 2), (third_edge.at[pl.ds(2, 2)], rows - 1, 2))
+    for step, rim, at, mid in ((odd_step, odd_rim, 0, 0), (-odd_step, even_rim, 2, rows + 2)):
+        extra = jnp.where(beside(down, nd, step), unpack(rim), 0.0)
+        for i in (0, 1):
+            pres_edge[at + i, own, :] = pres_mid[mid + i, own, :] + extra
+            pres_edge[at + i, halo, :] = pres_mid[mid + i, halo, :]
+    frame = Frame(nd, nc, cols, layers)
+    second = second_row(nd, nc, frame, more, q_late, first_late, src, gain, wx)
+    pres_edge[0] = pres_edge[0] + second
+    for x in (-1, 0, rows - 1, rows):
         third[x] = smooth(pres, gain, src, wx, wy, wz, x)
-    for x in range(rows):
-        out[counted(x, rows)] = smooth(third, gain, src, wx, wy, wz, x)[own]
+    copies = [copy_mid]
+    for side, xs in enumerate(((0, 1), (rows - 2, rows - 1))):
+        for x in xs:
+            at = counted(x, rows)
+            at = jnp.where(at < 2, at, at - (rows - 4))
+            out_edge[at] = smooth(third, gain, src, wx, wy, wz, x)[own]
+    for side, at in enumerate((0, rows - 2)):
+        copy = pltpu.make_async_copy(out_edge.at[pl.ds(2 * side, 2)], out.at[pl.ds(at, 2)], sems.at[1 + side])
+        copy.start()
+        copies.append(copy)
+    for copy in copies:
+        copy.wait()
 
 
 def whole(*shape):
     return jax.ShapeDtypeStruct(shape, FLOAT)
 
 
-def call(kernel, out_shape, spaces, scratch=(), vmem_bytes=VMEM_BYTES):
+def call(kernel, out_shape, spaces, scratch=(), vmem_bytes=VMEM_BYTES, out_space=pltpu.VMEM):
     return pl.pallas_call(
         kernel,
         out_shape=out_shape,
         in_specs=[pl.BlockSpec(memory_space=s) for s in spaces],
-        out_specs=jax.tree.map(lambda _: pl.BlockSpec(memory_space=pltpu.VMEM), out_shape),
+        out_specs=jax.tree.map(lambda _: pl.BlockSpec(memory_space=out_space), out_shape),
         scratch_shapes=list(scratch),
         compiler_params=pltpu.CompilerParams(vmem_limit_bytes=vmem_bytes),
     )
@@ -688,7 +714,7 @@
 
     shapes, perms = [], []
     for kind in pairings(nd):
-        shapes.append(whole(2 * DEPTH - 1, cols, layers))
+        shapes.append(whole(2 * DEPTH - (3 if kind else 1), cols, layers))
         perms.append(pairs_of(nd, nc, kind, None))
         if kind:
             for cross_kind in pairings(nc):
@@ -697,9 +723,9 @@
     strips = [whole(rows, STRIP, layers) for _ in pairings(nc)]
     packs, couples, tile_w = rows // 4, tiles // 2, cols // tiles
     tile_shape = (couples, tile_w, layers)
-    conduct, *messages = call(
+    conduct, more, *messages = call(
         functools.partial(pack_kernel, nd, nc),
-        [block] + shapes + strips,
+        [block, whole(2, cols, layers)] + shapes + strips,
         [pltpu.HBM] * 3,
         scratch=[
             pltpu.VMEM((rows, cols, layers), FLOAT),
@@ -723,7 +749,7 @@
             for m, cross_kind in zip(strips, pairings(nc))
         ]
     if not odd:
-        odd = [jnp.zeros((2 * DEPTH - 1, cols, layers), FLOAT)]
+        odd = [jnp.zeros((2 * DEPTH - 3, cols, layers), FLOAT)]
 
     first_part = call(
         functools.partial(early_kernel, nd, nc, tiles),
@@ -737,39 +763,48 @@
         ],
         [vmem] * (4 + len(strips)),
     )(right_side, conduct, tile_route, even, *strips)
-    *late_arrays, swapped, fix, summary = call(
+    *late_arrays, fix, near, far, chunks = call(
         functools.partial(late_kernel, nd, nc, tiles, rows),
         [whole(*span_shape(late[n], wide, layers)) for n in LATE_KEPT]
-        + [whole(4 * HALF, LANES), whole(packs, *tile_shape), whole(1, LANES)],
-        [vmem] * (len(odd) + len(first_part)),
+        + [
+            whole(packs, *tile_shape),
+            whole(tile_w, layers),
+            whole(2 * cols + tile_w, layers),
+            whole(nd * nc * CHUNK, LANES),
+        ],
+        [vmem] * (1 + len(odd) + len(first_part)),
         scratch=[pltpu.VMEM(span_shape(late[n], wide, layers), FLOAT) for n in LATE_SCRATCH],
-    )(*odd, *first_part)
+    )(more, *odd, *first_part)
     early_arrays = dict(zip(EARLY, first_part))
     late_arrays = dict(zip(LATE_KEPT, late_arrays))
-
-    partner = lax.ppermute(swapped, axes, pairs_of(nd, nc, False, None))
-    state, chunks = call(
-        functools.partial(spread_kernel, nd, nc, tiles),
-        [whole(rows + 4, wide, layers), whole(nd * nc * CHUNK, LANES)],
-        [vmem] * 5,
-    )(fix, swapped, summary, early_arrays["pres"], late_arrays["pres"])
-    chunks = call(
-        functools.partial(relay_kernel, nd, nc),
-        whole(nd * nc * CHUNK, LANES),
-        [vmem, vmem],
-    )(chunks, partner)
+    kept = [d[n] for d in (early_arrays, late_arrays) for n in KEPT]
+
     chunks = chunks.reshape(nd * nc, CHUNK, 1, LANES)
     arrived = lax.all_to_all(chunks, axes, 0, 0, tiled=True).reshape(nd * nc * CHUNK, LANES)
+    far = lax.ppermute(far, axes, pairs_of(nd, nc, True, None))
+    near = lax.ppermute(near, axes, pairs_of(nd, nc, False, None))
+    middle = call(
+        functools.partial(middle_kernel, nd, nc, tiles),
+        [
+            whole(rows + 4, wide, layers),
+            whole(rows - 2, wide, layers),
+            whole(rows - 4, cols, layers),
+        ],
+        [vmem] * (4 + len(kept)),
+        scratch=[pltpu.VMEM((nc, nd, LANES), FLOAT)],
+    )(arrived, fix, early_arrays["pres"], late_arrays["pres"], *kept)
     return call(
         functools.partial(last_kernel, nd, nc, tiles),
         block,
-        [vmem] * (3 + 2 * len(KEPT)),
+        [vmem] * (7 + len(kept)),
         scratch=[
-            pltpu.VMEM((nc, nd, LANES), FLOAT),
-            pltpu.VMEM((rows + 4, wide, layers), FLOAT),
-            pltpu.VMEM((rows + 2, wide, layers), FLOAT),
+            pltpu.VMEM((4, wide, layers), FLOAT),
+            pltpu.VMEM((4, wide, layers), FLOAT),
+            pltpu.VMEM((4, cols, layers), FLOAT),
+            pltpu.SemaphoreType.DMA((3,)),
         ],
-    )(arrived, partner, state, *(early_arrays[n] for n in KEPT), *(late_arrays[n] for n in KEPT))
+        out_space=pltpu.HBM,
+    )(near, far, late_arrays["q"], late_arrays["first"], *middle, *kept)
 
 
 def solution(mesh):

time: 30.9 us -> 28.8 us (0.932)
  blocking collectives: 15.2 us -> 0 us
  starting transfers between devices: 6.43 us -> 15.5 us
  waiting for transfers between devices: 3.76 us -> 7.23 us
  Pallas kernels: 5.26 us -> 5.8 us
    all_to_all x1 -> x0, blocking collectives: 15.2 us -> none  [body(): lax.all_to_all(chunks, axes, 0, 0, tiled=True)]
    all_to_all x0 -> x1, starting transfers between devices: none -> 7.46 us  [body(): lax.all_to_all(chunks, axes, 0, 0, tiled=True)]
    all_to_all x0 -> x1, waiting for transfers between devices: none -> 3.98 us  [body(): lax.all_to_all(chunks, axes, 0, 0, tiled=True)]
    ppermute x1 -> x2, starting transfers between devices: 2.23 us -> 3.86 us  [the longest x1 3.19 us: body(): near = lax.ppermute(near, axes, pairs_of(nd, nc, False, None))]
    pallas_call x1, Pallas kernels: 0.74 us -> 1.38 us  [body(): call(functools.partial(late_kernel, nd, nc, tiles, rows), [whole(*span_sh...]
    ppermute x1 -> x2, waiting for transfers between devices: 0.51 us -> 0.01 us  [the longest x1 0.01 us: body(): near = lax.ppermute(near, axes, pairs_of(nd, nc, False, None))]
    pallas_call x4 -> x3, Pallas kernels: 3.41 us -> 3.3 us  [the longest x1 1.18 us: body(): call(functools.partial(pack_kernel, nd, nc), [block, whole(2, cols, layer...]
  transfers between devices with their start and end apart: 5 -> 7, of which waited for: 4 -> 4; matrix products, arithmetic and copies ran while one was open for 0% -> 0% of each run, Pallas kernels for 5% -> 7%
where the time goes in v4:
time: 28.8 us; the launch traced here: 28.6 us
  starting transfers between devices  15.5 us (54%)
  waiting for transfers between devices  7.23 us (25%)
  Pallas kernels  5.8 us (20%)
    all_to_all x1, starting transfers between devices, body(): lax.all_to_all(chunks, axes, 0, 0, tiled=True)  7.46 us
    all_to_all x1, waiting for transfers between devices, body(): lax.all_to_all(chunks, axes, 0, 0, tiled=True)  3.98 us
    ppermute x1, starting transfers between devices, body(): near = lax.ppermute(near, axes, pairs_of(nd, nc, False, None))  3.19 us
    ppermute x1, starting transfers between devices, body(): lax.ppermute(m, axes, pairs_of(nd, nc, None, cross_kind))  2.92 us
    ppermute x1, waiting for transfers between devices, body(): lax.ppermute(m, axes, pairs_of(nd, nc, None, cross_kind))  2.42 us
    pallas_call x1, Pallas kernels, body(): call(functools.partial(late_kernel, nd, nc, tiles, rows), [whole(*span_sh...  1.38 us
    ppermute x3, starting transfers between devices, body(): received = [lax.ppermute(m, axes, p) for m, p in zip(messages, perms)]  1.26 us
    pallas_call x1, Pallas kernels, body(): call(functools.partial(pack_kernel, nd, nc), [block, whole(2, cols, layer...  1.18 us
  transfers between devices with their start and end apart: 7, of which 4 were waited for; matrix products, arithmetic and copies ran while one was open for 0% of the time, Pallas kernels for 7%

profile of v4, /device:TPU:0, one launch (start us, length us, event | category | flops | bytes accessed | tf_op | source)
XLA Modules:
  0.0 28.6 jit_solution(4941556534468832446)
XLA Ops:
  0.0 1.2 %shard_map.46 = (f32[8,32,256]{2,1,0:T(8,128)S(1)}, f32[2,32,256]{2,1,0:T(8,128)S(1)}, f32[7,32,256]{2,1,0:T(8,128)S(1)}, f32[5,32,256]{2,1,0:T(8,128)S(1)}, f32...) custom-call(f32[8,32,256]{2,1,0:T(8,128)} %rhs.1, f32[8,32,256]{2,1,0:T(8,128)} %kappa_hbm.1, s32[8,32,256]{2,1,0:T(8,128)} %mask_hbm.1), custom_call_target="tpu_custom_call" | custom-call | tf_op jit(solution)/shard_map/pallas_call | solution.py:726
  1.2 0.0 copy-start
  1.2 0.5 %collective-permute-start.2 = (f32[7,32,256]{2,1,0:T(8,128)S(1)}, f32[7,32,256]{2,1,0:T(8,128)S(1)}, u32[]{:S(2)}, u32[]{:S(2)}) collective-permute-start(f32[7,32,256]{2,1,0:T(8,128)S(1)} %get-tuple-element.44), channel_id=1, source_target_pairs={{0,2},{1,3},{2,0},{3,1},{4,6},{5,7},{6,4},{7,5},{8,10},{9,11},{10,... | collective-permute-start | bytes 688136 | tf_op jit(solution)/shard_map/ppermute | solution.py:739
  1.7 0.7 %collective-permute-start = (f32[5,32,256]{2,1,0:T(8,128)S(1)}, f32[5,32,256]{2,1,0:T(8,128)S(1)}, u32[]{:S(2)}, u32[]{:S(2)}) collective-permute-start(f32[5,32,256]{2,1,0:T(8,128)S(1)} %get-tuple-element.41), channel_id=1, source_target_pairs={{0,0},{1,1},{2,4},{3,5},{4,2},{5,3},{6,8},{7,9},{8,6},{9,7},{10,12... | collective-permute-start | bytes 491528 | tf_op jit(solution)/shard_map/ppermute | solution.py:739
  2.4 0.4 %collective-permute-done.2.even = f32[7,32,256]{2,1,0:T(8,128)S(1)} collective-permute-done((f32[7,32,256]{2,1,0:T(8,128)S(1)}, f32[7,32,256]{2,1,0:T(8,128)S(1)}, u32[]{:S(2)}, u32[]{:S(2)}) %collective-permute-start.2) | collective-permute-done | bytes 229408 | tf_op jit(solution)/shard_map/ppermute | solution.py:739
  2.8 2.9 %collective-permute-start.3 = (f32[11,8,256]{2,1,0:T(8,128)S(1)}, f32[11,8,256]{2,1,0:T(8,128)S(1)}, u32[]{:S(2)}, u32[]{:S(2)}) collective-permute-start(f32[11,8,256]{2,1,0:T(8,128)S(1)} %shard_map.47), channel_id=1, source_target_pairs={{0,1},{1,0},{2,3},{3,2},{4,5},{5,4},{6,7},{7,6},{8,9},{9,8},{10,11... | collective-permute-start | bytes 270344 | tf_op jit(solution)/shard_map/ppermute | solution.py:748
  5.8 0.0 copy-start.1
  5.8 0.1 collective-permute-start.1
  5.9 2.4 %collective-permute-done.3.refs_0_ = f32[11,8,256]{2,1,0:T(8,128)S(1)} collective-permute-done((f32[11,8,256]{2,1,0:T(8,128)S(1)}, f32[11,8,256]{2,1,0:T(8,128)S(1)}, u32[]{:S(2)}, u32[]{:S(2)}) %collective-permute-start.3) | collective-permute-done | bytes 90144 | tf_op jit(solution)/shard_map/ppermute | solution.py:748
  8.3 0.0 copy-done
  8.3 0.0 copy-done.1
  8.3 1.1 %shard_map.48 = (f32[12,40,256]{2,1,0:T(8,128)S(1)}, f32[11,40,256]{2,1,0:T(8,128)S(1)}, f32[10,40,256]{2,1,0:T(8,128)S(1)}, f32[10,40,256]{2,1,0:T(8,128)S(1)},...) custom-call(f32[8,32,256]{2,1,0:T(8,128)S(1)} %copy-done, ...), custom_call_target="tpu_custom_call" | custom-call | tf_op jit(solution)/shard_map/pallas_call | solution.py:754
  9.4 0.4 %collective-permute-done.1.refs_0_ = f32[3,8,256]{2,1,0:T(8,128)S(1)} collective-permute-done((f32[3,8,256]{2,1,0:T(8,128)S(1)}, f32[3,8,256]{2,1,0:T(8,128)S(1)}, u32[]{:S(2)}, u32[]{:S(2)}) %collective-permute-start.1) | collective-permute-done | bytes 24608 | tf_op jit(solution)/shard_map/ppermute | solution.py:739
  9.8 0.0 collective-permute-done.odd
  9.8 1.4 %shard_map.49 = (f32[2,40,256]{2,1,0:T(8,128)S(1)}, f32[3,40,256]{2,1,0:T(8,128)S(1)}, f32[2,40,256]{2,1,0:T(8,128)S(1)}, f32[1,40,256]{2,1,0:T(8,128)S(1)}, f32...) custom-call(f32[2,32,256]{2,1,0:T(8,128)S(1)} %get-tuple-element.40., ...), custom_call_target="tpu_custom_call" | custom-call | tf_op jit(solution)/shard_map/pallas_call | solution.py:766
  11.2 7.5 %all-to-all-start = ((f32[32,5,1,128]{3,2,1,0:T(1,128)}), f32[32,5,1,128]{3,2,1,0:T(1,128)S(1)}, u32[]{:S(2)}, u32[]{:S(2)}) async-start(f32[32,5,1,128]{3,2,1,0:T(1,128)} %bitcast), calls=%async_computation | async-start | bytes 163840 | tf_op jit(solution)/shard_map/all_to_all | solution.py:783
  18.6 0.7 %collective-permute-start.5 = (f32[72,256]{1,0:T(8,128)S(1)}, f32[72,256]{1,0:T(8,128)S(1)}, u32[]{:S(2)}, u32[]{:S(2)}) collective-permute-start(f32[72,256]{1,0:T(8,128)S(1)} %get-tuple-element.61), channel_id=1, source_target_pairs={{0,0},{1,1},{2,4},{3,5},{4,2},{5,3},{6,8},{7,9},{8,6},{9,7},{10,12... | collective-permute-start | bytes 221192 | tf_op jit(solution)/shard_map/ppermute | solution.py:784
  19.3 3.2 %collective-permute-start.4 = (f32[8,256]{1,0:T(8,128)S(1)}, f32[8,256]{1,0:T(8,128)S(1)}, u32[]{:S(2)}, u32[]{:S(2)}) collective-permute-start(f32[8,256]{1,0:T(8,128)S(1)} %get-tuple-element.60), channel_id=1, source_target_pairs={{0,2},{1,3},{2,0},{3,1},{4,6},{5,7},{6,4},{7,5},{8,10},{9,11},{10,... | collective-permute-start | bytes 24584 | tf_op jit(solution)/shard_map/ppermute | solution.py:785
  22.5 4.0 %all-to-all-done = f32[32,5,1,128]{3,2,1,0:T(1,128)S(1)} async-done(((f32[32,5,1,128]{3,2,1,0:T(1,128)}), f32[32,5,1,128]{3,2,1,0:T(1,128)S(1)}, u32[]{:S(2)}, u32[]{:S(2)}) %all-to-all-start) | async-done | bytes 81952 | tf_op jit(solution)/shard_map/all_to_all | solution.py:783
  26.5 1.0 %shard_map.50 = (f32[12,40,256]{2,1,0:T(8,128)S(1)}, f32[6,40,256]{2,1,0:T(8,128)S(1)}, f32[4,32,256]{2,1,0:T(8,128)S(1)}) custom-call(f32[160,128]{1,0:T(8,128)S(1)} %bitcast.2, f32[2,2,8,256]{3,2,1,0:T(8,128)S(1)} %get-tuple-element.65.fix, f32[8,40,256]{2,1,0:T(8,128)S(1)} %get-tuple-element.54.refs_9_.pres_early, ...), custom_call_target="tpu_custom_call" | custom-call | tf_op jit(solution)/shard_map/pallas_call | solution.py:786
  27.5 0.0 collective-permute-done.4.near
  27.5 0.0 collective-permute-done.5.far
  27.5 1.1 %shard_map.51 = f32[8,32,256]{2,1,0:T(8,128)} custom-call(f32[8,256]{1,0:T(8,128)S(1)} %collective-permute-done.4.near, f32[72,256]{1,0:T(8,128)S(1)} %collective-permute-done.5.far, f32[3,40,256]{2,1,0:T(8,128)S(1)} %get-tuple-element.62.q_late, f32[3,40,256]{2,1,0:T(8,128)S(1)} %get-tuple-element.63.first_late, ...), custom_call_target="tpu_custom_call" | custom-call | tf_op jit(solution)/shard_map/pallas_call | solution.py:796
  (1 shorter events, 0.0 us)
Async XLA Ops:
  1.2 7.1 %copy-start = (f32[8,32,256]{2,1,0:T(8,128)S(1)}, f32[8,32,256]{2,1,0:T(8,128)}, u32[]{:S(2)}) copy-start(f32[8,32,256]{2,1,0:T(8,128)} %rhs.1) | copy-start | bytes 786436
  1.2 1.6 %collective-permute-start.2 = (f32[7,32,256]{2,1,0:T(8,128)S(1)}, f32[7,32,256]{2,1,0:T(8,128)S(1)}, u32[]{:S(2)}, u32[]{:S(2)}) collective-permute-start(f32[7,32,256]{2,1,0:T(8,128)S(1)} %get-tuple-element.44), channel_id=1, source_target_pairs={{0,2},{1,3},{2,0},{3,1},{4,6},{5,7},{6,4},{7,5},{8,10},{9,11},{10,... | collective-permute-start | bytes 688136 | tf_op jit(solution)/shard_map/ppermute | solution.py:739
  1.7 8.1 %collective-permute-start = (f32[5,32,256]{2,1,0:T(8,128)S(1)}, f32[5,32,256]{2,1,0:T(8,128)S(1)}, u32[]{:S(2)}, u32[]{:S(2)}) collective-permute-start(f32[5,32,256]{2,1,0:T(8,128)S(1)} %get-tuple-element.41), channel_id=1, source_target_pairs={{0,0},{1,1},{2,4},{3,5},{4,2},{5,3},{6,8},{7,9},{8,6},{9,7},{10,12... | collective-permute-start | bytes 491528 | tf_op jit(solution)/shard_map/ppermute | solution.py:739
  2.8 5.4 %collective-permute-start.3 = (f32[11,8,256]{2,1,0:T(8,128)S(1)}, f32[11,8,256]{2,1,0:T(8,128)S(1)}, u32[]{:S(2)}, u32[]{:S(2)}) collective-permute-start(f32[11,8,256]{2,1,0:T(8,128)S(1)} %shard_map.47), channel_id=1, source_target_pairs={{0,1},{1,0},{2,3},{3,2},{4,5},{5,4},{6,7},{7,6},{8,9},{9,8},{10,11... | collective-permute-start | bytes 270344 | tf_op jit(solution)/shard_map/ppermute | solution.py:748
  5.8 2.5 %copy-start.1 = (s32[1,4]{1,0:T(1,128)S(1)}, s32[1,4]{1,0:T(1,128)}, u32[]{:S(2)}) copy-start(s32[1,4]{1,0:T(1,128)} %route.1) | copy-start | bytes 52
  5.8 4.0 %collective-permute-start.1 = (f32[3,8,256]{2,1,0:T(8,128)S(1)}, f32[3,8,256]{2,1,0:T(8,128)S(1)}, u32[]{:S(2)}, u32[]{:S(2)}) collective-permute-start(f32[3,8,256]{2,1,0:T(8,128)S(1)} %get-tuple-element.42), channel_id=1, source_target_pairs={{0,1},{1,0},{2,5},{3,4},{4,3},{5,2},{6,9},{7,8},{8,7},{9,6},{10,13... | collective-permute-start | bytes 73736 | tf_op jit(solution)/shard_map/ppermute | solution.py:739
  11.2 15.3 %all-to-all-start = ((f32[32,5,1,128]{3,2,1,0:T(1,128)}), f32[32,5,1,128]{3,2,1,0:T(1,128)S(1)}, u32[]{:S(2)}, u32[]{:S(2)}) async-start(f32[32,5,1,128]{3,2,1,0:T(1,128)} %bitcast), calls=%async_computation | async-start | bytes 163840 | tf_op jit(solution)/shard_map/all_to_all | solution.py:783
  18.6 8.9 %collective-permute-start.5 = (f32[72,256]{1,0:T(8,128)S(1)}, f32[72,256]{1,0:T(8,128)S(1)}, u32[]{:S(2)}, u32[]{:S(2)}) collective-permute-start(f32[72,256]{1,0:T(8,128)S(1)} %get-tuple-element.61), channel_id=1, source_target_pairs={{0,0},{1,1},{2,4},{3,5},{4,2},{5,3},{6,8},{7,9},{8,6},{9,7},{10,12... | collective-permute-start | bytes 221192 | tf_op jit(solution)/shard_map/ppermute | solution.py:784
  19.3 8.2 %collective-permute-start.4 = (f32[8,256]{1,0:T(8,128)S(1)}, f32[8,256]{1,0:T(8,128)S(1)}, u32[]{:S(2)}, u32[]{:S(2)}) collective-permute-start(f32[8,256]{1,0:T(8,128)S(1)} %get-tuple-element.60), channel_id=1, source_target_pairs={{0,2},{1,3},{2,0},{3,1},{4,6},{5,7},{6,4},{7,5},{8,10},{9,11},{10,... | collective-permute-start | bytes 24584 | tf_op jit(solution)/shard_map/ppermute | solution.py:785

commit v5 on v3

--- a/solution.py
+++ b/solution.py
@@ -13,14 +13,13 @@
 KEEP = 1.0 - OMEGA
 SNOW_FACTOR = 3.0
 
-DEPTH = 4
-CORNER = DEPTH - 1
+DEPTH = 3
+CORNER = DEPTH
 STRIP = 8
 LANES = 128
-HALF = 8
-CHUNK = HALF + 1
+CHUNK = 2
 FLOAT = jnp.float32
-VMEM_BYTES = 48 * 1024 * 1024
+VMEM_BYTES = 24 * 1024 * 1024
 
 
 def partners(count, odd):
@@ -141,8 +140,8 @@
             for cross_kind in pairings(nc):
                 right, _ = facing(cross, nc, cross_kind)
                 strip = edge_strip(right, cols)
-                tiles = [conduct[x, strip, :] for x in near[: DEPTH - 1]]
-                tiles += [rhs[counted(x, rows), strip, :] for x in near[: DEPTH - 2]]
+                tiles = [conduct[x, strip, :] for x in near]
+                tiles += [rhs[counted(x, rows), strip, :] for x in near[:-1]]
                 pack_rows(next(messages), 0, tiles, right)
     for cross_kind in pairings(nc):
         right, _ = facing(cross, nc, cross_kind)
@@ -160,8 +159,7 @@
         strip = edge_strip(right, cols)
         rows = own.shape[0]
         out[:rows] = own[...]
-        tiles = [even[i, strip, :] for i in range(DEPTH - 1)]
-        tiles += [even[DEPTH + i, strip, :] for i in range(DEPTH - 2)]
+        tiles = [even[i, strip, :] for i in range(2 * DEPTH - 1)]
         pack_rows(out, rows, tiles, right)
 
 
@@ -214,16 +212,19 @@
     def row(self, own, halo):
         return jnp.concatenate([own, halo], axis=0)
 
-    def weights(self, q, gain, src, first, diag, wx, wy, wz, x, valid=None):
-        here = q[x]
+    def diagonal(self, low, here, high, valid=None):
         above = jnp.where(self.last_lane, 0.0, roll(here, -1, 1))
         below = jnp.where(self.lane == 0, 0.0, roll(here, 1, 1))
         right = roll(here, -1, 0)
-        doubled = 6.0 * here + (q[x - 1] + q[x + 1]) + (right + roll(here, 1, 0)) + (above + below)
+        doubled = 6.0 * here + (low + high) + (right + roll(here, 1, 0)) + (above + below)
         ok = self.col_ok & (doubled > 0.0)
         if valid is not None:
             ok = ok & valid
-        gain_here = jnp.where(ok, (2.0 * OMEGA) / doubled, 0.0)
+        return doubled, jnp.where(ok, (2.0 * OMEGA) / doubled, 0.0), right, above
+
+    def weights(self, q, gain, src, first, diag, wx, wy, wz, x, valid=None):
+        here = q[x]
+        doubled, gain_here, right, above = self.diagonal(q[x - 1], here, q[x + 1], valid)
         gain[x] = gain_here
         first[x] = gain_here * src[x]
         if diag is not None:
@@ -244,14 +245,14 @@
 
 
 def spans(rows):
-    far = rows + DEPTH
     early = dict(
-        q=(0, far), src=(0, far - 1), gain=(1, far - 1), first=(1, far - 1), diag=(1, rows),
-        wx=(0, far - 2), wy=(0, rows + 2), wz=(0, rows + 2), pres=(2, rows + 2),
+        q=(0, rows + DEPTH), src=(0, rows + DEPTH - 1), gain=(1, rows + DEPTH - 1),
+        first=(1, rows + DEPTH - 1), diag=(1, rows), wx=(0, rows + 1), wy=(0, rows + 1),
+        wz=(0, rows + 1), pres=(2, rows + 1),
     )
     late = dict(
         q=(-DEPTH, 0), src=(1 - DEPTH, 0), gain=(1 - DEPTH, 1), first=(1 - DEPTH, 1), diag=(0, 1),
-        wx=(1 - DEPTH, 0), wy=(-2, 0), wz=(-2, 0), pres=(-2, 2),
+        wx=(1 - DEPTH, 0), wy=(-1, 0), wz=(-1, 0), pres=(-1, 2),
     )
     return early, late
 
@@ -292,12 +293,10 @@
         q[x] = frame.row(conduct[x], frame.merged(strips, 0, x))
         src[x] = frame.row(rhs[counted(x, rows)], frame.merged(strips, 0, rows + x))
     _, valid = facing(lax.axis_index("down"), nd, False)
-    blank = jnp.zeros((STRIP, layers), FLOAT)
     for i in range(DEPTH):
-        corner = frame.merged(strips, rows, i) if i < DEPTH - 1 else blank
-        q[rows + i] = jnp.where(valid, frame.row(even[i], corner), 0.0)
+        q[rows + i] = jnp.where(valid, frame.row(even[i], frame.merged(strips, rows, i)), 0.0)
     for i in range(DEPTH - 1):
-        corner = frame.merged(strips, rows, DEPTH - 1 + i) if i < DEPTH - 2 else blank
+        corner = frame.merged(strips, rows, DEPTH + i)
         src[rows + i] = jnp.where(valid, frame.row(even[DEPTH + i], corner), 0.0)
 
     here = q[0]
@@ -379,9 +378,12 @@
     n_in = n_cross + len(EARLY) + 5
     early_refs = dict(zip(EARLY, refs[n_cross:]))
     res_coarse, res_row, coef, sums, touched = refs[n_in - 5 : n_in]
-    names = LATE_KEPT + ("swapped", "fix", "summary") + LATE_SCRATCH
-    late_refs = dict(zip(names, refs[n_in:]))
-    swapped, fix_out, summary = (late_refs[n] for n in ("swapped", "fix", "summary"))
+    names = LATE_KEPT + ("fix", "near", "far", "chunks_hbm") + LATE_SCRATCH + ("chunks", "sem")
+    n_side = len(pairings(nc))
+    sides = refs[n_in : n_in + n_side]
+    late_refs = dict(zip(names, refs[n_in + n_side :]))
+    fix_out, near_out, far_out = (late_refs[n] for n in ("fix", "near", "far"))
+    chunks_hbm, chunks, sem = (late_refs[n] for n in ("chunks_hbm", "chunks", "sem"))
     wide, layers = early_refs["q"].shape[1:]
     cols = wide - STRIP
     tile_w = cols // tiles
@@ -395,19 +397,17 @@
     _, late = spans(rows)
 
     valid = beside(down, nd, jnp.where(even, -1, 1))
-    blank = jnp.zeros((STRIP, layers), FLOAT)
     for i in range(DEPTH):
-        corner = frame.merged(corners, 0, i) if i < DEPTH - 1 else blank
-        q[-1 - i] = jnp.where(valid, frame.row(odd[i], corner), 0.0)
+        q[-1 - i] = jnp.where(valid, frame.row(odd[i], frame.merged(corners, 0, i)), 0.0)
     for i in range(DEPTH - 1):
-        corner = frame.merged(corners, 0, DEPTH - 1 + i) if i < DEPTH - 2 else blank
+        corner = frame.merged(corners, 0, DEPTH + i)
         src[-1 - i] = jnp.where(valid, frame.row(odd[DEPTH + i], corner), 0.0)
     for x in range(*late["gain"]):
         frame.weights(
             q, gain, src, first,
             diag if x == 0 else None,
             wx if x < 0 else None,
-            wy if -2 <= x < 0 else None,
+            wy if x == -1 else None,
             wz, x, valid if x < 0 else None,
         )
     for x in range(*late["pres"]):
@@ -422,10 +422,10 @@
     link_down = jnp.where(even, link_even, link_odd)
     lines = jnp.concatenate([res_total, 0.25 * link_down, 0.25 * link_cross, 0.25 * outflow])
     lines = jnp.sum(lines, axis=1, keepdims=True)
-    line = iota((1, LANES), 1)
-    summary[...] = jnp.where(
-        line == 0, lines[0:1], jnp.where(line == 1, lines[1:2], jnp.where(line == 2, lines[2:3], lines[3:4]))
-    )
+    line = iota((1, layers), 1)
+    summary = jnp.zeros((1, layers), FLOAT)
+    for i in range(4):
+        summary = jnp.where(line == 2 * i + 1, lines[i : i + 1], summary)
 
     packs = rows // 4
     by_row = [coarse_rows(res[2 * k] + res[2 * k + 1], couples, tile_w) for k in range(2)]
@@ -453,92 +453,42 @@
     for k in range(packs):
         fix_out[k] = fix[k]
 
-    def rim(k, j):
-        part = unpack_pairs(fix[k], 1)[j]
-        sub = iota((tile_w, layers), 0) % couples
-        packed = part[0]
+    parts = [unpack_pairs(fix[k % packs], 1)[k // packs] for k in range(rows // 2)]
+    count = nd * nc
+    for i in range(CHUNK):
+        part = summary[:, i * LANES : (i + 1) * LANES]
+        chunks[pl.ds(i, count, stride=CHUNK), :] = jnp.broadcast_to(part, (count, LANES))
+    cross = lax.axis_index("cross")
+    odd_step = jnp.where(even, -1, 1)
+    edges = {}
+    for dy in (-1, 1):
+        at_couple, at_col = (0, 0) if dy < 0 else (couples - 1, tile_w - 1)
+        edge = jnp.concatenate([p[at_couple][at_col : at_col + 1] for p in parts])
+        edges[dy] = edge = unpack_pairs(edge, 1)[0 if dy < 0 else 1]
+        for k, step in ((0, odd_step), (rows // 2 - 1, -odd_step)):
+
+            @pl.when(beside(cross, nc, dy) & beside(down, nd, step))
+            def _(k=k, step=step, dy=dy, edge=edge):
+                both = jnp.where(line % 2 == 0, edge[k : k + 1], summary)
+                at = ((cross + dy) * nd + down + step) * CHUNK
+                for i in range(CHUNK):
+                    chunks[pl.ds(at + i, 1), :] = both[:, i * LANES : (i + 1) * LANES]
+
+    copy = pltpu.make_async_copy(chunks, chunks_hbm, sem)
+    copy.start()
+
+    sub = iota((tile_w, layers), 0) % couples
+    for out, k, x in ((far_out, 0, 1), (near_out, rows // 2 - 1, rows - 2)):
+        packed = parts[k][0]
         for t in range(1, couples):
-            packed = jnp.where(sub == t, part[t], packed)
-        return packed[:, :LANES], packed[:, LANES:]
-
-    even_rim, odd_rim = rim(packs - 1, 1), rim(0, 0)
-    swapped[:HALF] = even_rim[0]
-    swapped[HALF : 2 * HALF] = even_rim[1]
-    swapped[2 * HALF : 3 * HALF] = odd_rim[1]
-    swapped[3 * HALF :] = odd_rim[0]
-
-
-def spread_kernel(nd, nc, tiles, fix, swapped, summary, pres_early, pres_late, state, chunks):
-    packs, couples, tile_w, layers = fix.shape
-    rows = 4 * packs
-    cols = tiles * tile_w
-    own, halo = slice(0, cols), slice(cols, cols + STRIP)
-    down, cross = lax.axis_index("down"), lax.axis_index("cross")
-    pres = joined(rows, "pres", pres_early, pres_late)
-
-    fine = [None] * (rows // 2)
-    for k in range(packs):
-        for j, part in enumerate(unpack_pairs(fix[k], 1)):
-            both = unpack_pairs(part, 2)
-            fine[k + j * packs] = jnp.stack(both, axis=1).reshape(cols, layers)
-
-    for x in range(-2, rows + 2):
-        value = pres[x]
-        if 0 <= x < rows:
-            state[x + 2, own, :] = value[own] + fine[x // 2]
-            state[x + 2, halo, :] = value[halo]
-        else:
-            state[x + 2] = value
-
-    blank = jnp.zeros((HALF, LANES), FLOAT)
-    sums = summary[...]
-
-    def fill(b, carry):
-        at = b * CHUNK
-        chunks[pl.ds(at, HALF), :] = blank
-        chunks[pl.ds(at + HALF, 1), :] = sums
-        return carry
-
-    lax.fori_loop(0, nd * nc, fill, 0)
-    me = down * nc + cross
-    odd_step = jnp.where(down % 2 == 0, -1, 1)
-
-    @pl.when(beside(down, nd, odd_step))
-    def _():
-        chunks[pl.ds((me + odd_step * nc) * CHUNK, HALF), :] = swapped[3 * HALF :]
-
-    for dy in (-1, 1):
-        column = 0 if dy < 0 else cols - 1
-
-        @pl.when(beside(cross, nc, dy))
-        def _(dy=dy, column=column):
-            lines = []
-            for k in range(rows // 2):
-                f = fine[k][column : column + 1]
-                lines += [f[:, :LANES], f[:, LANES:]]
-            at = (me + dy) * CHUNK
-            for i, f in enumerate(lines):
-                chunks[pl.ds(at + i, 1), :] = f
-            for side in (0, 1):
-                dx = -odd_step if side else odd_step
-
-                @pl.when(beside(down, nd, dx))
-                def _(side=side, dx=dx):
-                    at = (me + dy + dx * nc) * CHUNK
-                    pair = lines[-2:] if side else lines[:2]
-                    chunks[pl.ds(at, 1), :] = pair[0]
-                    chunks[pl.ds(at + 1, 1), :] = pair[1]
-
-
-def relay_kernel(nd, nc, chunks_in, swapped, chunks):
-    chunks[...] = chunks_in[...]
-    down, cross = lax.axis_index("down"), lax.axis_index("cross")
-    step = jnp.where(down % 2 == 0, 2, -2)
-
-    @pl.when(beside(down, nd, step))
-    def _():
-        at = ((down + step) * nc + cross) * CHUNK
-        chunks[pl.ds(at, HALF), :] = swapped[2 * HALF : 3 * HALF]
+            packed = jnp.where(sub == t, parts[k][t], packed)
+        out[cols:] = packed
+        fine = jnp.stack(unpack_pairs(parts[k], 2), axis=1).reshape(cols, layers)
+        out[:cols] = pres[x][frame.own] + fine
+    for cross_kind, out in zip(pairings(nc), sides):
+        right, _ = facing(cross, nc, cross_kind)
+        out[: rows // 2] = jnp.where(right, edges[1], edges[-1])
+    copy.wait()
 
 
 def coarse_solve(totals, outflow, link_down, link_up, link_cross):
@@ -578,21 +528,66 @@
 KEPT = ("src", "gain", "wx", "wy", "wz")
 
 
-def last_kernel(nd, nc, tiles, got, swapped, state, *refs):
+def around(nd, nc, step, dy):
+    row = jnp.clip(lax.axis_index("down") + step, 0, nd - 1)
+    return row, jnp.clip(lax.axis_index("cross") + dy, 0, nc - 1)
+
+
+def fine_row(packed, couples):
+    sub = iota(packed.shape, 0) % couples
+    parts = []
+    for t in range(couples):
+        tall = jnp.where(sub == t, packed, 0.0)
+        for s in range(couples):
+            if s != t:
+                tall = tall + jnp.where(sub == s, roll(packed, s - t, 0), 0.0)
+        parts += unpack_pairs(tall, 1)
+    return jnp.concatenate(parts, axis=0)
+
+
+def base_kernel(nd, nc, tiles, near, fix, pres_early, pres_late, *refs):
+    *sides, base = refs
+    packs, couples, tile_w, layers = fix.shape
+    rows, cols = 4 * packs, tiles * tile_w
+    start = joined(rows, "pres", pres_early, pres_late)
+    down = lax.axis_index("down")
+    own, halo = slice(0, cols), slice(cols, cols + STRIP)
+    frame = Frame(nd, nc, cols, layers)
+    for k in range(packs):
+        for j, part in enumerate(unpack_pairs(fix[k], 1)):
+            both = unpack_pairs(part, 2)
+            fine = jnp.stack(both, axis=1).reshape(cols, layers)
+            row = k + j * packs
+            edge = jnp.zeros((STRIP, layers), FLOAT)
+            for place, side in zip(frame.sides, sides):
+                edge = jnp.where(place, side[row : row + 1], edge)
+            for x in (2 * row, 2 * row + 1):
+                base[x + 2, own, :] = start[x][own] + fine
+                base[x + 2, halo, :] = start[x][halo] + edge
+    there = beside(down, nd, jnp.where(down % 2 == 0, 1, -1))
+    rim = jnp.where(there, fine_row(near[cols:], couples), 0.0)
+    base[rows + 2, own, :] = start[rows][own] + rim
+    base[rows + 2, halo, :] = start[rows][halo]
+    base[rows + 3, own, :] = jnp.where(there, near[:cols], 0.0)
+    base[rows + 3, halo, :] = jnp.zeros((STRIP, layers), FLOAT)
+    base[1] = start[-1]
+    base[0] = jnp.zeros((cols + STRIP, layers), FLOAT)
+
+
+def last_kernel(nd, nc, tiles, got, far, base, *refs):
     early = dict(zip(KEPT, refs))
     late = dict(zip(KEPT, refs[len(KEPT) :]))
-    out, bricks, pres_ref, third_ref = refs[2 * len(KEPT) :]
+    out, pres_ref, third_ref, new, bricks, sems = refs[2 * len(KEPT) :]
     rows, cols, layers = out.shape
     src, gain, wx, wy, wz = (joined(rows, n, early[n], late[n]) for n in KEPT)
-    tile_w = cols // tiles
-    couples = tiles // 2
     down, cross = lax.axis_index("down"), lax.axis_index("cross")
     own, halo = slice(0, cols), slice(cols, cols + STRIP)
-
-    tables = [got[pl.ds(c * CHUNK + HALF, nd, stride=nc * CHUNK), :] for c in range(nc)]
+    even = down % 2 == 0
+
+    tables = [got[pl.ds(c * nd * CHUNK, nd, stride=CHUNK), :] for c in range(nc)]
 
     def spread_lane(table, at):
-        return jnp.broadcast_to(table[:, at : at + 1], (nd, LANES))
+        return jnp.broadcast_to(table[:, 2 * at + 1 : 2 * at + 2], (nd, LANES))
 
     last = iota((nd, LANES), 0) == nd - 1
     totals = [spread_lane(t, 0) for t in tables]
@@ -604,74 +599,72 @@
     for c in range(nc):
         bricks[c] = answer[c]
 
-    def brick(dx, dy):
-        line = bricks[jnp.clip(cross + dy, 0, nc - 1), pl.ds(jnp.clip(down + dx, 0, nd - 1), 1), :]
-        return jnp.concatenate([line] * (layers // LANES), axis=1)
-
-    def lines(dx, dy, count):
-        row, col = jnp.clip(down + dx, 0, nd - 1), jnp.clip(cross + dy, 0, nc - 1)
-        return got[pl.ds((row * nc + col) * CHUNK, count), :]
-
-    def line_pair(block, k):
-        return jnp.concatenate([block[2 * k : 2 * k + 1], block[2 * k + 1 : 2 * k + 2]], axis=1)
-
-    def unpack(packed):
-        sub = iota((tile_w, layers), 0) % couples
-        parts = []
-        for t in range(couples):
-            tall = jnp.where(sub == t, packed, 0.0)
-            for s in range(couples):
-                if s != t:
-                    tall = tall + jnp.where(sub == s, roll(packed, s - t, 0), 0.0)
-            parts += unpack_pairs(tall, 1)
-        return jnp.concatenate(parts, axis=0)
-
-    odd_step = jnp.where(down % 2 == 0, -1, 1)
-    even_rim = jnp.concatenate([swapped[:HALF], swapped[HALF : 2 * HALF]], axis=1)
-    odd_rim = jnp.concatenate([lines(odd_step, 0, HALF), lines(2 * odd_step, 0, HALF)], axis=1)
-    right = iota((STRIP, layers), 0) < STRIP // 2
-    there = (iota((STRIP, layers), 0) < jnp.where(cross < nc - 1, STRIP // 2, 0)) | (
-        iota((STRIP, layers), 0) >= jnp.where(cross > 0, STRIP // 2, STRIP)
+    def brick(step, dy):
+        row, col = around(nd, nc, step, dy)
+        return jnp.concatenate([bricks[col, pl.ds(row, 1), :]] * (layers // LANES), axis=1)
+
+    def corner_of(step, dy):
+        row, col = around(nd, nc, step, dy)
+        at = (col * nd + row) * CHUNK
+        both = jnp.concatenate([got[pl.ds(at + i, 1), :] for i in range(CHUNK)], axis=1)
+        return unpack_pairs(both, 1)[0] + brick(step, dy)
+
+    half = STRIP // 2
+    halo_col = iota((STRIP, layers), 0)
+    right = halo_col < half
+    there = (halo_col < jnp.where(cross < nc - 1, half, 0)) | (
+        halo_col >= jnp.where(cross > 0, half, STRIP)
     )
-
     pres = Rows((pres_ref, -2, rows + 4))
     third = Rows((third_ref, -1, rows + 2))
+    odd_step = jnp.where(even, -1, 1)
     mine = brick(0, 0)
-    side_bricks = brick(0, 1), brick(0, -1)
-    side_lines = lines(0, 1, HALF), lines(0, -1, HALF)
-    for k in range(rows // 2):
-        extra = jnp.where(right, *(line_pair(f, k) + b for f, b in zip(side_lines, side_bricks)))
-        extra = jnp.where(there, extra, 0.0)
-        for x in (2 * k, 2 * k + 1):
-            pres_ref[x + 2, own, :] = state[x + 2, own, :] + mine
-            pres_ref[x + 2, halo, :] = state[x + 2, halo, :] + extra
-    for step, rim, at in ((odd_step, odd_rim, 0), (-odd_step, even_rim, rows + 2)):
+    side = jnp.where(there, jnp.where(right, brick(0, 1), brick(0, -1)), 0.0)
+    valid = beside(down, nd, odd_step)
+    odd_rows = (fine_row(far[cols:], tiles // 2), far[:cols])
+    odd_rows = [jnp.where(valid, f, 0.0) for f in odd_rows]
+    for step, xs in ((-odd_step, (rows, rows + 1)), (odd_step, (-1, -2))):
         valid = beside(down, nd, step)
-        row = jnp.where(valid, unpack(rim) + brick(step, 0), 0.0)
-        corner = jnp.where(
-            right, *(line_pair(lines(step, dy, 2), 0) + brick(step, dy) for dy in (1, -1))
-        )
+        row = jnp.where(valid, brick(step, 0), 0.0)
+        corner = jnp.where(right, corner_of(step, 1), corner_of(step, -1))
         corner = jnp.where(there & valid, corner, 0.0)
-        for i in (at, at + 1):
-            pres_ref[i, own, :] = state[i, own, :] + row
-            pres_ref[i, halo, :] = state[i, halo, :] + corner
-
-    for x in range(-1, rows + 1):
+        for i, x in enumerate(xs):
+            value = base[x + 2, own, :] + row
+            pres_ref[x + 2, own, :] = value + odd_rows[i] if x < 0 else value
+            pres_ref[x + 2, halo, :] = base[x + 2, halo, :] + (0.0 if i else corner)
+    for x in reversed(range(rows)):
+        pres_ref[x + 2, own, :] = base[x + 2, own, :] + mine
+        pres_ref[x + 2, halo, :] = base[x + 2, halo, :] + side
+
+    copies = []
+    for x in reversed(range(-1, rows + 1)):
         third[x] = smooth(pres, gain, src, wx, wy, wz, x)
-    for x in range(rows):
-        out[counted(x, rows)] = smooth(third, gain, src, wx, wy, wz, x)[own]
+        if x + 1 < rows:
+            y = x + 1
+            new[counted(y, rows)] = smooth(third, gain, src, wx, wy, wz, y)[own]
+            if y in (rows // 2, 0):
+                at = jnp.where(even, y, rows // 2 - y)
+                span = pl.ds(at, rows // 2)
+                copies.append(pltpu.make_async_copy(new.at[span], out.at[span], sems.at[len(copies)]))
+                copies[-1].start()
+    for copy in copies:
+        copy.wait()
 
 
 def whole(*shape):
     return jax.ShapeDtypeStruct(shape, FLOAT)
 
 
-def call(kernel, out_shape, spaces, scratch=(), vmem_bytes=VMEM_BYTES):
+def call(kernel, out_shape, spaces, scratch=(), vmem_bytes=VMEM_BYTES, out_spaces=None):
     return pl.pallas_call(
         kernel,
         out_shape=out_shape,
         in_specs=[pl.BlockSpec(memory_space=s) for s in spaces],
-        out_specs=jax.tree.map(lambda _: pl.BlockSpec(memory_space=pltpu.VMEM), out_shape),
+        out_specs=jax.tree.map(
+            lambda _, s: pl.BlockSpec(memory_space=s),
+            out_shape,
+            out_spaces or jax.tree.map(lambda _: pltpu.VMEM, out_shape),
+        ),
         scratch_shapes=list(scratch),
         compiler_params=pltpu.CompilerParams(vmem_limit_bytes=vmem_bytes),
     )
@@ -707,7 +700,7 @@
             pltpu.VMEM((rows, cols, layers), band_mask.dtype),
             pltpu.SemaphoreType.DMA((3,)),
         ],
-        vmem_bytes=53 * 1024 * 1024,
+        vmem_bytes=54400 * 1024,
     )(right_side, kappa, band_mask)
 
     received = [lax.ppermute(m, axes, p) for m, p in zip(messages, perms)]
@@ -737,39 +730,54 @@
         ],
         [vmem] * (4 + len(strips)),
     )(right_side, conduct, tile_route, even, *strips)
-    *late_arrays, swapped, fix, summary = call(
+    late_arrays = call(
         functools.partial(late_kernel, nd, nc, tiles, rows),
-        [whole(*span_shape(late[n], wide, layers)) for n in LATE_KEPT]
-        + [whole(4 * HALF, LANES), whole(packs, *tile_shape), whole(1, LANES)],
+        [whole(STRIP, layers) for _ in pairings(nc)]
+        + [whole(*span_shape(late[n], wide, layers)) for n in LATE_KEPT]
+        + [
+            whole(packs, *tile_shape),
+            whole(cols + tile_w, layers),
+            whole(cols + tile_w, layers),
+            whole(nd * nc * CHUNK, LANES),
+        ],
         [vmem] * (len(odd) + len(first_part)),
-        scratch=[pltpu.VMEM(span_shape(late[n], wide, layers), FLOAT) for n in LATE_SCRATCH],
+        scratch=[pltpu.VMEM(span_shape(late[n], wide, layers), FLOAT) for n in LATE_SCRATCH]
+        + [pltpu.VMEM((nd * nc * CHUNK, LANES), FLOAT), pltpu.SemaphoreType.DMA],
+        out_spaces=[vmem] * (len(pairings(nc)) + len(LATE_KEPT) + 3) + [pltpu.HBM],
     )(*odd, *first_part)
+    n_side = len(pairings(nc))
+    sides, late_arrays = late_arrays[:n_side], late_arrays[n_side:]
+    *late_arrays, fix, near, far, chunks = late_arrays
     early_arrays = dict(zip(EARLY, first_part))
     late_arrays = dict(zip(LATE_KEPT, late_arrays))
-
-    partner = lax.ppermute(swapped, axes, pairs_of(nd, nc, False, None))
-    state, chunks = call(
-        functools.partial(spread_kernel, nd, nc, tiles),
-        [whole(rows + 4, wide, layers), whole(nd * nc * CHUNK, LANES)],
-        [vmem] * 5,
-    )(fix, swapped, summary, early_arrays["pres"], late_arrays["pres"])
-    chunks = call(
-        functools.partial(relay_kernel, nd, nc),
-        whole(nd * nc * CHUNK, LANES),
-        [vmem, vmem],
-    )(chunks, partner)
+    kept = [d[n] for d in (early_arrays, late_arrays) for n in KEPT]
+
     chunks = chunks.reshape(nd * nc, CHUNK, 1, LANES)
-    arrived = lax.all_to_all(chunks, axes, 0, 0, tiled=True).reshape(nd * nc * CHUNK, LANES)
+    arrived = lax.all_to_all(chunks, ("cross", "down"), 0, 0, tiled=True).reshape(nd * nc * CHUNK, LANES)
+    far = lax.ppermute(far, axes, pairs_of(nd, nc, True, None))
+    near = lax.ppermute(near, axes, pairs_of(nd, nc, False, None))
+    sides = [
+        lax.ppermute(m, axes, pairs_of(nd, nc, None, cross_kind))
+        for m, cross_kind in zip(sides, pairings(nc))
+    ]
+    base = call(
+        functools.partial(base_kernel, nd, nc, tiles),
+        whole(rows + 4, wide, layers),
+        [vmem] * (4 + n_side),
+    )(near, fix, early_arrays["pres"], late_arrays["pres"], *sides)
     return call(
         functools.partial(last_kernel, nd, nc, tiles),
         block,
-        [vmem] * (3 + 2 * len(KEPT)),
+        [vmem] * (3 + len(kept)),
         scratch=[
-            pltpu.VMEM((nc, nd, LANES), FLOAT),
             pltpu.VMEM((rows + 4, wide, layers), FLOAT),
             pltpu.VMEM((rows + 2, wide, layers), FLOAT),
+            pltpu.VMEM((rows, cols, layers), FLOAT),
+            pltpu.VMEM((nc, nd, LANES), FLOAT),
+            pltpu.SemaphoreType.DMA((2,)),
         ],
-    )(arrived, partner, state, *(early_arrays[n] for n in KEPT), *(late_arrays[n] for n in KEPT))
+        out_spaces=pltpu.HBM,
+    )(arrived, far, base, *kept)
 
 
 def solution(mesh):

time: 30.9 us -> 27.8 us (0.90)
  blocking collectives: 15.2 us -> 0 us
  starting transfers between devices: 6.43 us -> 14.2 us
  waiting for transfers between devices: 3.76 us -> 7.78 us
    all_to_all x1 -> x0, blocking collectives: 15.2 us -> none  [body(): lax.all_to_all(chunks, axes, 0, 0, tiled=True)]
    all_to_all x0 -> x1, starting transfers between devices: none -> 7.36 us  [body(): lax.all_to_all(chunks, ('cross', 'down'), 0, 0, tiled=True)]
    all_to_all x0 -> x1, waiting for transfers between devices: none -> 2.45 us  [body(): lax.all_to_all(chunks, ('cross', 'down'), 0, 0, tiled=True)]
    ppermute x1 -> x2, waiting for transfers between devices: 2.42 us -> 4.4 us  [body(): lax.ppermute(m, axes, pairs_of(nd, nc, None, cross_kind))]
    ppermute x1 -> x2, starting transfers between devices: 2.92 us -> 4.65 us  [body(): lax.ppermute(m, axes, pairs_of(nd, nc, None, cross_kind))]
    ppermute x1 -> x2, starting transfers between devices: 2.23 us -> 0.97 us  [the longest x1 0.65 us: body(): far = lax.ppermute(far, axes, pairs_of(nd, nc, True, None))]
    ppermute x1 -> x2, waiting for transfers between devices: 0.51 us -> 0.01 us  [the longest x1 0.01 us: body(): far = lax.ppermute(far, axes, pairs_of(nd, nc, True, None))]
    pallas_call x3 -> x2, Pallas kernels: 1.08 us -> 1.49 us  [the longest x1 1.38 us: body(): call(functools.partial(late_kernel, nd, nc, tiles, rows), [whole(STRIP, l...]
  transfers between devices with their start and end apart: 5 -> 8, of which waited for: 4 -> 5; matrix products, arithmetic and copies ran while one was open for 0% -> 0% of each run, Pallas kernels for 5% -> 4%
where the time goes in v5:
time: 27.8 us; the launch traced here: 27.6 us
  starting transfers between devices  14.2 us (51%)
  waiting for transfers between devices  7.78 us (28%)
  Pallas kernels  5.5 us (20%)
    all_to_all x1, starting transfers between devices, body(): lax.all_to_all(chunks, ('cross', 'down'), 0, 0, tiled=True)  7.36 us
    ppermute x2, starting transfers between devices, body(): lax.ppermute(m, axes, pairs_of(nd, nc, None, cross_kind))  4.65 us
    ppermute x2, waiting for transfers between devices, body(): lax.ppermute(m, axes, pairs_of(nd, nc, None, cross_kind))  4.4 us
    all_to_all x1, waiting for transfers between devices, body(): lax.all_to_all(chunks, ('cross', 'down'), 0, 0, tiled=True)  2.45 us
    pallas_call x1, Pallas kernels, body(): call(functools.partial(last_kernel, nd, nc, tiles), block, [vmem] * (3 +...  1.82 us
    pallas_call x1, Pallas kernels, body(): call(functools.partial(late_kernel, nd, nc, tiles, rows), [whole(STRIP, l...  1.38 us
    ppermute x3, starting transfers between devices, body(): received = [lax.ppermute(m, axes, p) for m, p in zip(messages, perms)]  1.26 us
    pallas_call x1, Pallas kernels, body(): call(functools.partial(pack_kernel, nd, nc), [block] + shapes + strips, [...  1.17 us
  transfers between devices with their start and end apart: 8, of which 5 were waited for; matrix products, arithmetic and copies ran while one was open for 0% of the time, Pallas kernels for 4%

profile of v5, /device:TPU:0, one launch (start us, length us, event | category | flops | bytes accessed | tf_op | source)
XLA Modules:
  0.0 27.6 jit_solution(6672305743152122669)
XLA Ops:
  0.0 1.2 %shard_map.46 = (f32[8,32,256]{2,1,0:T(8,128)S(1)}, f32[5,32,256]{2,1,0:T(8,128)S(1)}, f32[5,32,256]{2,1,0:T(8,128)S(1)}, f32[3,8,256]{2,1,0:T(8,128)S(1)}, f32[8,8,256]{2,1,0:T(8,128)S(1)}) custom-call(f32[8,32,256]{2,1,0:T(8,128)} %rhs.1, f32[8,32,256]{2,1,0:T(8,128)} %kappa_hbm.1, s32[8,32,256]{2,1,0:T(8,128)} %mask_hbm.1), custom_call_target="tpu_custom_call" | custom-call | tf_op jit(solution)/shard_map/pallas_call | solution.py:693
  1.2 0.0 copy-start
  1.2 0.5 %collective-permute-start.2 = (f32[5,32,256]{2,1,0:T(8,128)S(1)}, f32[5,32,256]{2,1,0:T(8,128)S(1)}, u32[]{:S(2)}, u32[]{:S(2)}) collective-permute-start(f32[5,32,256]{2,1,0:T(8,128)S(1)} %get-tuple-element.38), channel_id=1, source_target_pairs={{0,2},{1,3},{2,0},{3,1},{4,6},{5,7},{6,4},{7,5},{8,10},{9,11},{10,... | collective-permute-start | bytes 491528 | tf_op jit(solution)/shard_map/ppermute | solution.py:706
  1.7 0.7 %collective-permute-start = (f32[5,32,256]{2,1,0:T(8,128)S(1)}, f32[5,32,256]{2,1,0:T(8,128)S(1)}, u32[]{:S(2)}, u32[]{:S(2)}) collective-permute-start(f32[5,32,256]{2,1,0:T(8,128)S(1)} %get-tuple-element.35), channel_id=1, source_target_pairs={{0,0},{1,1},{2,4},{3,5},{4,2},{5,3},{6,8},{7,9},{8,6},{9,7},{10,12... | collective-permute-start | bytes 491528 | tf_op jit(solution)/shard_map/ppermute | solution.py:706
  2.4 0.4 %collective-permute-done.2.even = f32[5,32,256]{2,1,0:T(8,128)S(1)} collective-permute-done((f32[5,32,256]{2,1,0:T(8,128)S(1)}, f32[5,32,256]{2,1,0:T(8,128)S(1)}, u32[]{:S(2)}, u32[]{:S(2)}) %collective-permute-start.2) | collective-permute-done | bytes 163872 | tf_op jit(solution)/shard_map/ppermute | solution.py:706
  2.8 2.9 %collective-permute-start.3 = (f32[11,8,256]{2,1,0:T(8,128)S(1)}, f32[11,8,256]{2,1,0:T(8,128)S(1)}, u32[]{:S(2)}, u32[]{:S(2)}) collective-permute-start(f32[11,8,256]{2,1,0:T(8,128)S(1)} %shard_map.47), channel_id=1, source_target_pairs={{0,1},{1,0},{2,3},{3,2},{4,5},{5,4},{6,7},{7,6},{8,9},{9,8},{10,11... | collective-permute-start | bytes 270344 | tf_op jit(solution)/shard_map/ppermute | solution.py:715
  5.7 0.0 copy-start.1
  5.7 0.1 collective-permute-start.1
  5.8 2.4 %collective-permute-done.3.refs_0_ = f32[11,8,256]{2,1,0:T(8,128)S(1)} collective-permute-done((f32[11,8,256]{2,1,0:T(8,128)S(1)}, f32[11,8,256]{2,1,0:T(8,128)S(1)}, u32[]{:S(2)}, u32[]{:S(2)}) %collective-permute-start.3) | collective-permute-done | bytes 90144 | tf_op jit(solution)/shard_map/ppermute | solution.py:715
  8.2 0.0 copy-done
  8.2 0.0 copy-done.1
  8.2 1.0 %shard_map.48 = (f32[11,40,256]{2,1,0:T(8,128)S(1)}, f32[10,40,256]{2,1,0:T(8,128)S(1)}, f32[9,40,256]{2,1,0:T(8,128)S(1)}, f32[9,40,256]{2,1,0:T(8,128)S(1)}, f...) custom-call(f32[8,32,256]{2,1,0:T(8,128)S(1)} %copy-done, ...), custom_call_target="tpu_custom_call" | custom-call | tf_op jit(solution)/shard_map/pallas_call | solution.py:721
  9.2 0.6 %collective-permute-done.1.refs_0_ = f32[3,8,256]{2,1,0:T(8,128)S(1)} collective-permute-done((f32[3,8,256]{2,1,0:T(8,128)S(1)}, f32[3,8,256]{2,1,0:T(8,128)S(1)}, u32[]{:S(2)}, u32[]{:S(2)}) %collective-permute-start.1) | collective-permute-done | bytes 24608 | tf_op jit(solution)/shard_map/ppermute | solution.py:706
  9.8 0.0 collective-permute-done.odd
  9.8 1.4 %shard_map.49 = (f32[8,256]{1,0:T(8,128)S(1)}, f32[2,40,256]{2,1,0:T(8,128)S(1)}, f32[3,40,256]{2,1,0:T(8,128)S(1)}, f32[2,40,256]{2,1,0:T(8,128)S(1)}, f32[1,40...) custom-call(f32[5,32,256]{2,1,0:T(8,128)S(1)} %collective-permute-do, ...), custom_call_target="tpu_custom_call" | custom-call | tf_op jit(solution)/shard_map/pallas_call | solution.py:733
  11.1 7.4 %all-to-all-start = ((f32[32,2,1,128]{3,1,2,0:T(2,128)}), f32[32,2,1,128]{3,1,2,0:T(2,128)S(1)}, u32[]{:S(2)}, u32[]{:S(2)}) async-start(f32[32,2,1,128]{3,1,2,0:T(2,128)} %bitcast.1), calls=%async_computation | async-start | bytes 65536 | tf_op jit(solution)/shard_map/all_to_all | solution.py:756
  18.5 0.3 %collective-permute-start.5 = (f32[40,256]{1,0:T(8,128)S(1)}, f32[40,256]{1,0:T(8,128)S(1)}, u32[]{:S(2)}, u32[]{:S(2)}) collective-permute-start(f32[40,256]{1,0:T(8,128)S(1)} %get-tuple-element.56), channel_id=1, source_target_pairs={{0,2},{1,3},{2,0},{3,1},{4,6},{5,7},{6,4},{7,5},{8,10},{9,11},{10,... | collective-permute-start | bytes 122888 | tf_op jit(solution)/shard_map/ppermute | solution.py:758
  18.8 0.7 %collective-permute-start.4 = (f32[40,256]{1,0:T(8,128)S(1)}, f32[40,256]{1,0:T(8,128)S(1)}, u32[]{:S(2)}, u32[]{:S(2)}) collective-permute-start(f32[40,256]{1,0:T(8,128)S(1)} %get-tuple-element.55), channel_id=1, source_target_pairs={{0,0},{1,1},{2,4},{3,5},{4,2},{5,3},{6,8},{7,9},{8,6},{9,7},{10,12... | collective-permute-start | bytes 122888 | tf_op jit(solution)/shard_map/ppermute | solution.py:757
  19.5 1.7 %collective-permute-start.6 = (f32[8,256]{1,0:T(8,128)S(1)}, f32[8,256]{1,0:T(8,128)S(1)}, u32[]{:S(2)}, u32[]{:S(2)}) collective-permute-start(f32[8,256]{1,0:T(8,128)S(1)} %get-tuple-element.59), channel_id=1, source_target_pairs={{0,1},{1,0},{2,3},{3,2},{4,5},{5,4},{6,7},{7,6},{8,9},{9,8},{10,11... | collective-permute-start | bytes 24584 | tf_op jit(solution)/shard_map/ppermute | solution.py:760
  21.2 2.0 %collective-permute-done.6.refs_0_ = f32[8,256]{1,0:T(8,128)S(1)} collective-permute-done((f32[8,256]{1,0:T(8,128)S(1)}, f32[8,256]{1,0:T(8,128)S(1)}, u32[]{:S(2)}, u32[]{:S(2)}) %collective-permute-start.6) | collective-permute-done | bytes 8224 | tf_op jit(solution)/shard_map/ppermute | solution.py:760
  23.2 0.0 collective-permute-done.5.near
  23.2 0.1 shard_map.50.base
  23.3 0.0 collective-permute-done.4.far
  23.3 2.5 %all-to-all-done = f32[32,2,1,128]{3,1,2,0:T(2,128)S(1)} async-done(((f32[32,2,1,128]{3,1,2,0:T(2,128)}), f32[32,2,1,128]{3,1,2,0:T(2,128)S(1)}, u32[]{:S(2)}, u32[]{:S(2)}) %all-to-all-start) | async-done | bytes 32800 | tf_op jit(solution)/shard_map/all_to_all | solution.py:756
  25.8 1.8 %shard_map.51 = f32[8,32,256]{2,1,0:T(8,128)} custom-call(f32[64,128]{1,0:T(8,128)S(1)} %bitcast.4, f32[40,256]{1,0:T(8,128)S(1)} %collective-permute-done.4.far, f32[12,40,256]{2,1,0:T(8,128)S(1)} %shard_map.50.base, f32[10,40,256]{2,1,0:T(8,128)S(1)} %get-tuple-element.41.refs_2_.refs_0_, f32[9,40,256]{2,1,0:T(8,128)S(1)} %get-tuple-element.42.refs_3_.refs_1_, ...), custom_call_target="tpu_custom_call" | custom-call | tf_op jit(solution)/shard_map/pallas_call | solution.py:768
  (1 shorter events, 0.0 us)
Async XLA Ops:
  1.2 7.0 %copy-start = (f32[8,32,256]{2,1,0:T(8,128)S(1)}, f32[8,32,256]{2,1,0:T(8,128)}, u32[]{:S(2)}) copy-start(f32[8,32,256]{2,1,0:T(8,128)} %rhs.1) | copy-start | bytes 786436
  1.2 1.5 %collective-permute-start.2 = (f32[5,32,256]{2,1,0:T(8,128)S(1)}, f32[5,32,256]{2,1,0:T(8,128)S(1)}, u32[]{:S(2)}, u32[]{:S(2)}) collective-permute-start(f32[5,32,256]{2,1,0:T(8,128)S(1)} %get-tuple-element.38), channel_id=1, source_target_pairs={{0,2},{1,3},{2,0},{3,1},{4,6},{5,7},{6,4},{7,5},{8,10},{9,11},{10,... | collective-permute-start | bytes 491528 | tf_op jit(solution)/shard_map/ppermute | solution.py:706
  1.7 8.1 %collective-permute-start = (f32[5,32,256]{2,1,0:T(8,128)S(1)}, f32[5,32,256]{2,1,0:T(8,128)S(1)}, u32[]{:S(2)}, u32[]{:S(2)}) collective-permute-start(f32[5,32,256]{2,1,0:T(8,128)S(1)} %get-tuple-element.35), channel_id=1, source_target_pairs={{0,0},{1,1},{2,4},{3,5},{4,2},{5,3},{6,8},{7,9},{8,6},{9,7},{10,12... | collective-permute-start | bytes 491528 | tf_op jit(solution)/shard_map/ppermute | solution.py:706
  2.8 5.4 %collective-permute-start.3 = (f32[11,8,256]{2,1,0:T(8,128)S(1)}, f32[11,8,256]{2,1,0:T(8,128)S(1)}, u32[]{:S(2)}, u32[]{:S(2)}) collective-permute-start(f32[11,8,256]{2,1,0:T(8,128)S(1)} %shard_map.47), channel_id=1, source_target_pairs={{0,1},{1,0},{2,3},{3,2},{4,5},{5,4},{6,7},{7,6},{8,9},{9,8},{10,11... | collective-permute-start | bytes 270344 | tf_op jit(solution)/shard_map/ppermute | solution.py:715
  5.7 2.5 %copy-start.1 = (s32[1,4]{1,0:T(1,128)S(1)}, s32[1,4]{1,0:T(1,128)}, u32[]{:S(2)}) copy-start(s32[1,4]{1,0:T(1,128)} %route.1) | copy-start | bytes 52
  5.7 4.1 %collective-permute-start.1 = (f32[3,8,256]{2,1,0:T(8,128)S(1)}, f32[3,8,256]{2,1,0:T(8,128)S(1)}, u32[]{:S(2)}, u32[]{:S(2)}) collective-permute-start(f32[3,8,256]{2,1,0:T(8,128)S(1)} %get-tuple-element.36), channel_id=1, source_target_pairs={{0,1},{1,0},{2,5},{3,4},{4,3},{5,2},{6,9},{7,8},{8,7},{9,6},{10,13... | collective-permute-start | bytes 73736 | tf_op jit(solution)/shard_map/ppermute | solution.py:706
  11.1 14.6 %all-to-all-start = ((f32[32,2,1,128]{3,1,2,0:T(2,128)}), f32[32,2,1,128]{3,1,2,0:T(2,128)S(1)}, u32[]{:S(2)}, u32[]{:S(2)}) async-start(f32[32,2,1,128]{3,1,2,0:T(2,128)} %bitcast.1), calls=%async_computation | async-start | bytes 65536 | tf_op jit(solution)/shard_map/all_to_all | solution.py:756
  18.5 4.7 %collective-permute-start.5 = (f32[40,256]{1,0:T(8,128)S(1)}, f32[40,256]{1,0:T(8,128)S(1)}, u32[]{:S(2)}, u32[]{:S(2)}) collective-permute-start(f32[40,256]{1,0:T(8,128)S(1)} %get-tuple-element.56), channel_id=1, source_target_pairs={{0,2},{1,3},{2,0},{3,1},{4,6},{5,7},{6,4},{7,5},{8,10},{9,11},{10,... | collective-permute-start | bytes 122888 | tf_op jit(solution)/shard_map/ppermute | solution.py:758
  18.8 4.5 %collective-permute-start.4 = (f32[40,256]{1,0:T(8,128)S(1)}, f32[40,256]{1,0:T(8,128)S(1)}, u32[]{:S(2)}, u32[]{:S(2)}) collective-permute-start(f32[40,256]{1,0:T(8,128)S(1)} %get-tuple-element.55), channel_id=1, source_target_pairs={{0,0},{1,1},{2,4},{3,5},{4,2},{5,3},{6,8},{7,9},{8,6},{9,7},{10,12... | collective-permute-start | bytes 122888 | tf_op jit(solution)/shard_map/ppermute | solution.py:757
  19.5 3.7 %collective-permute-start.6 = (f32[8,256]{1,0:T(8,128)S(1)}, f32[8,256]{1,0:T(8,128)S(1)}, u32[]{:S(2)}, u32[]{:S(2)}) collective-permute-start(f32[8,256]{1,0:T(8,128)S(1)} %get-tuple-element.59), channel_id=1, source_target_pairs={{0,1},{1,0},{2,3},{3,2},{4,5},{5,4},{6,7},{7,6},{8,9},{9,8},{10,11... | collective-permute-start | bytes 24584 | tf_op jit(solution)/shard_map/ppermute | solution.py:760

commit v6 on v5

--- a/solution.py
+++ b/solution.py
@@ -545,14 +545,33 @@
     return jnp.concatenate(parts, axis=0)
 
 
-def base_kernel(nd, nc, tiles, near, fix, pres_early, pres_late, *refs):
-    *sides, base = refs
+def strip_mask(nc, layers):
+    cross, half = lax.axis_index("cross"), STRIP // 2
+    col = iota((STRIP, layers), 0)
+    there = (col < jnp.where(cross < nc - 1, half, 0)) | (col >= jnp.where(cross > 0, half, STRIP))
+    return there, col < half
+
+
+def sides_of(nd):
+    down = lax.axis_index("down")
+    step = jnp.where(down % 2 == 0, -1, 1)
+    return step, beside(down, nd, step), beside(down, nd, -step)
+
+
+def base_kernel(nd, nc, tiles, near, far, fix, pres_early, pres_late, *refs):
+    n_side = len(pairings(nc))
+    sides = refs[:n_side]
+    early = dict(zip(KEPT, refs[n_side:]))
+    late = dict(zip(KEPT, refs[n_side + len(KEPT) :]))
+    out, pres_ref, third_ref = refs[n_side + 2 * len(KEPT) :]
     packs, couples, tile_w, layers = fix.shape
     rows, cols = 4 * packs, tiles * tile_w
+    src, gain, wx, wy, wz = (joined(rows, n, early[n], late[n]) for n in KEPT)
     start = joined(rows, "pres", pres_early, pres_late)
-    down = lax.axis_index("down")
     own, halo = slice(0, cols), slice(cols, cols + STRIP)
     frame = Frame(nd, nc, cols, layers)
+    pres = Rows((pres_ref, -2, rows + 4))
+    third = Rows((third_ref, -1, rows + 2))
     for k in range(packs):
         for j, part in enumerate(unpack_pairs(fix[k], 1)):
             both = unpack_pairs(part, 2)
@@ -562,26 +581,83 @@
             for place, side in zip(frame.sides, sides):
                 edge = jnp.where(place, side[row : row + 1], edge)
             for x in (2 * row, 2 * row + 1):
-                base[x + 2, own, :] = start[x][own] + fine
-                base[x + 2, halo, :] = start[x][halo] + edge
-    there = beside(down, nd, jnp.where(down % 2 == 0, 1, -1))
-    rim = jnp.where(there, fine_row(near[cols:], couples), 0.0)
-    base[rows + 2, own, :] = start[rows][own] + rim
-    base[rows + 2, halo, :] = start[rows][halo]
-    base[rows + 3, own, :] = jnp.where(there, near[:cols], 0.0)
-    base[rows + 3, halo, :] = jnp.zeros((STRIP, layers), FLOAT)
-    base[1] = start[-1]
-    base[0] = jnp.zeros((cols + STRIP, layers), FLOAT)
-
-
-def last_kernel(nd, nc, tiles, got, far, base, *refs):
+                pres_ref[x + 2, own, :] = start[x][own] + fine
+                pres_ref[x + 2, halo, :] = start[x][halo] + edge
+    _, odd_there, even_there = sides_of(nd)
+    for message, there, xs in ((near, even_there, (rows, rows + 1)), (far, odd_there, (-1, -2))):
+        rim = jnp.where(there, fine_row(message[cols:], couples), 0.0)
+        pres_ref[xs[0] + 2, own, :] = start[xs[0]][own] + rim
+        pres_ref[xs[0] + 2, halo, :] = start[xs[0]][halo]
+        pres_ref[xs[1] + 2, own, :] = jnp.where(there, message[:cols], 0.0)
+        pres_ref[xs[1] + 2, halo, :] = jnp.zeros((STRIP, layers), FLOAT)
+    for x in range(-1, rows + 1):
+        third[x] = smooth(pres, gain, src, wx, wy, wz, x)
+    for x in range(rows):
+        out[x] = smooth(third, gain, src, wx, wy, wz, x)[own]
+
+
+def plain_sweep(field, gain, wx, wy, wz, x):
+    total = 0.0
+    if x in field:
+        value = field[x]
+        total = wy[x] * roll(value, -1, 0) + roll(wy[x] * value, 1, 0)
+        total = total + wz[x] * roll(value, -1, 1) + roll(wz[x] * value, 1, 1)
+    if x + 1 in field:
+        total = total + wx[x] * field[x + 1]
+    if x - 1 in field:
+        total = total + wx[x - 1] * field[x - 1]
+    total = gain[x] * total
+    return KEEP * field[x] + total if x in field else total
+
+
+def response_kernel(nd, nc, rows, *refs):
     early = dict(zip(KEPT, refs))
     late = dict(zip(KEPT, refs[len(KEPT) :]))
-    out, pres_ref, third_ref, new, bricks, sems = refs[2 * len(KEPT) :]
+    every, by_odd, by_even, by_side, by_corner = refs[2 * len(KEPT) :]
+    _, gain, wx, wy, wz = (joined(rows, n, early[n], late[n]) for n in KEPT)
+    cols, layers = every.shape[1:]
+    _, odd_there, even_there = sides_of(nd)
+    there, _ = strip_mask(nc, layers)
+    strip = jnp.where(there, 1.0, 0.0)
+    blank = jnp.zeros((cols, layers), FLOAT)
+    ones = jnp.ones((cols, layers), FLOAT)
+    row_all = jnp.concatenate([ones, strip])
+    row_own = jnp.concatenate([ones, jnp.zeros((STRIP, layers), FLOAT)])
+    row_strip = jnp.concatenate([blank, strip])
+
+    def sweeps(field, first, second):
+        once = {x: plain_sweep(field, gain, wx, wy, wz, x) for x in first}
+        return [plain_sweep(once, gain, wx, wy, wz, x)[:cols] for x in second]
+
+    def ends(value):
+        return value[:STRIP], value[cols - STRIP :]
+
+    def put(ref, x, value):
+        ref[x, :STRIP, :], ref[x, STRIP:, :] = ends(value)
+
+    odd_row, even_row = (jnp.where(t, row_own, 0.0) for t in (odd_there, even_there))
+    field = {x: row_all for x in range(rows)}
+    field |= {-2: odd_row, rows + 1: even_row}
+    field |= {-1: jnp.where(odd_there, row_all, 0.0), rows: jnp.where(even_there, row_all, 0.0)}
+    for x, value in enumerate(sweeps(field, range(-1, rows + 1), range(rows))):
+        every[x] = value
+    for x, value in enumerate(sweeps({-2: odd_row, -1: odd_row}, (-1, 0), (0, 1))):
+        by_odd[x] = value
+    field = {rows: even_row, rows + 1: even_row}
+    for x, value in enumerate(sweeps(field, (rows - 1, rows), (rows - 2, rows - 1))):
+        by_even[x] = value
+    field = {x: row_strip for x in range(rows)}
+    for x, value in enumerate(sweeps(field, range(-1, rows + 1), range(rows))):
+        put(by_side, x, value)
+    for i, (at, x, t) in enumerate(((-1, 0, odd_there), (rows, rows - 1, even_there))):
+        field = {at: jnp.where(t, row_strip, 0.0)}
+        put(by_corner, i, sweeps(field, (at, x), (x,))[0])
+
+
+def last_kernel(nd, nc, got, base, every, by_odd, by_even, by_side, by_corner, *refs):
+    out, new, bricks, sems = refs
     rows, cols, layers = out.shape
-    src, gain, wx, wy, wz = (joined(rows, n, early[n], late[n]) for n in KEPT)
     down, cross = lax.axis_index("down"), lax.axis_index("cross")
-    own, halo = slice(0, cols), slice(cols, cols + STRIP)
     even = down % 2 == 0
 
     tables = [got[pl.ds(c * nd * CHUNK, nd, stride=CHUNK), :] for c in range(nc)]
@@ -603,50 +679,39 @@
         row, col = around(nd, nc, step, dy)
         return jnp.concatenate([bricks[col, pl.ds(row, 1), :]] * (layers // LANES), axis=1)
 
-    def corner_of(step, dy):
+    def corner(step, dy):
         row, col = around(nd, nc, step, dy)
         at = (col * nd + row) * CHUNK
         both = jnp.concatenate([got[pl.ds(at + i, 1), :] for i in range(CHUNK)], axis=1)
-        return unpack_pairs(both, 1)[0] + brick(step, dy)
-
-    half = STRIP // 2
-    halo_col = iota((STRIP, layers), 0)
-    right = halo_col < half
-    there = (halo_col < jnp.where(cross < nc - 1, half, 0)) | (
-        halo_col >= jnp.where(cross > 0, half, STRIP)
-    )
-    pres = Rows((pres_ref, -2, rows + 4))
-    third = Rows((third_ref, -1, rows + 2))
-    odd_step = jnp.where(even, -1, 1)
+        return unpack_pairs(both, 1)[0] + brick(step, dy) - mine
+
+    odd_step, _, _ = sides_of(nd)
     mine = brick(0, 0)
-    side = jnp.where(there, jnp.where(right, brick(0, 1), brick(0, -1)), 0.0)
-    valid = beside(down, nd, odd_step)
-    odd_rows = (fine_row(far[cols:], tiles // 2), far[:cols])
-    odd_rows = [jnp.where(valid, f, 0.0) for f in odd_rows]
-    for step, xs in ((-odd_step, (rows, rows + 1)), (odd_step, (-1, -2))):
-        valid = beside(down, nd, step)
-        row = jnp.where(valid, brick(step, 0), 0.0)
-        corner = jnp.where(right, corner_of(step, 1), corner_of(step, -1))
-        corner = jnp.where(there & valid, corner, 0.0)
-        for i, x in enumerate(xs):
-            value = base[x + 2, own, :] + row
-            pres_ref[x + 2, own, :] = value + odd_rows[i] if x < 0 else value
-            pres_ref[x + 2, halo, :] = base[x + 2, halo, :] + (0.0 if i else corner)
+    more_odd, more_even = brick(odd_step, 0) - mine, brick(-odd_step, 0) - mine
+    more_side = brick(0, -1) - mine, brick(0, 1) - mine
+    more_corner = [[corner(step, dy) for dy in (-1, 1)] for step in (odd_step, -odd_step)]
+    halves = slice(0, STRIP), slice(STRIP, 2 * STRIP)
+    ends = slice(0, STRIP), slice(cols - STRIP, cols)
+    copies = []
     for x in reversed(range(rows)):
-        pres_ref[x + 2, own, :] = base[x + 2, own, :] + mine
-        pres_ref[x + 2, halo, :] = base[x + 2, halo, :] + side
-
-    copies = []
-    for x in reversed(range(-1, rows + 1)):
-        third[x] = smooth(pres, gain, src, wx, wy, wz, x)
-        if x + 1 < rows:
-            y = x + 1
-            new[counted(y, rows)] = smooth(third, gain, src, wx, wy, wz, y)[own]
-            if y in (rows // 2, 0):
-                at = jnp.where(even, y, rows // 2 - y)
-                span = pl.ds(at, rows // 2)
-                copies.append(pltpu.make_async_copy(new.at[span], out.at[span], sems.at[len(copies)]))
-                copies[-1].start()
+        at = counted(x, rows)
+        value = base[x] + mine * every[x]
+        if x < 2:
+            value = value + more_odd * by_odd[x]
+        if x >= rows - 2:
+            value = value + more_even * by_even[x - (rows - 2)]
+        new[at] = value
+        for end, half, side, odd_corner, even_corner in zip(ends, halves, more_side, *more_corner):
+            part = value[end] + side * by_side[x, half, :]
+            if x == 0:
+                part = part + odd_corner * by_corner[0, half, :]
+            if x == rows - 1:
+                part = part + even_corner * by_corner[1, half, :]
+            new[at, end, :] = part
+        if x % 2 == 0:
+            span = pl.ds(jnp.where(even, x, rows - 2 - x), 2)
+            copies.append(pltpu.make_async_copy(new.at[span], out.at[span], sems.at[len(copies)]))
+            copies[-1].start()
     for copy in copies:
         copy.wait()
 
@@ -762,22 +827,35 @@
     ]
     base = call(
         functools.partial(base_kernel, nd, nc, tiles),
-        whole(rows + 4, wide, layers),
-        [vmem] * (4 + n_side),
-    )(near, fix, early_arrays["pres"], late_arrays["pres"], *sides)
-    return call(
-        functools.partial(last_kernel, nd, nc, tiles),
         block,
-        [vmem] * (3 + len(kept)),
+        [vmem] * (5 + n_side + len(kept)),
         scratch=[
             pltpu.VMEM((rows + 4, wide, layers), FLOAT),
             pltpu.VMEM((rows + 2, wide, layers), FLOAT),
+        ],
+    )(near, far, fix, early_arrays["pres"], late_arrays["pres"], *sides, *kept)
+    responses = call(
+        functools.partial(response_kernel, nd, nc, rows),
+        [
+            block,
+            whole(2, cols, layers),
+            whole(2, cols, layers),
+            whole(rows, 2 * STRIP, layers),
+            whole(2, 2 * STRIP, layers),
+        ],
+        [vmem] * len(kept),
+    )(*kept)
+    return call(
+        functools.partial(last_kernel, nd, nc),
+        block,
+        [vmem] * (2 + len(responses)),
+        scratch=[
             pltpu.VMEM((rows, cols, layers), FLOAT),
             pltpu.VMEM((nc, nd, LANES), FLOAT),
-            pltpu.SemaphoreType.DMA((2,)),
+            pltpu.SemaphoreType.DMA((rows // 2,)),
         ],
         out_spaces=pltpu.HBM,
-    )(arrived, far, base, *kept)
+    )(arrived, base, *responses)
 
 
 def solution(mesh):

time: 27.8 us -> 27.3 us (0.982)
  waiting for transfers between devices: 7.78 us -> 6.29 us
  Pallas kernels: 5.5 us -> 6.48 us
    pallas_call x2 -> x3, Pallas kernels: 1.94 us -> 2.92 us  [the longest x1 1.31 us: body(): call(functools.partial(last_kernel, nd, nc), block, [vmem] * (2 + len(res...]
    ppermute x2, waiting for transfers between devices: 4.4 us -> 3.46 us  [body(): lax.ppermute(m, axes, pairs_of(nd, nc, None, cross_kind))]
    all_to_all x1, waiting for transfers between devices: 2.45 us -> 1.9 us  [body(): lax.all_to_all(chunks, ('cross', 'down'), 0, 0, tiled=True)]
  transfers between devices with their start and end apart: 8 -> 8, of which waited for: 5 -> 5; matrix products, arithmetic and copies ran while one was open for 0% -> 0% of each run, Pallas kernels for 4% -> 10%
where the time goes in v6:
time: 27.3 us; the launch traced here: 27.1 us
  starting transfers between devices  14.2 us (52%)
  Pallas kernels  6.48 us (24%)
  waiting for transfers between devices  6.29 us (23%)
    all_to_all x1, starting transfers between devices, body(): lax.all_to_all(chunks, ('cross', 'down'), 0, 0, tiled=True)  7.36 us
    ppermute x2, starting transfers between devices, body(): lax.ppermute(m, axes, pairs_of(nd, nc, None, cross_kind))  4.65 us
    ppermute x2, waiting for transfers between devices, body(): lax.ppermute(m, axes, pairs_of(nd, nc, None, cross_kind))  3.46 us
    all_to_all x1, waiting for transfers between devices, body(): lax.all_to_all(chunks, ('cross', 'down'), 0, 0, tiled=True)  1.9 us
    pallas_call x1, Pallas kernels, body(): call(functools.partial(late_kernel, nd, nc, tiles, rows), [whole(STRIP, l...  1.37 us
    pallas_call x1, Pallas kernels, body(): call(functools.partial(last_kernel, nd, nc), block, [vmem] * (2 + len(res...  1.31 us
    ppermute x3, starting transfers between devices, body(): received = [lax.ppermute(m, axes, p) for m, p in zip(messages, perms)]  1.26 us
    pallas_call x1, Pallas kernels, body(): call(functools.partial(pack_kernel, nd, nc), [block] + shapes + strips, [...  1.17 us
  transfers between devices with their start and end apart: 8, of which 5 were waited for; matrix products, arithmetic and copies ran while one was open for 0% of the time, Pallas kernels for 10%

profile of v6, /device:TPU:0, one launch (start us, length us, event | category | flops | bytes accessed | tf_op | source)
XLA Modules:
  0.0 27.1 jit_solution(15178268910870612469)
XLA Ops:
  0.0 1.2 %shard_map.46 = (f32[8,32,256]{2,1,0:T(8,128)S(1)}, f32[5,32,256]{2,1,0:T(8,128)S(1)}, f32[5,32,256]{2,1,0:T(8,128)S(1)}, f32[3,8,256]{2,1,0:T(8,128)S(1)}, f32[8,8,256]{2,1,0:T(8,128)S(1)}) custom-call(f32[8,32,256]{2,1,0:T(8,128)} %rhs.1, f32[8,32,256]{2,1,0:T(8,128)} %kappa_hbm.1, s32[8,32,256]{2,1,0:T(8,128)} %mask_hbm.1), custom_call_target="tpu_custom_call" | custom-call | tf_op jit(solution)/shard_map/pallas_call | solution.py:758
  1.2 0.0 copy-start
  1.2 0.5 %collective-permute-start.2 = (f32[5,32,256]{2,1,0:T(8,128)S(1)}, f32[5,32,256]{2,1,0:T(8,128)S(1)}, u32[]{:S(2)}, u32[]{:S(2)}) collective-permute-start(f32[5,32,256]{2,1,0:T(8,128)S(1)} %get-tuple-element.43), channel_id=1, source_target_pairs={{0,2},{1,3},{2,0},{3,1},{4,6},{5,7},{6,4},{7,5},{8,10},{9,11},{10,... | collective-permute-start | bytes 491528 | tf_op jit(solution)/shard_map/ppermute | solution.py:771
  1.7 0.7 %collective-permute-start = (f32[5,32,256]{2,1,0:T(8,128)S(1)}, f32[5,32,256]{2,1,0:T(8,128)S(1)}, u32[]{:S(2)}, u32[]{:S(2)}) collective-permute-start(f32[5,32,256]{2,1,0:T(8,128)S(1)} %get-tuple-element.40), channel_id=1, source_target_pairs={{0,0},{1,1},{2,4},{3,5},{4,2},{5,3},{6,8},{7,9},{8,6},{9,7},{10,12... | collective-permute-start | bytes 491528 | tf_op jit(solution)/shard_map/ppermute | solution.py:771
  2.4 0.4 %collective-permute-done.2.even = f32[5,32,256]{2,1,0:T(8,128)S(1)} collective-permute-done((f32[5,32,256]{2,1,0:T(8,128)S(1)}, f32[5,32,256]{2,1,0:T(8,128)S(1)}, u32[]{:S(2)}, u32[]{:S(2)}) %collective-permute-start.2) | collective-permute-done | bytes 163872 | tf_op jit(solution)/shard_map/ppermute | solution.py:771
  2.8 2.9 %collective-permute-start.3 = (f32[11,8,256]{2,1,0:T(8,128)S(1)}, f32[11,8,256]{2,1,0:T(8,128)S(1)}, u32[]{:S(2)}, u32[]{:S(2)}) collective-permute-start(f32[11,8,256]{2,1,0:T(8,128)S(1)} %shard_map.47), channel_id=1, source_target_pairs={{0,1},{1,0},{2,3},{3,2},{4,5},{5,4},{6,7},{7,6},{8,9},{9,8},{10,11... | collective-permute-start | bytes 270344 | tf_op jit(solution)/shard_map/ppermute | solution.py:780
  5.7 0.0 copy-start.1
  5.7 0.1 collective-permute-start.1
  5.8 2.4 %collective-permute-done.3.refs_0_ = f32[11,8,256]{2,1,0:T(8,128)S(1)} collective-permute-done((f32[11,8,256]{2,1,0:T(8,128)S(1)}, f32[11,8,256]{2,1,0:T(8,128)S(1)}, u32[]{:S(2)}, u32[]{:S(2)}) %collective-permute-start.3) | collective-permute-done | bytes 90144 | tf_op jit(solution)/shard_map/ppermute | solution.py:780
  8.2 0.0 copy-done
  8.2 0.0 copy-done.1
  8.2 1.0 %shard_map.48 = (f32[11,40,256]{2,1,0:T(8,128)S(1)}, f32[10,40,256]{2,1,0:T(8,128)S(1)}, f32[9,40,256]{2,1,0:T(8,128)S(1)}, f32[9,40,256]{2,1,0:T(8,128)S(1)}, f...) custom-call(f32[8,32,256]{2,1,0:T(8,128)S(1)} %copy-done, ...), custom_call_target="tpu_custom_call" | custom-call | tf_op jit(solution)/shard_map/pallas_call | solution.py:786
  9.2 0.6 %collective-permute-done.1.refs_0_ = f32[3,8,256]{2,1,0:T(8,128)S(1)} collective-permute-done((f32[3,8,256]{2,1,0:T(8,128)S(1)}, f32[3,8,256]{2,1,0:T(8,128)S(1)}, u32[]{:S(2)}, u32[]{:S(2)}) %collective-permute-start.1) | collective-permute-done | bytes 24608 | tf_op jit(solution)/shard_map/ppermute | solution.py:771
  9.8 0.0 collective-permute-done.odd
  9.8 1.4 %shard_map.49 = (f32[8,256]{1,0:T(8,128)S(1)}, f32[2,40,256]{2,1,0:T(8,128)S(1)}, f32[3,40,256]{2,1,0:T(8,128)S(1)}, f32[2,40,256]{2,1,0:T(8,128)S(1)}, f32[1,40...) custom-call(f32[5,32,256]{2,1,0:T(8,128)S(1)} %collective-permute-do, ...), custom_call_target="tpu_custom_call" | custom-call | tf_op jit(solution)/shard_map/pallas_call | solution.py:798
  11.1 7.4 %all-to-all-start = ((f32[32,2,1,128]{3,1,2,0:T(2,128)}), f32[32,2,1,128]{3,1,2,0:T(2,128)S(1)}, u32[]{:S(2)}, u32[]{:S(2)}) async-start(f32[32,2,1,128]{3,1,2,0:T(2,128)} %bitcast.1), calls=%async_computation | async-start | bytes 65536 | tf_op jit(solution)/shard_map/all_to_all | solution.py:821
  18.5 0.3 %collective-permute-start.4 = (f32[40,256]{1,0:T(8,128)S(1)}, f32[40,256]{1,0:T(8,128)S(1)}, u32[]{:S(2)}, u32[]{:S(2)}) collective-permute-start(f32[40,256]{1,0:T(8,128)S(1)} %get-tuple-element.60), channel_id=1, source_target_pairs={{0,2},{1,3},{2,0},{3,1},{4,6},{5,7},{6,4},{7,5},{8,10},{9,11},{10,... | collective-permute-start | bytes 122888 | tf_op jit(solution)/shard_map/ppermute | solution.py:823
  18.8 0.7 %collective-permute-start.5 = (f32[40,256]{1,0:T(8,128)S(1)}, f32[40,256]{1,0:T(8,128)S(1)}, u32[]{:S(2)}, u32[]{:S(2)}) collective-permute-start(f32[40,256]{1,0:T(8,128)S(1)} %get-tuple-element.61), channel_id=1, source_target_pairs={{0,0},{1,1},{2,4},{3,5},{4,2},{5,3},{6,8},{7,9},{8,6},{9,7},{10,12... | collective-permute-start | bytes 122888 | tf_op jit(solution)/shard_map/ppermute | solution.py:822
  19.5 1.7 %collective-permute-start.6 = (f32[8,256]{1,0:T(8,128)S(1)}, f32[8,256]{1,0:T(8,128)S(1)}, u32[]{:S(2)}, u32[]{:S(2)}) collective-permute-start(f32[8,256]{1,0:T(8,128)S(1)} %get-tuple-element.64), channel_id=1, source_target_pairs={{0,1},{1,0},{2,3},{3,2},{4,5},{5,4},{6,7},{7,6},{8,9},{9,8},{10,11... | collective-permute-start | bytes 24584 | tf_op jit(solution)/shard_map/ppermute | solution.py:825
  21.2 0.9 %shard_map.51 = (f32[8,32,256]{2,1,0:T(8,128)S(1)}, f32[2,32,256]{2,1,0:T(8,128)S(1)}, f32[2,32,256]{2,1,0:T(8,128)S(1)}, f32[8,16,256]{2,1,0:T(8,128)S(1)}, f32[2,16,256]{2,1,0:T(8,128)S(1)}) custom-call(f32[10,40,256]{2,1,0:T(8,128)S(1)} %get-tuple-element.46.refs_2_.refs_1_.refs_0_, f32[9,40,256]{2,1,0:T(8,128)S(1)} %get-tuple-element.47.refs_3_.refs_2_.refs_1_, ...), custom_call_target="tpu_custom_call" | custom-call | tf_op jit(solution)/shard_map/pallas_call | solution.py:837
  22.2 1.0 %collective-permute-done.6.refs_0_ = f32[8,256]{1,0:T(8,128)S(1)} collective-permute-done((f32[8,256]{1,0:T(8,128)S(1)}, f32[8,256]{1,0:T(8,128)S(1)}, u32[]{:S(2)}, u32[]{:S(2)}) %collective-permute-start.6) | collective-permute-done | bytes 8224 | tf_op jit(solution)/shard_map/ppermute | solution.py:825
  23.2 0.0 collective-permute-done.4.near
  23.2 0.0 collective-permute-done.5.far
  23.2 0.7 %shard_map.50.base = f32[8,32,256]{2,1,0:T(8,128)S(1)} custom-call(f32[40,256]{1,0:T(8,128)S(1)} %collective-permute-done.4.near, f32[40,256]{1,0:T(8,128)S(1)} %collective-permute-done.5.far, f32[2,2,8,256]{3,2,1,0:T(8,128)S(1)} %get-tuple-element.62.fix, f32[7,40,256]{2,1,0:T(8,128)S(1)} %get-tuple-element.53.refs_9_.pres_early, ...), custom_call_target="tpu_custom_call" | custom-call | tf_op jit(solution)/shard_map/pallas_call | solution.py:828
  23.9 1.9 %all-to-all-done = f32[32,2,1,128]{3,1,2,0:T(2,128)S(1)} async-done(((f32[32,2,1,128]{3,1,2,0:T(2,128)}), f32[32,2,1,128]{3,1,2,0:T(2,128)S(1)}, u32[]{:S(2)}, u32[]{:S(2)}) %all-to-all-start) | async-done | bytes 32800 | tf_op jit(solution)/shard_map/all_to_all | solution.py:821
  25.8 1.3 %shard_map.52 = f32[8,32,256]{2,1,0:T(8,128)} custom-call(f32[64,128]{1,0:T(8,128)S(1)} %bitcast.4, f32[8,32,256]{2,1,0:T(8,128)S(1)} %shard_map.50.base, f32[8,32,256]{2,1,0:T(8,128)S(1)} %get-tuple-element.70.every, f32[2,32,256]{2,1,0:T(8,128)S(1)} %get-tuple-element.71.by_odd, f32[2,32,256]{2,1,0:T(8,128)S(1)} %get-tuple-element.72.by_even, ...), custom_call_target="tpu_custom_call" | custom-call | tf_op jit(solution)/shard_map/pallas_call | solution.py:848
  (1 shorter events, 0.0 us)
Async XLA Ops:
  1.2 7.0 %copy-start = (f32[8,32,256]{2,1,0:T(8,128)S(1)}, f32[8,32,256]{2,1,0:T(8,128)}, u32[]{:S(2)}) copy-start(f32[8,32,256]{2,1,0:T(8,128)} %rhs.1) | copy-start | bytes 786436
  1.2 1.5 %collective-permute-start.2 = (f32[5,32,256]{2,1,0:T(8,128)S(1)}, f32[5,32,256]{2,1,0:T(8,128)S(1)}, u32[]{:S(2)}, u32[]{:S(2)}) collective-permute-start(f32[5,32,256]{2,1,0:T(8,128)S(1)} %get-tuple-element.43), channel_id=1, source_target_pairs={{0,2},{1,3},{2,0},{3,1},{4,6},{5,7},{6,4},{7,5},{8,10},{9,11},{10,... | collective-permute-start | bytes 491528 | tf_op jit(solution)/shard_map/ppermute | solution.py:771
  1.7 8.1 %collective-permute-start = (f32[5,32,256]{2,1,0:T(8,128)S(1)}, f32[5,32,256]{2,1,0:T(8,128)S(1)}, u32[]{:S(2)}, u32[]{:S(2)}) collective-permute-start(f32[5,32,256]{2,1,0:T(8,128)S(1)} %get-tuple-element.40), channel_id=1, source_target_pairs={{0,0},{1,1},{2,4},{3,5},{4,2},{5,3},{6,8},{7,9},{8,6},{9,7},{10,12... | collective-permute-start | bytes 491528 | tf_op jit(solution)/shard_map/ppermute | solution.py:771
  2.8 5.4 %collective-permute-start.3 = (f32[11,8,256]{2,1,0:T(8,128)S(1)}, f32[11,8,256]{2,1,0:T(8,128)S(1)}, u32[]{:S(2)}, u32[]{:S(2)}) collective-permute-start(f32[11,8,256]{2,1,0:T(8,128)S(1)} %shard_map.47), channel_id=1, source_target_pairs={{0,1},{1,0},{2,3},{3,2},{4,5},{5,4},{6,7},{7,6},{8,9},{9,8},{10,11... | collective-permute-start | bytes 270344 | tf_op jit(solution)/shard_map/ppermute | solution.py:780
  5.7 2.5 %copy-start.1 = (s32[1,4]{1,0:T(1,128)S(1)}, s32[1,4]{1,0:T(1,128)}, u32[]{:S(2)}) copy-start(s32[1,4]{1,0:T(1,128)} %route.1) | copy-start | bytes 52
  5.7 4.1 %collective-permute-start.1 = (f32[3,8,256]{2,1,0:T(8,128)S(1)}, f32[3,8,256]{2,1,0:T(8,128)S(1)}, u32[]{:S(2)}, u32[]{:S(2)}) collective-permute-start(f32[3,8,256]{2,1,0:T(8,128)S(1)} %get-tuple-element.41), channel_id=1, source_target_pairs={{0,1},{1,0},{2,5},{3,4},{4,3},{5,2},{6,9},{7,8},{8,7},{9,6},{10,13... | collective-permute-start | bytes 73736 | tf_op jit(solution)/shard_map/ppermute | solution.py:771
  11.1 14.6 %all-to-all-start = ((f32[32,2,1,128]{3,1,2,0:T(2,128)}), f32[32,2,1,128]{3,1,2,0:T(2,128)S(1)}, u32[]{:S(2)}, u32[]{:S(2)}) async-start(f32[32,2,1,128]{3,1,2,0:T(2,128)} %bitcast.1), calls=%async_computation | async-start | bytes 65536 | tf_op jit(solution)/shard_map/all_to_all | solution.py:821
  18.5 4.7 %collective-permute-start.4 = (f32[40,256]{1,0:T(8,128)S(1)}, f32[40,256]{1,0:T(8,128)S(1)}, u32[]{:S(2)}, u32[]{:S(2)}) collective-permute-start(f32[40,256]{1,0:T(8,128)S(1)} %get-tuple-element.60), channel_id=1, source_target_pairs={{0,2},{1,3},{2,0},{3,1},{4,6},{5,7},{6,4},{7,5},{8,10},{9,11},{10,... | collective-permute-start | bytes 122888 | tf_op jit(solution)/shard_map/ppermute | solution.py:823
  18.8 4.4 %collective-permute-start.5 = (f32[40,256]{1,0:T(8,128)S(1)}, f32[40,256]{1,0:T(8,128)S(1)}, u32[]{:S(2)}, u32[]{:S(2)}) collective-permute-start(f32[40,256]{1,0:T(8,128)S(1)} %get-tuple-element.61), channel_id=1, source_target_pairs={{0,0},{1,1},{2,4},{3,5},{4,2},{5,3},{6,8},{7,9},{8,6},{9,7},{10,12... | collective-permute-start | bytes 122888 | tf_op jit(solution)/shard_map/ppermute | solution.py:822
  19.5 3.7 %collective-permute-start.6 = (f32[8,256]{1,0:T(8,128)S(1)}, f32[8,256]{1,0:T(8,128)S(1)}, u32[]{:S(2)}, u32[]{:S(2)}) collective-permute-start(f32[8,256]{1,0:T(8,128)S(1)} %get-tuple-element.64), channel_id=1, source_target_pairs={{0,1},{1,0},{2,3},{3,2},{4,5},{5,4},{6,7},{7,6},{8,9},{9,8},{10,11... | collective-permute-start | bytes 24584 | tf_op jit(solution)/shard_map/ppermute | solution.py:825

commit v7 on v6

--- a/solution.py
+++ b/solution.py
@@ -62,7 +62,9 @@
 
 
 def gather(value, low, high, wx_low, wx_high, wy, wz):
-    total = wx_high * high + wx_low * low
+    total = wx_high * high
+    if low is not None:
+        total = total + wx_low * low
     total = total + wy * roll(value, -1, 0) + roll(wy * value, 1, 0)
     return total + wz * roll(value, -1, 1) + roll(wz * value, 1, 1)
 
@@ -212,19 +214,23 @@
     def row(self, own, halo):
         return jnp.concatenate([own, halo], axis=0)
 
-    def diagonal(self, low, here, high, valid=None):
+    def doubled(self, low, here, high):
         above = jnp.where(self.last_lane, 0.0, roll(here, -1, 1))
         below = jnp.where(self.lane == 0, 0.0, roll(here, 1, 1))
         right = roll(here, -1, 0)
-        doubled = 6.0 * here + (low + high) + (right + roll(here, 1, 0)) + (above + below)
+        ends = high if low is None else low + high
+        return 6.0 * here + ends + (right + roll(here, 1, 0)) + (above + below), right, above
+
+    def gain_of(self, doubled, valid=None):
         ok = self.col_ok & (doubled > 0.0)
         if valid is not None:
             ok = ok & valid
-        return doubled, jnp.where(ok, (2.0 * OMEGA) / doubled, 0.0), right, above
+        return jnp.where(ok, (2.0 * OMEGA) / doubled, 0.0)
 
     def weights(self, q, gain, src, first, diag, wx, wy, wz, x, valid=None):
         here = q[x]
-        doubled, gain_here, right, above = self.diagonal(q[x - 1], here, q[x + 1], valid)
+        doubled, right, above = self.doubled(q[x - 1], here, q[x + 1])
+        gain_here = self.gain_of(doubled, valid)
         gain[x] = gain_here
         first[x] = gain_here * src[x]
         if diag is not None:
@@ -276,68 +282,18 @@
     return pack_pairs(t[:, 0], t[:, 1], 2)
 
 
-def early_kernel(nd, nc, tiles, rhs, conduct, route, even, *refs):
+def tile_kernel(tiles, conduct, route, coef, touched):
     rows, cols, layers = conduct.shape
     tile_w = cols // tiles
     couples = tiles // 2
-    n_cross = len(pairings(nc))
-    strips = refs[:n_cross]
-    *arrays, res_coarse, res_row, coef, sums, touched = refs[n_cross:]
-    early, _ = spans(rows)
-    at = {n: Rows((r, early[n][0], r.shape[0])) for n, r in zip(EARLY, arrays)}
-    q, src, gain, first, diag, wx, wy, wz, pres = (at[n] for n in EARLY)
-    frame = Frame(nd, nc, cols, layers)
-    own, halo = frame.own, frame.halo
-
-    for x in range(rows):
-        q[x] = frame.row(conduct[x], frame.merged(strips, 0, x))
-        src[x] = frame.row(rhs[counted(x, rows)], frame.merged(strips, 0, rows + x))
-    _, valid = facing(lax.axis_index("down"), nd, False)
-    for i in range(DEPTH):
-        q[rows + i] = jnp.where(valid, frame.row(even[i], frame.merged(strips, rows, i)), 0.0)
-    for i in range(DEPTH - 1):
-        corner = frame.merged(strips, rows, DEPTH + i)
-        src[rows + i] = jnp.where(valid, frame.row(even[DEPTH + i], corner), 0.0)
-
-    here = q[0]
-    above = jnp.where(frame.last_lane, 0.0, roll(here, -1, 1))
-    frame.plane_weights(wy, wz, 0, here, roll(here, -1, 0), above)
-    wx[0] = 0.5 * (here + q[1])
-    for x in range(*early["gain"]):
-        frame.weights(
-            q, gain, src, first,
-            diag if x < rows else None,
-            wx if x < early["wx"][1] else None,
-            wy if x < early["wy"][1] else None,
-            wz, x, valid if x >= rows else None,
-        )
-    for x in range(*early["pres"]):
-        pres[x] = smooth(first, gain, src, wx, wy, wz, x)
-
-    res = {x: residual(frame, src, diag, pres, wx, wy, wz, x) for x in range(3, rows)}
-    res_row[...] = res[3]
-    for k in range(2, rows // 2):
-        res_coarse[k - 2] = coarse_rows(res[2 * k] + res[2 * k + 1], couples, tile_w)
-
     even_lane = iota((tile_w, layers), 1) % 2 == 0
     for t in range(couples):
         numbers = [jnp.broadcast_to(route[0:1, i : i + 1], (tile_w, layers)) for i in (2 * t, 2 * t + 1)]
         touched[t] = jnp.where(jnp.where(even_lane, *numbers) >= 0, 1.0, 0.0)
 
-    strip_col = iota((STRIP, layers), 0)
-    plane = sum(q[x][own] for x in range(rows))
-    beyond = sum(q[x][halo] for x in range(rows))
-    own_lane = iota((cols, layers), 1)
-    low, high = strip_col < 2, strip_col >= STRIP - 2
-    sums[0:1] = fold(sum(res.values()))
-    sums[1:2] = fold(sum(q[x][own] for x in range(rows - 2, rows + 2)))
-    sums[2:3] = fold(jnp.where(high, plane[cols - STRIP :], 0.0) + jnp.where(low, beyond, 0.0))
-    sums[3:4] = fold(jnp.where(low, plane[:STRIP], 0.0) + jnp.where(high, beyond, 0.0))
-    sums[4:5] = fold(jnp.where((own_lane < 2) | (own_lane >= layers - 2), plane, 0.0))
-
     packs = rows // 4
     by_row = [
-        coarse_rows(0.125 * (q[2 * k][own] + q[2 * k + 1][own]), couples, tile_w)
+        coarse_rows(0.125 * (conduct[2 * k] + conduct[2 * k + 1]), couples, tile_w)
         for k in range(rows // 2)
     ]
     con = [pack_pairs(by_row[k], by_row[k + packs], 1) for k in range(packs)]
@@ -372,12 +328,74 @@
         coef[2 * packs + k] = jnp.where(z_end, 0.0, 2.0 * (c + z_high))
 
 
+def early_kernel(nd, nc, tiles, rhs, conduct, even, *refs):
+    rows, cols, layers = conduct.shape
+    tile_w = cols // tiles
+    couples = tiles // 2
+    n_cross = len(pairings(nc))
+    strips = refs[:n_cross]
+    *arrays, res_coarse, res_row, part, sums = refs[n_cross:]
+    early, _ = spans(rows)
+    at = {n: Rows((r, early[n][0], r.shape[0])) for n, r in zip(EARLY, arrays)}
+    q, src, gain, first, diag, wx, wy, wz, pres = (at[n] for n in EARLY)
+    frame = Frame(nd, nc, cols, layers)
+    own, halo = frame.own, frame.halo
+
+    for x in range(rows):
+        q[x] = frame.row(conduct[x], frame.merged(strips, 0, x))
+        src[x] = frame.row(rhs[counted(x, rows)], frame.merged(strips, 0, rows + x))
+    _, valid = facing(lax.axis_index("down"), nd, False)
+    for i in range(DEPTH):
+        q[rows + i] = jnp.where(valid, frame.row(even[i], frame.merged(strips, rows, i)), 0.0)
+    for i in range(DEPTH - 1):
+        corner = frame.merged(strips, rows, DEPTH + i)
+        src[rows + i] = jnp.where(valid, frame.row(even[DEPTH + i], corner), 0.0)
+
+    here = q[0]
+    above = jnp.where(frame.last_lane, 0.0, roll(here, -1, 1))
+    frame.plane_weights(wy, wz, 0, here, roll(here, -1, 0), above)
+    wx[0] = 0.5 * (here + q[1])
+    part[0] = frame.doubled(None, here, q[1])[0]
+    for x in range(*early["gain"]):
+        frame.weights(
+            q, gain, src, first,
+            diag if x < rows else None,
+            wx if x < early["wx"][1] else None,
+            wy if x < early["wy"][1] else None,
+            wz, x, valid if x >= rows else None,
+        )
+    for x in range(*early["pres"]):
+        pres[x] = smooth(first, gain, src, wx, wy, wz, x)
+
+    spread = gather(first[1], None, first[2], None, wx[1], wy[1], wz[1])
+    part[1] = KEEP * first[1] + gain[1] * (src[1] + spread)
+    part[2] = gain[1] * wx[0]
+    spread = gather(pres[2], None, pres[3], None, wx[2], wy[2], wz[2])
+    part[3] = src[2] - diag[2] * pres[2] + spread
+
+    res = {x: residual(frame, src, diag, pres, wx, wy, wz, x) for x in range(3, rows)}
+    res_row[...] = res[3]
+    for k in range(2, rows // 2):
+        res_coarse[k - 2] = coarse_rows(res[2 * k] + res[2 * k + 1], couples, tile_w)
+
+    strip_col = iota((STRIP, layers), 0)
+    plane = sum(q[x][own] for x in range(rows))
+    beyond = sum(q[x][halo] for x in range(rows))
+    own_lane = iota((cols, layers), 1)
+    low, high = strip_col < 2, strip_col >= STRIP - 2
+    sums[0:1] = fold(sum(res.values()))
+    sums[1:2] = fold(sum(q[x][own] for x in range(rows - 2, rows + 2)))
+    sums[2:3] = fold(jnp.where(high, plane[cols - STRIP :], 0.0) + jnp.where(low, beyond, 0.0))
+    sums[3:4] = fold(jnp.where(low, plane[:STRIP], 0.0) + jnp.where(high, beyond, 0.0))
+    sums[4:5] = fold(jnp.where((own_lane < 2) | (own_lane >= layers - 2), plane, 0.0))
+
+
 def late_kernel(nd, nc, tiles, rows, odd, *refs):
     n_cross = len(pairings(nc)) if len(pairings(nd)) > 1 else 0
     corners = refs[:n_cross]
-    n_in = n_cross + len(EARLY) + 5
+    n_in = n_cross + len(EARLY) + 6
     early_refs = dict(zip(EARLY, refs[n_cross:]))
-    res_coarse, res_row, coef, sums, touched = refs[n_in - 5 : n_in]
+    res_coarse, res_row, part, sums, coef, touched = refs[n_in - 6 : n_in]
     names = LATE_KEPT + ("fix", "near", "far", "chunks_hbm") + LATE_SCRATCH + ("chunks", "sem")
     n_side = len(pairings(nc))
     sides = refs[n_in : n_in + n_side]
@@ -402,17 +420,19 @@
     for i in range(DEPTH - 1):
         corner = frame.merged(corners, 0, DEPTH + i)
         src[-1 - i] = jnp.where(valid, frame.row(odd[DEPTH + i], corner), 0.0)
-    for x in range(*late["gain"]):
+    for x in range(*late["wx"]):
         frame.weights(
-            q, gain, src, first,
-            diag if x == 0 else None,
-            wx if x < 0 else None,
-            wy if x == -1 else None,
-            wz, x, valid if x < 0 else None,
+            q, gain, src, first, None, wx, wy if x == -1 else None, wz, x, valid
         )
-    for x in range(*late["pres"]):
+    doubled = part[0] + q[-1]
+    gain[0] = frame.gain_of(doubled)
+    first[0] = gain[0] * src[0]
+    diag[0] = 0.5 * doubled
+    for x in (-1, 0):
         pres[x] = smooth(first, gain, src, wx, wy, wz, x)
-    res = [residual(frame, src, diag, pres, wx, wy, wz, x) for x in range(3)]
+    pres[1] = part[1] + part[2] * first[0]
+    res = [residual(frame, src, diag, pres, wx, wy, wz, x) for x in (0, 1)]
+    res.append((part[3] + wx[1] * pres[1])[frame.own])
     res.append(res_row[...])
 
     res_total = sums[0:1] + fold(res[0] + res[1] + res[2])
@@ -510,18 +530,21 @@
 
     answer = [jnp.zeros_like(t) for t in totals]
     resid = search = totals
-    norm = dot(totals, totals)
+    image = operate(resid)
+    norm, bend = dot(resid, resid), dot(resid, image)
+    alpha = norm / bend
     for step in range(COARSE_ITERS):
-        image = operate(search)
-        alpha = norm / dot(search, image)
         answer = [a + alpha * s for a, s in zip(answer, search)]
         if step == COARSE_ITERS - 1:
             break
+        scale = 1.0 / norm
         resid = [r - alpha * m for r, m in zip(resid, image)]
-        norm_next = dot(resid, resid)
-        beta = norm_next / norm
+        moved = operate(resid)
+        norm, bend = dot(resid, resid), dot(resid, moved)
+        beta = norm * scale
+        alpha = norm / (bend - beta * norm / alpha)
         search = [r + beta * s for r, s in zip(resid, search)]
-        norm = norm_next
+        image = [m + beta * i for m, i in zip(moved, image)]
     return answer
 
 
@@ -789,12 +812,16 @@
         + [
             whole(rows // 2 - 2, *tile_shape),
             whole(cols, layers),
-            whole(4 * packs + 1, *tile_shape),
+            whole(4, wide, layers),
             whole(5, LANES),
-            whole(*tile_shape),
         ],
-        [vmem] * (4 + len(strips)),
-    )(right_side, conduct, tile_route, even, *strips)
+        [vmem] * (3 + len(strips)),
+    )(right_side, conduct, even, *strips)
+    first_part += call(
+        functools.partial(tile_kernel, tiles),
+        [whole(4 * packs + 1, *tile_shape), whole(*tile_shape)],
+        [vmem] * 2,
+    )(conduct, tile_route)
     late_arrays = call(
         functools.partial(late_kernel, nd, nc, tiles, rows),
         [whole(STRIP, layers) for _ in pairings(nc)]

time: 27.3 us -> 27.1 us (level)
  waiting for transfers between devices: 6.29 us -> 5.53 us
  local copies, waits for them, and re-layouts: 0.01 us -> 0.57 us
    ppermute x2, waiting for transfers between devices: 3.46 us -> 2.69 us  [body(): lax.ppermute(m, axes, pairs_of(nd, nc, None, cross_kind))]
    unnamed x4, local copies, waits for them, and re-layouts: 0.01 us -> 0.57 us
  transfers between devices with their start and end apart: 8 -> 8, of which waited for: 5 -> 5; matrix products, arithmetic and copies ran while one was open for 0% -> 0% of each run, Pallas kernels for 10% -> 11%
where the time goes in v7:
time: 27.1 us; the launch traced here: 26.9 us
  starting transfers between devices  14.3 us (53%)
  Pallas kernels  6.48 us (24%)
  waiting for transfers between devices  5.53 us (20%)
  local copies, waits for them, and re-layouts  0.57 us (2%)
    all_to_all x1, starting transfers between devices, body(): lax.all_to_all(chunks, ('cross', 'down'), 0, 0, tiled=True)  7.37 us
    ppermute x2, starting transfers between devices, body(): lax.ppermute(m, axes, pairs_of(nd, nc, None, cross_kind))  4.66 us
    ppermute x2, waiting for transfers between devices, body(): lax.ppermute(m, axes, pairs_of(nd, nc, None, cross_kind))  2.69 us
    all_to_all x1, waiting for transfers between devices, body(): lax.all_to_all(chunks, ('cross', 'down'), 0, 0, tiled=True)  1.9 us
    pallas_call x1, Pallas kernels, body(): call(functools.partial(late_kernel, nd, nc, tiles, rows), [whole(STRIP, l...  1.29 us
    ppermute x3, starting transfers between devices, body(): received = [lax.ppermute(m, axes, p) for m, p in zip(messages, perms)]  1.26 us
    pallas_call x1, Pallas kernels, body(): call(functools.partial(last_kernel, nd, nc), block, [vmem] * (2 + len(res...  1.2 us
    pallas_call x1, Pallas kernels, body(): call(functools.partial(pack_kernel, nd, nc), [block] + shapes + strips, [...  1.17 us
  transfers between devices with their start and end apart: 8, of which 5 were waited for; matrix products, arithmetic and copies ran while one was open for 0% of the time, Pallas kernels for 11%

profile of v7, /device:TPU:0, one launch (start us, length us, event | category | flops | bytes accessed | tf_op | source)
XLA Modules:
  0.0 26.9 jit_solution(7424279236810360423)
XLA Ops:
  0.0 1.2 %shard_map.46 = (f32[8,32,256]{2,1,0:T(8,128)S(1)}, f32[5,32,256]{2,1,0:T(8,128)S(1)}, f32[5,32,256]{2,1,0:T(8,128)S(1)}, f32[3,8,256]{2,1,0:T(8,128)S(1)}, f32[8,8,256]{2,1,0:T(8,128)S(1)}) custom-call(f32[8,32,256]{2,1,0:T(8,128)} %rhs.1, f32[8,32,256]{2,1,0:T(8,128)} %kappa_hbm.1, s32[8,32,256]{2,1,0:T(8,128)} %mask_hbm.1), custom_call_target="tpu_custom_call" | custom-call | tf_op jit(solution)/shard_map/pallas_call | solution.py:781
  1.2 0.5 %collective-permute-start.2 = (f32[5,32,256]{2,1,0:T(8,128)S(1)}, f32[5,32,256]{2,1,0:T(8,128)S(1)}, u32[]{:S(2)}, u32[]{:S(2)}) collective-permute-start(f32[5,32,256]{2,1,0:T(8,128)S(1)} %get-tuple-element.44), channel_id=1, source_target_pairs={{0,2},{1,3},{2,0},{3,1},{4,6},{5,7},{6,4},{7,5},{8,10},{9,11},{10,... | collective-permute-start | bytes 491528 | tf_op jit(solution)/shard_map/ppermute | solution.py:794
  1.7 0.7 %collective-permute-start = (f32[5,32,256]{2,1,0:T(8,128)S(1)}, f32[5,32,256]{2,1,0:T(8,128)S(1)}, u32[]{:S(2)}, u32[]{:S(2)}) collective-permute-start(f32[5,32,256]{2,1,0:T(8,128)S(1)} %get-tuple-element.41), channel_id=1, source_target_pairs={{0,0},{1,1},{2,4},{3,5},{4,2},{5,3},{6,8},{7,9},{8,6},{9,7},{10,12... | collective-permute-start | bytes 491528 | tf_op jit(solution)/shard_map/ppermute | solution.py:794
  2.4 0.4 %collective-permute-done.2.even = f32[5,32,256]{2,1,0:T(8,128)S(1)} collective-permute-done((f32[5,32,256]{2,1,0:T(8,128)S(1)}, f32[5,32,256]{2,1,0:T(8,128)S(1)}, u32[]{:S(2)}, u32[]{:S(2)}) %collective-permute-start.2) | collective-permute-done | bytes 163872 | tf_op jit(solution)/shard_map/ppermute | solution.py:794
  2.7 0.0 copy-start
  2.7 2.9 %collective-permute-start.3 = (f32[11,8,256]{2,1,0:T(8,128)S(1)}, f32[11,8,256]{2,1,0:T(8,128)S(1)}, u32[]{:S(2)}, u32[]{:S(2)}) collective-permute-start(f32[11,8,256]{2,1,0:T(8,128)S(1)} %shard_map.47), channel_id=1, source_target_pairs={{0,1},{1,0},{2,3},{3,2},{4,5},{5,4},{6,7},{7,6},{8,9},{9,8},{10,11... | collective-permute-start | bytes 270344 | tf_op jit(solution)/shard_map/ppermute | solution.py:803
  5.7 0.0 copy-start.1
  5.7 0.1 collective-permute-start.1
  5.8 0.6 %copy-done.1 = s32[1,4]{1,0:T(1,128)S(1)} copy-done((s32[1,4]{1,0:T(1,128)S(1)}, s32[1,4]{1,0:T(1,128)}, u32[]{:S(2)}) %copy-start.1) | copy-done | bytes 40
  6.3 0.2 shard_map.49
  6.5 1.6 %collective-permute-done.3.refs_0_ = f32[11,8,256]{2,1,0:T(8,128)S(1)} collective-permute-done((f32[11,8,256]{2,1,0:T(8,128)S(1)}, f32[11,8,256]{2,1,0:T(8,128)S(1)}, u32[]{:S(2)}, u32[]{:S(2)}) %collective-permute-start.3) | collective-permute-done | bytes 90144 | tf_op jit(solution)/shard_map/ppermute | solution.py:803
  8.2 0.0 copy-done
  8.2 1.0 %shard_map.48 = (f32[11,40,256]{2,1,0:T(8,128)S(1)}, f32[10,40,256]{2,1,0:T(8,128)S(1)}, f32[9,40,256]{2,1,0:T(8,128)S(1)}, f32[9,40,256]{2,1,0:T(8,128)S(1)}, f...) custom-call(f32[8,32,256]{2,1,0:T(8,128)S(1)} %copy-done, ...), custom_call_target="tpu_custom_call" | custom-call | tf_op jit(solution)/shard_map/pallas_call | solution.py:809
  9.2 0.6 %collective-permute-done.1.refs_0_ = f32[3,8,256]{2,1,0:T(8,128)S(1)} collective-permute-done((f32[3,8,256]{2,1,0:T(8,128)S(1)}, f32[3,8,256]{2,1,0:T(8,128)S(1)}, u32[]{:S(2)}, u32[]{:S(2)}) %collective-permute-start.1) | collective-permute-done | bytes 24608 | tf_op jit(solution)/shard_map/ppermute | solution.py:794
  9.8 0.0 collective-permute-done.odd
  9.8 1.3 %shard_map.50 = (f32[8,256]{1,0:T(8,128)S(1)}, f32[2,40,256]{2,1,0:T(8,128)S(1)}, f32[3,40,256]{2,1,0:T(8,128)S(1)}, f32[2,40,256]{2,1,0:T(8,128)S(1)}, f32[1,40...) custom-call(f32[5,32,256]{2,1,0:T(8,128)S(1)} %collective-permute-do, ...), custom_call_target="tpu_custom_call" | custom-call | tf_op jit(solution)/shard_map/pallas_call | solution.py:825
  11.1 7.4 %all-to-all-start = ((f32[32,2,1,128]{3,1,2,0:T(2,128)}), f32[32,2,1,128]{3,1,2,0:T(2,128)S(1)}, u32[]{:S(2)}, u32[]{:S(2)}) async-start(f32[32,2,1,128]{3,1,2,0:T(2,128)} %bitcast.1), calls=%async_computation | async-start | bytes 65536 | tf_op jit(solution)/shard_map/all_to_all | solution.py:848
  18.4 0.3 %collective-permute-start.4 = (f32[40,256]{1,0:T(8,128)S(1)}, f32[40,256]{1,0:T(8,128)S(1)}, u32[]{:S(2)}, u32[]{:S(2)}) collective-permute-start(f32[40,256]{1,0:T(8,128)S(1)} %get-tuple-element.62), channel_id=1, source_target_pairs={{0,2},{1,3},{2,0},{3,1},{4,6},{5,7},{6,4},{7,5},{8,10},{9,11},{10,... | collective-permute-start | bytes 122888 | tf_op jit(solution)/shard_map/ppermute | solution.py:850
  18.8 0.7 %collective-permute-start.5 = (f32[40,256]{1,0:T(8,128)S(1)}, f32[40,256]{1,0:T(8,128)S(1)}, u32[]{:S(2)}, u32[]{:S(2)}) collective-permute-start(f32[40,256]{1,0:T(8,128)S(1)} %get-tuple-element.63), channel_id=1, source_target_pairs={{0,0},{1,1},{2,4},{3,5},{4,2},{5,3},{6,8},{7,9},{8,6},{9,7},{10,12... | collective-permute-start | bytes 122888 | tf_op jit(solution)/shard_map/ppermute | solution.py:849
  19.4 1.7 %collective-permute-start.6 = (f32[8,256]{1,0:T(8,128)S(1)}, f32[8,256]{1,0:T(8,128)S(1)}, u32[]{:S(2)}, u32[]{:S(2)}) collective-permute-start(f32[8,256]{1,0:T(8,128)S(1)} %get-tuple-element.66), channel_id=1, source_target_pairs={{0,1},{1,0},{2,3},{3,2},{4,5},{5,4},{6,7},{7,6},{8,9},{9,8},{10,11... | collective-permute-start | bytes 24584 | tf_op jit(solution)/shard_map/ppermute | solution.py:852
  21.1 0.9 %shard_map.52 = (f32[8,32,256]{2,1,0:T(8,128)S(1)}, f32[2,32,256]{2,1,0:T(8,128)S(1)}, f32[2,32,256]{2,1,0:T(8,128)S(1)}, f32[8,16,256]{2,1,0:T(8,128)S(1)}, f32[2,16,256]{2,1,0:T(8,128)S(1)}) custom-call(f32[10,40,256]{2,1,0:T(8,128)S(1)} %get-tuple-element.47.refs_2_.refs_1_.refs_0_, f32[9,40,256]{2,1,0:T(8,128)S(1)} %get-tuple-element.48.refs_3_.refs_2_.refs_1_, ...), custom_call_target="tpu_custom_call" | custom-call | tf_op jit(solution)/shard_map/pallas_call | solution.py:864
  22.1 1.0 %collective-permute-done.6.refs_0_ = f32[8,256]{1,0:T(8,128)S(1)} collective-permute-done((f32[8,256]{1,0:T(8,128)S(1)}, f32[8,256]{1,0:T(8,128)S(1)}, u32[]{:S(2)}, u32[]{:S(2)}) %collective-permute-start.6) | collective-permute-done | bytes 8224 | tf_op jit(solution)/shard_map/ppermute | solution.py:852
  23.1 0.0 collective-permute-done.4.near
  23.1 0.0 collective-permute-done.5.far
  23.1 0.7 %shard_map.51.base = f32[8,32,256]{2,1,0:T(8,128)S(1)} custom-call(f32[40,256]{1,0:T(8,128)S(1)} %collective-permute-done.4.near, f32[40,256]{1,0:T(8,128)S(1)} %collective-permute-done.5.far, f32[2,2,8,256]{3,2,1,0:T(8,128)S(1)} %get-tuple-element.64.fix, f32[7,40,256]{2,1,0:T(8,128)S(1)} %get-tuple-element.54.refs_9_.pres_early, ...), custom_call_target="tpu_custom_call" | custom-call | tf_op jit(solution)/shard_map/pallas_call | solution.py:855
  23.8 1.9 %all-to-all-done = f32[32,2,1,128]{3,1,2,0:T(2,128)S(1)} async-done(((f32[32,2,1,128]{3,1,2,0:T(2,128)}), f32[32,2,1,128]{3,1,2,0:T(2,128)S(1)}, u32[]{:S(2)}, u32[]{:S(2)}) %all-to-all-start) | async-done | bytes 32800 | tf_op jit(solution)/shard_map/all_to_all | solution.py:848
  25.7 1.2 %shard_map.53 = f32[8,32,256]{2,1,0:T(8,128)} custom-call(f32[64,128]{1,0:T(8,128)S(1)} %bitcast.4, f32[8,32,256]{2,1,0:T(8,128)S(1)} %shard_map.51.base, f32[8,32,256]{2,1,0:T(8,128)S(1)} %get-tuple-element.72.every, f32[2,32,256]{2,1,0:T(8,128)S(1)} %get-tuple-element.73.by_odd, f32[2,32,256]{2,1,0:T(8,128)S(1)} %get-tuple-element.74.by_even, ...), custom_call_target="tpu_custom_call" | custom-call | tf_op jit(solution)/shard_map/pallas_call | solution.py:875
  (1 shorter events, 0.0 us)
Async XLA Ops:
  1.2 1.5 %collective-permute-start.2 = (f32[5,32,256]{2,1,0:T(8,128)S(1)}, f32[5,32,256]{2,1,0:T(8,128)S(1)}, u32[]{:S(2)}, u32[]{:S(2)}) collective-permute-start(f32[5,32,256]{2,1,0:T(8,128)S(1)} %get-tuple-element.44), channel_id=1, source_target_pairs={{0,2},{1,3},{2,0},{3,1},{4,6},{5,7},{6,4},{7,5},{8,10},{9,11},{10,... | collective-permute-start | bytes 491528 | tf_op jit(solution)/shard_map/ppermute | solution.py:794
  1.7 8.1 %collective-permute-start = (f32[5,32,256]{2,1,0:T(8,128)S(1)}, f32[5,32,256]{2,1,0:T(8,128)S(1)}, u32[]{:S(2)}, u32[]{:S(2)}) collective-permute-start(f32[5,32,256]{2,1,0:T(8,128)S(1)} %get-tuple-element.41), channel_id=1, source_target_pairs={{0,0},{1,1},{2,4},{3,5},{4,2},{5,3},{6,8},{7,9},{8,6},{9,7},{10,12... | collective-permute-start | bytes 491528 | tf_op jit(solution)/shard_map/ppermute | solution.py:794
  2.7 5.5 %copy-start = (f32[8,32,256]{2,1,0:T(8,128)S(1)}, f32[8,32,256]{2,1,0:T(8,128)}, u32[]{:S(2)}) copy-start(f32[8,32,256]{2,1,0:T(8,128)} %rhs.1) | copy-start | bytes 786436
  2.7 5.4 %collective-permute-start.3 = (f32[11,8,256]{2,1,0:T(8,128)S(1)}, f32[11,8,256]{2,1,0:T(8,128)S(1)}, u32[]{:S(2)}, u32[]{:S(2)}) collective-permute-start(f32[11,8,256]{2,1,0:T(8,128)S(1)} %shard_map.47), channel_id=1, source_target_pairs={{0,1},{1,0},{2,3},{3,2},{4,5},{5,4},{6,7},{7,6},{8,9},{9,8},{10,11... | collective-permute-start | bytes 270344 | tf_op jit(solution)/shard_map/ppermute | solution.py:803
  5.7 0.7 %copy-start.1 = (s32[1,4]{1,0:T(1,128)S(1)}, s32[1,4]{1,0:T(1,128)}, u32[]{:S(2)}) copy-start(s32[1,4]{1,0:T(1,128)} %route.1) | copy-start | bytes 52
  5.7 4.1 %collective-permute-start.1 = (f32[3,8,256]{2,1,0:T(8,128)S(1)}, f32[3,8,256]{2,1,0:T(8,128)S(1)}, u32[]{:S(2)}, u32[]{:S(2)}) collective-permute-start(f32[3,8,256]{2,1,0:T(8,128)S(1)} %get-tuple-element.42), channel_id=1, source_target_pairs={{0,1},{1,0},{2,5},{3,4},{4,3},{5,2},{6,9},{7,8},{8,7},{9,6},{10,13... | collective-permute-start | bytes 73736 | tf_op jit(solution)/shard_map/ppermute | solution.py:794
  11.1 14.7 %all-to-all-start = ((f32[32,2,1,128]{3,1,2,0:T(2,128)}), f32[32,2,1,128]{3,1,2,0:T(2,128)S(1)}, u32[]{:S(2)}, u32[]{:S(2)}) async-start(f32[32,2,1,128]{3,1,2,0:T(2,128)} %bitcast.1), calls=%async_computation | async-start | bytes 65536 | tf_op jit(solution)/shard_map/all_to_all | solution.py:848
  18.4 4.7 %collective-permute-start.4 = (f32[40,256]{1,0:T(8,128)S(1)}, f32[40,256]{1,0:T(8,128)S(1)}, u32[]{:S(2)}, u32[]{:S(2)}) collective-permute-start(f32[40,256]{1,0:T(8,128)S(1)} %get-tuple-element.62), channel_id=1, source_target_pairs={{0,2},{1,3},{2,0},{3,1},{4,6},{5,7},{6,4},{7,5},{8,10},{9,11},{10,... | collective-permute-start | bytes 122888 | tf_op jit(solution)/shard_map/ppermute | solution.py:850
  18.8 4.4 %collective-permute-start.5 = (f32[40,256]{1,0:T(8,128)S(1)}, f32[40,256]{1,0:T(8,128)S(1)}, u32[]{:S(2)}, u32[]{:S(2)}) collective-permute-start(f32[40,256]{1,0:T(8,128)S(1)} %get-tuple-element.63), channel_id=1, source_target_pairs={{0,0},{1,1},{2,4},{3,5},{4,2},{5,3},{6,8},{7,9},{8,6},{9,7},{10,12... | collective-permute-start | bytes 122888 | tf_op jit(solution)/shard_map/ppermute | solution.py:849
  19.4 3.7 %collective-permute-start.6 = (f32[8,256]{1,0:T(8,128)S(1)}, f32[8,256]{1,0:T(8,128)S(1)}, u32[]{:S(2)}, u32[]{:S(2)}) collective-permute-start(f32[8,256]{1,0:T(8,128)S(1)} %get-tuple-element.66), channel_id=1, source_target_pairs={{0,1},{1,0},{2,3},{3,2},{4,5},{5,4},{6,7},{7,6},{8,9},{9,8},{10,11... | collective-permute-start | bytes 24584 | tf_op jit(solution)/shard_map/ppermute | solution.py:852

commit v8 on v7

--- a/solution.py
+++ b/solution.py
@@ -14,7 +14,7 @@
 SNOW_FACTOR = 3.0
 
 DEPTH = 3
-CORNER = DEPTH
+CORNER = 2
 STRIP = 8
 LANES = 128
 CHUNK = 2
@@ -101,17 +101,70 @@
     return pl.ds(pl.multiple_of(jnp.where(right, cols - STRIP, 0), STRIP), STRIP)
 
 
-def pack_rows(out, start, tiles, right):
-    for i in range(0, len(tiles), 2):
-        a, b = tiles[i], tiles[min(i + 1, len(tiles) - 1)]
-        upper = iota(a.shape, 0) < STRIP // 2
-        a, b = jnp.where(right, roll(a, STRIP // 2, 0), a), jnp.where(right, b, roll(b, STRIP // 2, 0))
-        out[start + i // 2] = jnp.where(upper, a, b)
+def upper_half(tile, right):
+    return jnp.where(right, roll(tile, STRIP // 2, 0), tile)
+
+
+def lower_half(tile, right):
+    return jnp.where(right, tile, roll(tile, STRIP // 2, 0))
+
+
+def pack_rows(tiles, right):
+    upper = iota(tiles[0].shape, 0) < STRIP // 2
+    return [
+        jnp.where(upper, upper_half(a, right), lower_half(b, right)) for a, b in zip(tiles[::2], tiles[1::2])
+    ]
+
+
+def pack_source(tiles, right):
+    *packed, last = pack_rows(tiles, right)
+    col = iota(last.shape, 0) % (STRIP // 2)
+    free = col == jnp.where(right, 0, 3)
+    for m in range(3):
+        packed[m] = jnp.where(free, jnp.where(right, roll(last, -1 - m, 0), roll(last, 3 - m, 0)), packed[m])
+    return packed
+
+
+def pack_corner(tiles, right):
+    near, far = pack_rows(tiles[:4], right)
+    last = upper_half(tiles[4], right)
+    free = iota(last.shape, 0) == jnp.where(right, 0, 3)
+    return [near, jnp.where(free, jnp.where(right, roll(last, -3, 0), roll(last, 3, 0)), far)]
 
 
 def unpack_row(message, start, i, right):
     tile = message[start + i // 2]
     return jnp.where(right == (i % 2 == 0), tile, roll(tile, STRIP // 2, 0))
+
+
+def unpack_source(message, start, rows, i, right):
+    if i < rows - 2:
+        return unpack_row(message, start, i, right)
+    tiles = [message[start + m] for m in range(3)]
+    col = iota(tiles[0].shape, 0) % (STRIP // 2)
+    last = jnp.zeros(tiles[0].shape, FLOAT)
+    for m, tile in enumerate(tiles):
+        from_right = jnp.where(col == m, roll(tile, m - 3, 0), last)
+        last = jnp.where(right, from_right, jnp.where(col == m + 1, roll(tile, m + 1, 0), last))
+    return jnp.where(right == (i % 2 == 0), last, roll(last, STRIP // 2, 0))
+
+
+def unpack_corner(message, start, i, right):
+    if i < 2 or i == 3:
+        return unpack_row(message, start, i, right)
+    tile = message[start + 1]
+    col = iota(tile.shape, 0)
+    if i == 2:
+        tile = jnp.where(col == jnp.where(right, 3, 0), 0.0, tile)
+    else:
+        place = col == jnp.where(right, 0, 3)
+        tile = jnp.where(place, jnp.where(right, roll(tile, -3, 0), roll(tile, 3, 0)), 0.0)
+    return jnp.where(right, tile, roll(tile, STRIP // 2, 0))
+
+
+def put_tiles(out, start, tiles):
+    for i, tile in enumerate(tiles):
+        out[start + i] = tile
 
 
 def pack_kernel(nd, nc, rhs_hbm, kappa_hbm, mask_hbm, conduct, *refs):
@@ -144,13 +197,13 @@
                 strip = edge_strip(right, cols)
                 tiles = [conduct[x, strip, :] for x in near]
                 tiles += [rhs[counted(x, rows), strip, :] for x in near[:-1]]
-                pack_rows(next(messages), 0, tiles, right)
+                put_tiles(next(messages), 0, pack_corner(tiles, right))
     for cross_kind in pairings(nc):
         right, _ = facing(cross, nc, cross_kind)
         strip = edge_strip(right, cols)
-        tiles = [conduct[x, strip, :] for x in range(rows)]
-        tiles += [rhs[counted(x, rows), strip, :] for x in range(rows)]
-        pack_rows(next(messages), 0, tiles, right)
+        tiles = pack_rows([conduct[x, strip, :] for x in range(rows)], right)
+        tiles += pack_source([rhs[counted(x, rows), strip, :] for x in range(rows)], right)
+        put_tiles(next(messages), 0, tiles)
 
 
 def strip_kernel(nd, nc, even, *refs):
@@ -159,10 +212,9 @@
     for cross_kind, own, out in zip(pairings(nc), refs[:count], refs[count:]):
         right, _ = facing(lax.axis_index("cross"), nc, cross_kind)
         strip = edge_strip(right, cols)
-        rows = own.shape[0]
-        out[:rows] = own[...]
-        tiles = [even[i, strip, :] for i in range(2 * DEPTH - 1)]
-        pack_rows(out, rows, tiles, right)
+        count = own.shape[0]
+        out[:count] = own[...]
+        put_tiles(out, count, pack_corner([even[i, strip, :] for i in range(2 * DEPTH - 1)], right))
 
 
 def fold(x):
@@ -205,10 +257,10 @@
             self.sides.append((halo_col >= start) & (halo_col < stop))
             self.rights.append(right)
 
-    def merged(self, messages, start, i):
+    def merged(self, messages, unpack, *place):
         total = jnp.zeros((STRIP, self.layers), FLOAT)
         for side, right, message in zip(self.sides, self.rights, messages):
-            total = jnp.where(side, unpack_row(message, start, i, right), total)
+            total = jnp.where(side, unpack(message, *place, right), total)
         return total
 
     def row(self, own, halo):
@@ -342,13 +394,15 @@
     own, halo = frame.own, frame.halo
 
     for x in range(rows):
-        q[x] = frame.row(conduct[x], frame.merged(strips, 0, x))
-        src[x] = frame.row(rhs[counted(x, rows)], frame.merged(strips, 0, rows + x))
+        q[x] = frame.row(conduct[x], frame.merged(strips, unpack_row, 0, x))
+        edge = frame.merged(strips, unpack_source, rows // 2, rows, x)
+        src[x] = frame.row(rhs[counted(x, rows)], edge)
     _, valid = facing(lax.axis_index("down"), nd, False)
     for i in range(DEPTH):
-        q[rows + i] = jnp.where(valid, frame.row(even[i], frame.merged(strips, rows, i)), 0.0)
+        corner = frame.merged(strips, unpack_corner, rows - 1, i)
+        q[rows + i] = jnp.where(valid, frame.row(even[i], corner), 0.0)
     for i in range(DEPTH - 1):
-        corner = frame.merged(strips, rows, DEPTH + i)
+        corner = frame.merged(strips, unpack_corner, rows - 1, DEPTH + i)
         src[rows + i] = jnp.where(valid, frame.row(even[DEPTH + i], corner), 0.0)
 
     here = q[0]
@@ -416,9 +470,10 @@
 
     valid = beside(down, nd, jnp.where(even, -1, 1))
     for i in range(DEPTH):
-        q[-1 - i] = jnp.where(valid, frame.row(odd[i], frame.merged(corners, 0, i)), 0.0)
+        corner = frame.merged(corners, unpack_corner, 0, i)
+        q[-1 - i] = jnp.where(valid, frame.row(odd[i], corner), 0.0)
     for i in range(DEPTH - 1):
-        corner = frame.merged(corners, 0, DEPTH + i)
+        corner = frame.merged(corners, unpack_corner, 0, DEPTH + i)
         src[-1 - i] = jnp.where(valid, frame.row(odd[DEPTH + i], corner), 0.0)
     for x in range(*late["wx"]):
         frame.weights(
@@ -775,7 +830,7 @@
             for cross_kind in pairings(nc):
                 shapes.append(whole(CORNER, STRIP, layers))
                 perms.append(pairs_of(nd, nc, kind, cross_kind))
-    strips = [whole(rows, STRIP, layers) for _ in pairings(nc)]
+    strips = [whole(rows - 1, STRIP, layers) for _ in pairings(nc)]
     packs, couples, tile_w = rows // 4, tiles // 2, cols // tiles
     tile_shape = (couples, tile_w, layers)
     conduct, *messages = call(
@@ -796,7 +851,7 @@
     if strips:
         strips = call(
             functools.partial(strip_kernel, nd, nc),
-            [whole(rows + CORNER, STRIP, layers) for _ in strips],
+            [whole(rows - 1 + CORNER, STRIP, layers) for _ in strips],
             [vmem] * (1 + len(strips)),
         )(even, *messages[len(perms) :])
         strips = [

time: 27.1 us -> 26.7 us (0.985)
  no operation moved by 1% of the time
where the time goes in v8:
time: 26.7 us; the launch traced here: 26.5 us
  starting transfers between devices  14.1 us (53%)
  Pallas kernels  6.51 us (24%)
  waiting for transfers between devices  5.34 us (20%)
  local copies, waits for them, and re-layouts  0.57 us (2%)
    all_to_all x1, starting transfers between devices, body(): lax.all_to_all(chunks, ('cross', 'down'), 0, 0, tiled=True)  7.17 us
    ppermute x2, starting transfers between devices, body(): lax.ppermute(m, axes, pairs_of(nd, nc, None, cross_kind))  4.65 us
    ppermute x2, waiting for transfers between devices, body(): lax.ppermute(m, axes, pairs_of(nd, nc, None, cross_kind))  2.52 us
    all_to_all x1, waiting for transfers between devices, body(): lax.all_to_all(chunks, ('cross', 'down'), 0, 0, tiled=True)  1.9 us
    pallas_call x1, Pallas kernels, body(): call(functools.partial(late_kernel, nd, nc, tiles, rows), [whole(STRIP, l...  1.3 us
    ppermute x3, starting transfers between devices, body(): received = [lax.ppermute(m, axes, p) for m, p in zip(messages, perms)]  1.26 us
    pallas_call x1, Pallas kernels, body(): call(functools.partial(last_kernel, nd, nc), block, [vmem] * (2 + len(res...  1.2 us
    pallas_call x1, Pallas kernels, body(): call(functools.partial(pack_kernel, nd, nc), [block] + shapes + strips, [...  1.17 us
  transfers between devices with their start and end apart: 8, of which 5 were waited for; matrix products, arithmetic and copies ran while one was open for 0% of the time, Pallas kernels for 11%

profile of v8, /device:TPU:0, one launch (start us, length us, event | category | flops | bytes accessed | tf_op | source)
XLA Modules:
  0.0 26.5 jit_solution(4897703400488642062)
XLA Ops:
  0.0 1.2 %shard_map.46 = (f32[8,32,256]{2,1,0:T(8,128)S(1)}, f32[5,32,256]{2,1,0:T(8,128)S(1)}, f32[5,32,256]{2,1,0:T(8,128)S(1)}, f32[2,8,256]{2,1,0:T(8,128)S(1)}, f32[7,8,256]{2,1,0:T(8,128)S(1)}) custom-call(f32[8,32,256]{2,1,0:T(8,128)} %rhs.1, f32[8,32,256]{2,1,0:T(8,128)} %kappa_hbm.1, s32[8,32,256]{2,1,0:T(8,128)} %mask_hbm.1), custom_call_target="tpu_custom_call" | custom-call | tf_op jit(solution)/shard_map/pallas_call | solution.py:836
  1.2 0.5 %collective-permute-start.2 = (f32[5,32,256]{2,1,0:T(8,128)S(1)}, f32[5,32,256]{2,1,0:T(8,128)S(1)}, u32[]{:S(2)}, u32[]{:S(2)}) collective-permute-start(f32[5,32,256]{2,1,0:T(8,128)S(1)} %get-tuple-element.44), channel_id=1, source_target_pairs={{0,2},{1,3},{2,0},{3,1},{4,6},{5,7},{6,4},{7,5},{8,10},{9,11},{10,... | collective-permute-start | bytes 491528 | tf_op jit(solution)/shard_map/ppermute | solution.py:849
  1.7 0.7 %collective-permute-start = (f32[5,32,256]{2,1,0:T(8,128)S(1)}, f32[5,32,256]{2,1,0:T(8,128)S(1)}, u32[]{:S(2)}, u32[]{:S(2)}) collective-permute-start(f32[5,32,256]{2,1,0:T(8,128)S(1)} %get-tuple-element.41), channel_id=1, source_target_pairs={{0,0},{1,1},{2,4},{3,5},{4,2},{5,3},{6,8},{7,9},{8,6},{9,7},{10,12... | collective-permute-start | bytes 491528 | tf_op jit(solution)/shard_map/ppermute | solution.py:849
  2.4 0.4 %collective-permute-done.2.even = f32[5,32,256]{2,1,0:T(8,128)S(1)} collective-permute-done((f32[5,32,256]{2,1,0:T(8,128)S(1)}, f32[5,32,256]{2,1,0:T(8,128)S(1)}, u32[]{:S(2)}, u32[]{:S(2)}) %collective-permute-start.2) | collective-permute-done | bytes 163872 | tf_op jit(solution)/shard_map/ppermute | solution.py:849
  2.7 0.0 copy-start
  2.7 2.9 %collective-permute-start.3 = (f32[9,8,256]{2,1,0:T(8,128)S(1)}, f32[9,8,256]{2,1,0:T(8,128)S(1)}, u32[]{:S(2)}, u32[]{:S(2)}) collective-permute-start(f32[9,8,256]{2,1,0:T(8,128)S(1)} %shard_map.47), channel_id=1, source_target_pairs={{0,1},{1,0},{2,3},{3,2},{4,5},{5,4},{6,7},{7,6},{8,9},{9,8},{10,11... | collective-permute-start | bytes 221192 | tf_op jit(solution)/shard_map/ppermute | solution.py:858
  5.7 0.0 copy-start.1
  5.7 0.1 collective-permute-start.1
  5.8 0.6 %copy-done.1 = s32[1,4]{1,0:T(1,128)S(1)} copy-done((s32[1,4]{1,0:T(1,128)S(1)}, s32[1,4]{1,0:T(1,128)}, u32[]{:S(2)}) %copy-start.1) | copy-done | bytes 40
  6.3 0.2 shard_map.49
  6.5 1.5 %collective-permute-done.3.refs_0_ = f32[9,8,256]{2,1,0:T(8,128)S(1)} collective-permute-done((f32[9,8,256]{2,1,0:T(8,128)S(1)}, f32[9,8,256]{2,1,0:T(8,128)S(1)}, u32[]{:S(2)}, u32[]{:S(2)}) %collective-permute-start.3) | collective-permute-done | bytes 73760 | tf_op jit(solution)/shard_map/ppermute | solution.py:858
  8.0 0.0 copy-done
  8.0 1.0 %shard_map.48 = (f32[11,40,256]{2,1,0:T(8,128)S(1)}, f32[10,40,256]{2,1,0:T(8,128)S(1)}, f32[9,40,256]{2,1,0:T(8,128)S(1)}, f32[9,40,256]{2,1,0:T(8,128)S(1)}, f...) custom-call(f32[8,32,256]{2,1,0:T(8,128)S(1)} %copy-done, ...), custom_call_target="tpu_custom_call" | custom-call | tf_op jit(solution)/shard_map/pallas_call | solution.py:864
  9.0 0.5 %collective-permute-done.1.refs_0_ = f32[2,8,256]{2,1,0:T(8,128)S(1)} collective-permute-done((f32[2,8,256]{2,1,0:T(8,128)S(1)}, f32[2,8,256]{2,1,0:T(8,128)S(1)}, u32[]{:S(2)}, u32[]{:S(2)}) %collective-permute-start.1) | collective-permute-done | bytes 16416 | tf_op jit(solution)/shard_map/ppermute | solution.py:849
  9.6 0.0 collective-permute-done.odd
  9.6 1.3 %shard_map.50 = (f32[8,256]{1,0:T(8,128)S(1)}, f32[2,40,256]{2,1,0:T(8,128)S(1)}, f32[3,40,256]{2,1,0:T(8,128)S(1)}, f32[2,40,256]{2,1,0:T(8,128)S(1)}, f32[1,40...) custom-call(f32[5,32,256]{2,1,0:T(8,128)S(1)} %collective-permute-do, ...), custom_call_target="tpu_custom_call" | custom-call | tf_op jit(solution)/shard_map/pallas_call | solution.py:880
  10.9 7.2 %all-to-all-start = ((f32[32,2,1,128]{3,1,2,0:T(2,128)}), f32[32,2,1,128]{3,1,2,0:T(2,128)S(1)}, u32[]{:S(2)}, u32[]{:S(2)}) async-start(f32[32,2,1,128]{3,1,2,0:T(2,128)} %bitcast.1), calls=%async_computation | async-start | bytes 65536 | tf_op jit(solution)/shard_map/all_to_all | solution.py:903
  18.1 0.3 %collective-permute-start.4 = (f32[40,256]{1,0:T(8,128)S(1)}, f32[40,256]{1,0:T(8,128)S(1)}, u32[]{:S(2)}, u32[]{:S(2)}) collective-permute-start(f32[40,256]{1,0:T(8,128)S(1)} %get-tuple-element.62), channel_id=1, source_target_pairs={{0,2},{1,3},{2,0},{3,1},{4,6},{5,7},{6,4},{7,5},{8,10},{9,11},{10,... | collective-permute-start | bytes 122888 | tf_op jit(solution)/shard_map/ppermute | solution.py:905
  18.4 0.7 %collective-permute-start.5 = (f32[40,256]{1,0:T(8,128)S(1)}, f32[40,256]{1,0:T(8,128)S(1)}, u32[]{:S(2)}, u32[]{:S(2)}) collective-permute-start(f32[40,256]{1,0:T(8,128)S(1)} %get-tuple-element.63), channel_id=1, source_target_pairs={{0,0},{1,1},{2,4},{3,5},{4,2},{5,3},{6,8},{7,9},{8,6},{9,7},{10,12... | collective-permute-start | bytes 122888 | tf_op jit(solution)/shard_map/ppermute | solution.py:904
  19.0 1.7 %collective-permute-start.6 = (f32[8,256]{1,0:T(8,128)S(1)}, f32[8,256]{1,0:T(8,128)S(1)}, u32[]{:S(2)}, u32[]{:S(2)}) collective-permute-start(f32[8,256]{1,0:T(8,128)S(1)} %get-tuple-element.66), channel_id=1, source_target_pairs={{0,1},{1,0},{2,3},{3,2},{4,5},{5,4},{6,7},{7,6},{8,9},{9,8},{10,11... | collective-permute-start | bytes 24584 | tf_op jit(solution)/shard_map/ppermute | solution.py:907
  20.8 0.9 %shard_map.52 = (f32[8,32,256]{2,1,0:T(8,128)S(1)}, f32[2,32,256]{2,1,0:T(8,128)S(1)}, f32[2,32,256]{2,1,0:T(8,128)S(1)}, f32[8,16,256]{2,1,0:T(8,128)S(1)}, f32[2,16,256]{2,1,0:T(8,128)S(1)}) custom-call(f32[10,40,256]{2,1,0:T(8,128)S(1)} %get-tuple-element.47.refs_2_.refs_1_.refs_0_, f32[9,40,256]{2,1,0:T(8,128)S(1)} %get-tuple-element.48.refs_3_.refs_2_.refs_1_, ...), custom_call_target="tpu_custom_call" | custom-call | tf_op jit(solution)/shard_map/pallas_call | solution.py:919
  21.7 1.0 %collective-permute-done.6.refs_0_ = f32[8,256]{1,0:T(8,128)S(1)} collective-permute-done((f32[8,256]{1,0:T(8,128)S(1)}, f32[8,256]{1,0:T(8,128)S(1)}, u32[]{:S(2)}, u32[]{:S(2)}) %collective-permute-start.6) | collective-permute-done | bytes 8224 | tf_op jit(solution)/shard_map/ppermute | solution.py:907
  22.8 0.0 collective-permute-done.4.near
  22.8 0.0 collective-permute-done.5.far
  22.8 0.7 %shard_map.51.base = f32[8,32,256]{2,1,0:T(8,128)S(1)} custom-call(f32[40,256]{1,0:T(8,128)S(1)} %collective-permute-done.4.near, f32[40,256]{1,0:T(8,128)S(1)} %collective-permute-done.5.far, f32[2,2,8,256]{3,2,1,0:T(8,128)S(1)} %get-tuple-element.64.fix, f32[7,40,256]{2,1,0:T(8,128)S(1)} %get-tuple-element.54.refs_9_.pres_early, ...), custom_call_target="tpu_custom_call" | custom-call | tf_op jit(solution)/shard_map/pallas_call | solution.py:910
  23.4 1.9 %all-to-all-done = f32[32,2,1,128]{3,1,2,0:T(2,128)S(1)} async-done(((f32[32,2,1,128]{3,1,2,0:T(2,128)}), f32[32,2,1,128]{3,1,2,0:T(2,128)S(1)}, u32[]{:S(2)}, u32[]{:S(2)}) %all-to-all-start) | async-done | bytes 32800 | tf_op jit(solution)/shard_map/all_to_all | solution.py:903
  25.3 1.2 %shard_map.53 = f32[8,32,256]{2,1,0:T(8,128)} custom-call(f32[64,128]{1,0:T(8,128)S(1)} %bitcast.4, f32[8,32,256]{2,1,0:T(8,128)S(1)} %shard_map.51.base, f32[8,32,256]{2,1,0:T(8,128)S(1)} %get-tuple-element.72.every, f32[2,32,256]{2,1,0:T(8,128)S(1)} %get-tuple-element.73.by_odd, f32[2,32,256]{2,1,0:T(8,128)S(1)} %get-tuple-element.74.by_even, ...), custom_call_target="tpu_custom_call" | custom-call | tf_op jit(solution)/shard_map/pallas_call | solution.py:930
  (1 shorter events, 0.0 us)
Async XLA Ops:
  1.2 1.5 %collective-permute-start.2 = (f32[5,32,256]{2,1,0:T(8,128)S(1)}, f32[5,32,256]{2,1,0:T(8,128)S(1)}, u32[]{:S(2)}, u32[]{:S(2)}) collective-permute-start(f32[5,32,256]{2,1,0:T(8,128)S(1)} %get-tuple-element.44), channel_id=1, source_target_pairs={{0,2},{1,3},{2,0},{3,1},{4,6},{5,7},{6,4},{7,5},{8,10},{9,11},{10,... | collective-permute-start | bytes 491528 | tf_op jit(solution)/shard_map/ppermute | solution.py:849
  1.7 7.9 %collective-permute-start = (f32[5,32,256]{2,1,0:T(8,128)S(1)}, f32[5,32,256]{2,1,0:T(8,128)S(1)}, u32[]{:S(2)}, u32[]{:S(2)}) collective-permute-start(f32[5,32,256]{2,1,0:T(8,128)S(1)} %get-tuple-element.41), channel_id=1, source_target_pairs={{0,0},{1,1},{2,4},{3,5},{4,2},{5,3},{6,8},{7,9},{8,6},{9,7},{10,12... | collective-permute-start | bytes 491528 | tf_op jit(solution)/shard_map/ppermute | solution.py:849
  2.7 5.3 %copy-start = (f32[8,32,256]{2,1,0:T(8,128)S(1)}, f32[8,32,256]{2,1,0:T(8,128)}, u32[]{:S(2)}) copy-start(f32[8,32,256]{2,1,0:T(8,128)} %rhs.1) | copy-start | bytes 786436
  2.7 5.3 %collective-permute-start.3 = (f32[9,8,256]{2,1,0:T(8,128)S(1)}, f32[9,8,256]{2,1,0:T(8,128)S(1)}, u32[]{:S(2)}, u32[]{:S(2)}) collective-permute-start(f32[9,8,256]{2,1,0:T(8,128)S(1)} %shard_map.47), channel_id=1, source_target_pairs={{0,1},{1,0},{2,3},{3,2},{4,5},{5,4},{6,7},{7,6},{8,9},{9,8},{10,11... | collective-permute-start | bytes 221192 | tf_op jit(solution)/shard_map/ppermute | solution.py:858
  5.7 0.7 %copy-start.1 = (s32[1,4]{1,0:T(1,128)S(1)}, s32[1,4]{1,0:T(1,128)}, u32[]{:S(2)}) copy-start(s32[1,4]{1,0:T(1,128)} %route.1) | copy-start | bytes 52
  5.7 3.9 %collective-permute-start.1 = (f32[2,8,256]{2,1,0:T(8,128)S(1)}, f32[2,8,256]{2,1,0:T(8,128)S(1)}, u32[]{:S(2)}, u32[]{:S(2)}) collective-permute-start(f32[2,8,256]{2,1,0:T(8,128)S(1)} %get-tuple-element.42), channel_id=1, source_target_pairs={{0,1},{1,0},{2,5},{3,4},{4,3},{5,2},{6,9},{7,8},{8,7},{9,6},{10,13... | collective-permute-start | bytes 49160 | tf_op jit(solution)/shard_map/ppermute | solution.py:849
  10.9 14.5 %all-to-all-start = ((f32[32,2,1,128]{3,1,2,0:T(2,128)}), f32[32,2,1,128]{3,1,2,0:T(2,128)S(1)}, u32[]{:S(2)}, u32[]{:S(2)}) async-start(f32[32,2,1,128]{3,1,2,0:T(2,128)} %bitcast.1), calls=%async_computation | async-start | bytes 65536 | tf_op jit(solution)/shard_map/all_to_all | solution.py:903
  18.1 4.7 %collective-permute-start.4 = (f32[40,256]{1,0:T(8,128)S(1)}, f32[40,256]{1,0:T(8,128)S(1)}, u32[]{:S(2)}, u32[]{:S(2)}) collective-permute-start(f32[40,256]{1,0:T(8,128)S(1)} %get-tuple-element.62), channel_id=1, source_target_pairs={{0,2},{1,3},{2,0},{3,1},{4,6},{5,7},{6,4},{7,5},{8,10},{9,11},{10,... | collective-permute-start | bytes 122888 | tf_op jit(solution)/shard_map/ppermute | solution.py:905
  18.4 4.4 %collective-permute-start.5 = (f32[40,256]{1,0:T(8,128)S(1)}, f32[40,256]{1,0:T(8,128)S(1)}, u32[]{:S(2)}, u32[]{:S(2)}) collective-permute-start(f32[40,256]{1,0:T(8,128)S(1)} %get-tuple-element.63), channel_id=1, source_target_pairs={{0,0},{1,1},{2,4},{3,5},{4,2},{5,3},{6,8},{7,9},{8,6},{9,7},{10,12... | collective-permute-start | bytes 122888 | tf_op jit(solution)/shard_map/ppermute | solution.py:904
  19.0 3.7 %collective-permute-start.6 = (f32[8,256]{1,0:T(8,128)S(1)}, f32[8,256]{1,0:T(8,128)S(1)}, u32[]{:S(2)}, u32[]{:S(2)}) collective-permute-start(f32[8,256]{1,0:T(8,128)S(1)} %get-tuple-element.66), channel_id=1, source_target_pairs={{0,1},{1,0},{2,3},{3,2},{4,5},{5,4},{6,7},{7,6},{8,9},{9,8},{10,11... | collective-permute-start | bytes 24584 | tf_op jit(solution)/shard_map/ppermute | solution.py:907

commit v9 on v8

--- a/solution.py
+++ b/solution.py
@@ -101,6 +101,10 @@
     return pl.ds(pl.multiple_of(jnp.where(right, cols - STRIP, 0), STRIP), STRIP)
 
 
+def strip_tiles(rows):
+    return rows // 2 - 1 + rows // 4
+
+
 def upper_half(tile, right):
     return jnp.where(right, roll(tile, STRIP // 2, 0), tile)
 
@@ -116,7 +120,27 @@
     ]
 
 
-def pack_source(tiles, right):
+def pack_pair_columns(tiles, right):
+    packed = []
+    for i in range(0, len(tiles), 4):
+        out = jnp.zeros(tiles[0].shape, FLOAT)
+        for j, tile in enumerate(tiles[i : i + 4]):
+            half = upper_half(tile, right)
+            moved = jnp.where(right, roll(half, 2 * j - 2, 0), roll(half, 2 * j, 0))
+            out = jnp.where(iota(out.shape, 0) // 2 == j, moved, out)
+        packed.append(out)
+    return packed
+
+
+def unpack_pair_columns(message, start, i, right):
+    tile = message[start + i // 4]
+    col, j = iota(tile.shape, 0), i % 4
+    from_right = jnp.where(col < 2, roll(tile, -2 * j, 0), 0.0)
+    from_left = jnp.where(col >= STRIP - 2, roll(tile, STRIP - 2 - 2 * j, 0), 0.0)
+    return jnp.where(right, from_right, from_left)
+
+
+def pack_three(tiles, right):
     *packed, last = pack_rows(tiles, right)
     col = iota(last.shape, 0) % (STRIP // 2)
     free = col == jnp.where(right, 0, 3)
@@ -137,7 +161,7 @@
     return jnp.where(right == (i % 2 == 0), tile, roll(tile, STRIP // 2, 0))
 
 
-def unpack_source(message, start, rows, i, right):
+def unpack_three(message, start, rows, i, right):
     if i < rows - 2:
         return unpack_row(message, start, i, right)
     tiles = [message[start + m] for m in range(3)]
@@ -201,8 +225,8 @@
     for cross_kind in pairings(nc):
         right, _ = facing(cross, nc, cross_kind)
         strip = edge_strip(right, cols)
-        tiles = pack_rows([conduct[x, strip, :] for x in range(rows)], right)
-        tiles += pack_source([rhs[counted(x, rows), strip, :] for x in range(rows)], right)
+        tiles = pack_three([conduct[x, strip, :] for x in range(rows)], right)
+        tiles += pack_pair_columns([rhs[counted(x, rows), strip, :] for x in range(rows)], right)
         put_tiles(next(messages), 0, tiles)
 
 
@@ -394,15 +418,15 @@
     own, halo = frame.own, frame.halo
 
     for x in range(rows):
-        q[x] = frame.row(conduct[x], frame.merged(strips, unpack_row, 0, x))
-        edge = frame.merged(strips, unpack_source, rows // 2, rows, x)
+        q[x] = frame.row(conduct[x], frame.merged(strips, unpack_three, 0, rows, x))
+        edge = frame.merged(strips, unpack_pair_columns, rows // 2 - 1, x)
         src[x] = frame.row(rhs[counted(x, rows)], edge)
     _, valid = facing(lax.axis_index("down"), nd, False)
     for i in range(DEPTH):
-        corner = frame.merged(strips, unpack_corner, rows - 1, i)
+        corner = frame.merged(strips, unpack_corner, strip_tiles(rows), i)
         q[rows + i] = jnp.where(valid, frame.row(even[i], corner), 0.0)
     for i in range(DEPTH - 1):
-        corner = frame.merged(strips, unpack_corner, rows - 1, DEPTH + i)
+        corner = frame.merged(strips, unpack_corner, strip_tiles(rows), DEPTH + i)
         src[rows + i] = jnp.where(valid, frame.row(even[DEPTH + i], corner), 0.0)
 
     here = q[0]
@@ -562,7 +586,11 @@
         out[:cols] = pres[x][frame.own] + fine
     for cross_kind, out in zip(pairings(nc), sides):
         right, _ = facing(cross, nc, cross_kind)
-        out[: rows // 2] = jnp.where(right, edges[1], edges[-1])
+        edge = jnp.where(right, edges[1], edges[-1])
+        out[: rows // 2] = edge
+        for x in range(rows):
+            second = jnp.where(right, pres[x][cols - 2 : cols - 1], pres[x][1:2])
+            out[STRIP + x : STRIP + x + 1] = second + edge[x // 2 : x // 2 + 1]
     copy.wait()
 
 
@@ -650,6 +678,7 @@
     frame = Frame(nd, nc, cols, layers)
     pres = Rows((pres_ref, -2, rows + 4))
     third = Rows((third_ref, -1, rows + 2))
+    halo_col = iota((STRIP, layers), 0)
     for k in range(packs):
         for j, part in enumerate(unpack_pairs(fix[k], 1)):
             both = unpack_pairs(part, 2)
@@ -660,7 +689,11 @@
                 edge = jnp.where(place, side[row : row + 1], edge)
             for x in (2 * row, 2 * row + 1):
                 pres_ref[x + 2, own, :] = start[x][own] + fine
-                pres_ref[x + 2, halo, :] = start[x][halo] + edge
+                strip = start[x][halo] + edge
+                for place, right, side in zip(frame.sides, frame.rights, sides):
+                    second = place & (halo_col == jnp.where(right, 1, STRIP - 2))
+                    strip = jnp.where(second, side[STRIP + x : STRIP + x + 1], strip)
+                pres_ref[x + 2, halo, :] = strip
     _, odd_there, even_there = sides_of(nd)
     for message, there, xs in ((near, even_there, (rows, rows + 1)), (far, odd_there, (-1, -2))):
         rim = jnp.where(there, fine_row(message[cols:], couples), 0.0)
@@ -830,7 +863,7 @@
             for cross_kind in pairings(nc):
                 shapes.append(whole(CORNER, STRIP, layers))
                 perms.append(pairs_of(nd, nc, kind, cross_kind))
-    strips = [whole(rows - 1, STRIP, layers) for _ in pairings(nc)]
+    strips = [whole(strip_tiles(rows), STRIP, layers) for _ in pairings(nc)]
     packs, couples, tile_w = rows // 4, tiles // 2, cols // tiles
     tile_shape = (couples, tile_w, layers)
     conduct, *messages = call(
@@ -851,7 +884,7 @@
     if strips:
         strips = call(
             functools.partial(strip_kernel, nd, nc),
-            [whole(rows - 1 + CORNER, STRIP, layers) for _ in strips],
+            [whole(strip_tiles(rows) + CORNER, STRIP, layers) for _ in strips],
             [vmem] * (1 + len(strips)),
         )(even, *messages[len(perms) :])
         strips = [
@@ -879,7 +912,7 @@
     )(conduct, tile_route)
     late_arrays = call(
         functools.partial(late_kernel, nd, nc, tiles, rows),
-        [whole(STRIP, layers) for _ in pairings(nc)]
+        [whole(STRIP + rows, layers) for _ in pairings(nc)]
         + [whole(*span_shape(late[n], wide, layers)) for n in LATE_KEPT]
         + [
             whole(packs, *tile_shape),

time: 26.7 us -> 26.8 us (level)
  no operation moved by 1% of the time
where the time goes in v9:
time: 26.8 us; the launch traced here: 26.6 us
  starting transfers between devices  14.1 us (53%)
  Pallas kernels  6.52 us (24%)
  waiting for transfers between devices  5.36 us (20%)
  local copies, waits for them, and re-layouts  0.57 us (2%)
    all_to_all x1, starting transfers between devices, body(): lax.all_to_all(chunks, ('cross', 'down'), 0, 0, tiled=True)  7.18 us
    ppermute x2, starting transfers between devices, body(): lax.ppermute(m, axes, pairs_of(nd, nc, None, cross_kind))  4.65 us
    ppermute x2, waiting for transfers between devices, body(): lax.ppermute(m, axes, pairs_of(nd, nc, None, cross_kind))  2.44 us
    all_to_all x1, waiting for transfers between devices, body(): lax.all_to_all(chunks, ('cross', 'down'), 0, 0, tiled=True)  1.83 us
    pallas_call x1, Pallas kernels, body(): call(functools.partial(late_kernel, nd, nc, tiles, rows), [whole(STRIP +...  1.3 us
    ppermute x3, starting transfers between devices, body(): received = [lax.ppermute(m, axes, p) for m, p in zip(messages, perms)]  1.26 us
    pallas_call x1, Pallas kernels, body(): call(functools.partial(last_kernel, nd, nc), block, [vmem] * (2 + len(res...  1.2 us
    pallas_call x1, Pallas kernels, body(): call(functools.partial(pack_kernel, nd, nc), [block] + shapes + strips, [...  1.18 us
  transfers between devices with their start and end apart: 8, of which 5 were waited for; matrix products, arithmetic and copies ran while one was open for 0% of the time, Pallas kernels for 11%

profile of v9, /device:TPU:0, one launch (start us, length us, event | category | flops | bytes accessed | tf_op | source)
XLA Modules:
  0.0 26.6 jit_solution(8205056854505674511)
XLA Ops:
  0.0 1.2 %shard_map.46 = (f32[8,32,256]{2,1,0:T(8,128)S(1)}, f32[5,32,256]{2,1,0:T(8,128)S(1)}, f32[5,32,256]{2,1,0:T(8,128)S(1)}, f32[2,8,256]{2,1,0:T(8,128)S(1)}, f32[5,8,256]{2,1,0:T(8,128)S(1)}) custom-call(f32[8,32,256]{2,1,0:T(8,128)} %rhs.1, f32[8,32,256]{2,1,0:T(8,128)} %kappa_hbm.1, s32[8,32,256]{2,1,0:T(8,128)} %mask_hbm.1), custom_call_target="tpu_custom_call" | custom-call | tf_op jit(solution)/shard_map/pallas_call | solution.py:869
  1.2 0.5 %collective-permute-start.2 = (f32[5,32,256]{2,1,0:T(8,128)S(1)}, f32[5,32,256]{2,1,0:T(8,128)S(1)}, u32[]{:S(2)}, u32[]{:S(2)}) collective-permute-start(f32[5,32,256]{2,1,0:T(8,128)S(1)} %get-tuple-element.44), channel_id=1, source_target_pairs={{0,2},{1,3},{2,0},{3,1},{4,6},{5,7},{6,4},{7,5},{8,10},{9,11},{10,... | collective-permute-start | bytes 491528 | tf_op jit(solution)/shard_map/ppermute | solution.py:882
  1.7 0.7 %collective-permute-start = (f32[5,32,256]{2,1,0:T(8,128)S(1)}, f32[5,32,256]{2,1,0:T(8,128)S(1)}, u32[]{:S(2)}, u32[]{:S(2)}) collective-permute-start(f32[5,32,256]{2,1,0:T(8,128)S(1)} %get-tuple-element.41), channel_id=1, source_target_pairs={{0,0},{1,1},{2,4},{3,5},{4,2},{5,3},{6,8},{7,9},{8,6},{9,7},{10,12... | collective-permute-start | bytes 491528 | tf_op jit(solution)/shard_map/ppermute | solution.py:882
  2.4 0.4 %collective-permute-done.2.even = f32[5,32,256]{2,1,0:T(8,128)S(1)} collective-permute-done((f32[5,32,256]{2,1,0:T(8,128)S(1)}, f32[5,32,256]{2,1,0:T(8,128)S(1)}, u32[]{:S(2)}, u32[]{:S(2)}) %collective-permute-start.2) | collective-permute-done | bytes 163872 | tf_op jit(solution)/shard_map/ppermute | solution.py:882
  2.7 0.0 copy-start
  2.8 2.9 %collective-permute-start.3 = (f32[7,8,256]{2,1,0:T(8,128)S(1)}, f32[7,8,256]{2,1,0:T(8,128)S(1)}, u32[]{:S(2)}, u32[]{:S(2)}) collective-permute-start(f32[7,8,256]{2,1,0:T(8,128)S(1)} %shard_map.47), channel_id=1, source_target_pairs={{0,1},{1,0},{2,3},{3,2},{4,5},{5,4},{6,7},{7,6},{8,9},{9,8},{10,11... | collective-permute-start | bytes 172040 | tf_op jit(solution)/shard_map/ppermute | solution.py:891
  5.7 0.0 copy-start.1
  5.7 0.1 collective-permute-start.1
  5.8 0.6 %copy-done.1 = s32[1,4]{1,0:T(1,128)S(1)} copy-done((s32[1,4]{1,0:T(1,128)S(1)}, s32[1,4]{1,0:T(1,128)}, u32[]{:S(2)}) %copy-start.1) | copy-done | bytes 40
  6.3 0.2 shard_map.49
  6.5 1.3 %collective-permute-done.3.refs_0_ = f32[7,8,256]{2,1,0:T(8,128)S(1)} collective-permute-done((f32[7,8,256]{2,1,0:T(8,128)S(1)}, f32[7,8,256]{2,1,0:T(8,128)S(1)}, u32[]{:S(2)}, u32[]{:S(2)}) %collective-permute-start.3) | collective-permute-done | bytes 57376 | tf_op jit(solution)/shard_map/ppermute | solution.py:891
  7.8 0.0 copy-done
  7.8 1.0 %shard_map.48 = (f32[11,40,256]{2,1,0:T(8,128)S(1)}, f32[10,40,256]{2,1,0:T(8,128)S(1)}, f32[9,40,256]{2,1,0:T(8,128)S(1)}, f32[9,40,256]{2,1,0:T(8,128)S(1)}, f...) custom-call(f32[8,32,256]{2,1,0:T(8,128)S(1)} %copy-done, ...), custom_call_target="tpu_custom_call" | custom-call | tf_op jit(solution)/shard_map/pallas_call | solution.py:897
  8.9 0.7 %collective-permute-done.1.refs_0_ = f32[2,8,256]{2,1,0:T(8,128)S(1)} collective-permute-done((f32[2,8,256]{2,1,0:T(8,128)S(1)}, f32[2,8,256]{2,1,0:T(8,128)S(1)}, u32[]{:S(2)}, u32[]{:S(2)}) %collective-permute-start.1) | collective-permute-done | bytes 16416 | tf_op jit(solution)/shard_map/ppermute | solution.py:882
  9.6 0.0 collective-permute-done.odd
  9.6 1.3 %shard_map.50 = (f32[16,256]{1,0:T(8,128)S(1)}, f32[2,40,256]{2,1,0:T(8,128)S(1)}, f32[3,40,256]{2,1,0:T(8,128)S(1)}, f32[2,40,256]{2,1,0:T(8,128)S(1)}, f32[1,4...) custom-call(f32[5,32,256]{2,1,0:T(8,128)S(1)} %collective-permute-do, ...), custom_call_target="tpu_custom_call" | custom-call | tf_op jit(solution)/shard_map/pallas_call | solution.py:913
  10.9 7.2 %all-to-all-start = ((f32[32,2,1,128]{3,1,2,0:T(2,128)}), f32[32,2,1,128]{3,1,2,0:T(2,128)S(1)}, u32[]{:S(2)}, u32[]{:S(2)}) async-start(f32[32,2,1,128]{3,1,2,0:T(2,128)} %bitcast.1), calls=%async_computation | async-start | bytes 65536 | tf_op jit(solution)/shard_map/all_to_all | solution.py:936
  18.1 0.3 %collective-permute-start.4 = (f32[40,256]{1,0:T(8,128)S(1)}, f32[40,256]{1,0:T(8,128)S(1)}, u32[]{:S(2)}, u32[]{:S(2)}) collective-permute-start(f32[40,256]{1,0:T(8,128)S(1)} %get-tuple-element.62), channel_id=1, source_target_pairs={{0,2},{1,3},{2,0},{3,1},{4,6},{5,7},{6,4},{7,5},{8,10},{9,11},{10,... | collective-permute-start | bytes 122888 | tf_op jit(solution)/shard_map/ppermute | solution.py:938
  18.4 0.7 %collective-permute-start.5 = (f32[40,256]{1,0:T(8,128)S(1)}, f32[40,256]{1,0:T(8,128)S(1)}, u32[]{:S(2)}, u32[]{:S(2)}) collective-permute-start(f32[40,256]{1,0:T(8,128)S(1)} %get-tuple-element.63), channel_id=1, source_target_pairs={{0,0},{1,1},{2,4},{3,5},{4,2},{5,3},{6,8},{7,9},{8,6},{9,7},{10,12... | collective-permute-start | bytes 122888 | tf_op jit(solution)/shard_map/ppermute | solution.py:937
  19.1 1.7 %collective-permute-start.6 = (f32[16,256]{1,0:T(8,128)S(1)}, f32[16,256]{1,0:T(8,128)S(1)}, u32[]{:S(2)}, u32[]{:S(2)}) collective-permute-start(f32[16,256]{1,0:T(8,128)S(1)} %get-tuple-element.66), channel_id=1, source_target_pairs={{0,1},{1,0},{2,3},{3,2},{4,5},{5,4},{6,7},{7,6},{8,9},{9,8},{10,11... | collective-permute-start | bytes 49160 | tf_op jit(solution)/shard_map/ppermute | solution.py:940
  20.8 0.9 %shard_map.52 = (f32[8,32,256]{2,1,0:T(8,128)S(1)}, f32[2,32,256]{2,1,0:T(8,128)S(1)}, f32[2,32,256]{2,1,0:T(8,128)S(1)}, f32[8,16,256]{2,1,0:T(8,128)S(1)}, f32[2,16,256]{2,1,0:T(8,128)S(1)}) custom-call(f32[10,40,256]{2,1,0:T(8,128)S(1)} %get-tuple-element.47.refs_2_.refs_1_.refs_0_, f32[9,40,256]{2,1,0:T(8,128)S(1)} %get-tuple-element.48.refs_3_.refs_2_.refs_1_, ...), custom_call_target="tpu_custom_call" | custom-call | tf_op jit(solution)/shard_map/pallas_call | solution.py:952
  21.7 1.1 %collective-permute-done.6.refs_0_ = f32[16,256]{1,0:T(8,128)S(1)} collective-permute-done((f32[16,256]{1,0:T(8,128)S(1)}, f32[16,256]{1,0:T(8,128)S(1)}, u32[]{:S(2)}, u32[]{:S(2)}) %collective-permute-start.6) | collective-permute-done | bytes 16416 | tf_op jit(solution)/shard_map/ppermute | solution.py:940
  22.9 0.0 collective-permute-done.4.near
  22.9 0.0 collective-permute-done.5.far
  22.9 0.7 %shard_map.51.base = f32[8,32,256]{2,1,0:T(8,128)S(1)} custom-call(f32[40,256]{1,0:T(8,128)S(1)} %collective-permute-done.4.near, f32[40,256]{1,0:T(8,128)S(1)} %collective-permute-done.5.far, f32[2,2,8,256]{3,2,1,0:T(8,128)S(1)} %get-tuple-element.64.fix, f32[7,40,256]{2,1,0:T(8,128)S(1)} %get-tuple-element.54.refs_9_.pres_early, ...), custom_call_target="tpu_custom_call" | custom-call | tf_op jit(solution)/shard_map/pallas_call | solution.py:943
  23.6 1.8 %all-to-all-done = f32[32,2,1,128]{3,1,2,0:T(2,128)S(1)} async-done(((f32[32,2,1,128]{3,1,2,0:T(2,128)}), f32[32,2,1,128]{3,1,2,0:T(2,128)S(1)}, u32[]{:S(2)}, u32[]{:S(2)}) %all-to-all-start) | async-done | bytes 32800 | tf_op jit(solution)/shard_map/all_to_all | solution.py:936
  25.4 1.2 %shard_map.53 = f32[8,32,256]{2,1,0:T(8,128)} custom-call(f32[64,128]{1,0:T(8,128)S(1)} %bitcast.4, f32[8,32,256]{2,1,0:T(8,128)S(1)} %shard_map.51.base, f32[8,32,256]{2,1,0:T(8,128)S(1)} %get-tuple-element.72.every, f32[2,32,256]{2,1,0:T(8,128)S(1)} %get-tuple-element.73.by_odd, f32[2,32,256]{2,1,0:T(8,128)S(1)} %get-tuple-element.74.by_even, ...), custom_call_target="tpu_custom_call" | custom-call | tf_op jit(solution)/shard_map/pallas_call | solution.py:963
  (1 shorter events, 0.0 us)
Async XLA Ops:
  1.2 1.5 %collective-permute-start.2 = (f32[5,32,256]{2,1,0:T(8,128)S(1)}, f32[5,32,256]{2,1,0:T(8,128)S(1)}, u32[]{:S(2)}, u32[]{:S(2)}) collective-permute-start(f32[5,32,256]{2,1,0:T(8,128)S(1)} %get-tuple-element.44), channel_id=1, source_target_pairs={{0,2},{1,3},{2,0},{3,1},{4,6},{5,7},{6,4},{7,5},{8,10},{9,11},{10,... | collective-permute-start | bytes 491528 | tf_op jit(solution)/shard_map/ppermute | solution.py:882
  1.7 7.9 %collective-permute-start = (f32[5,32,256]{2,1,0:T(8,128)S(1)}, f32[5,32,256]{2,1,0:T(8,128)S(1)}, u32[]{:S(2)}, u32[]{:S(2)}) collective-permute-start(f32[5,32,256]{2,1,0:T(8,128)S(1)} %get-tuple-element.41), channel_id=1, source_target_pairs={{0,0},{1,1},{2,4},{3,5},{4,2},{5,3},{6,8},{7,9},{8,6},{9,7},{10,12... | collective-permute-start | bytes 491528 | tf_op jit(solution)/shard_map/ppermute | solution.py:882
  2.7 5.1 %copy-start = (f32[8,32,256]{2,1,0:T(8,128)S(1)}, f32[8,32,256]{2,1,0:T(8,128)}, u32[]{:S(2)}) copy-start(f32[8,32,256]{2,1,0:T(8,128)} %rhs.1) | copy-start | bytes 786436
  2.8 5.1 %collective-permute-start.3 = (f32[7,8,256]{2,1,0:T(8,128)S(1)}, f32[7,8,256]{2,1,0:T(8,128)S(1)}, u32[]{:S(2)}, u32[]{:S(2)}) collective-permute-start(f32[7,8,256]{2,1,0:T(8,128)S(1)} %shard_map.47), channel_id=1, source_target_pairs={{0,1},{1,0},{2,3},{3,2},{4,5},{5,4},{6,7},{7,6},{8,9},{9,8},{10,11... | collective-permute-start | bytes 172040 | tf_op jit(solution)/shard_map/ppermute | solution.py:891
  5.7 0.7 %copy-start.1 = (s32[1,4]{1,0:T(1,128)S(1)}, s32[1,4]{1,0:T(1,128)}, u32[]{:S(2)}) copy-start(s32[1,4]{1,0:T(1,128)} %route.1) | copy-start | bytes 52
  5.7 3.9 %collective-permute-start.1 = (f32[2,8,256]{2,1,0:T(8,128)S(1)}, f32[2,8,256]{2,1,0:T(8,128)S(1)}, u32[]{:S(2)}, u32[]{:S(2)}) collective-permute-start(f32[2,8,256]{2,1,0:T(8,128)S(1)} %get-tuple-element.42), channel_id=1, source_target_pairs={{0,1},{1,0},{2,5},{3,4},{4,3},{5,2},{6,9},{7,8},{8,7},{9,6},{10,13... | collective-permute-start | bytes 49160 | tf_op jit(solution)/shard_map/ppermute | solution.py:882
  10.9 14.5 %all-to-all-start = ((f32[32,2,1,128]{3,1,2,0:T(2,128)}), f32[32,2,1,128]{3,1,2,0:T(2,128)S(1)}, u32[]{:S(2)}, u32[]{:S(2)}) async-start(f32[32,2,1,128]{3,1,2,0:T(2,128)} %bitcast.1), calls=%async_computation | async-start | bytes 65536 | tf_op jit(solution)/shard_map/all_to_all | solution.py:936
  18.1 4.8 %collective-permute-start.4 = (f32[40,256]{1,0:T(8,128)S(1)}, f32[40,256]{1,0:T(8,128)S(1)}, u32[]{:S(2)}, u32[]{:S(2)}) collective-permute-start(f32[40,256]{1,0:T(8,128)S(1)} %get-tuple-element.62), channel_id=1, source_target_pairs={{0,2},{1,3},{2,0},{3,1},{4,6},{5,7},{6,4},{7,5},{8,10},{9,11},{10,... | collective-permute-start | bytes 122888 | tf_op jit(solution)/shard_map/ppermute | solution.py:938
  18.4 4.5 %collective-permute-start.5 = (f32[40,256]{1,0:T(8,128)S(1)}, f32[40,256]{1,0:T(8,128)S(1)}, u32[]{:S(2)}, u32[]{:S(2)}) collective-permute-start(f32[40,256]{1,0:T(8,128)S(1)} %get-tuple-element.63), channel_id=1, source_target_pairs={{0,0},{1,1},{2,4},{3,5},{4,2},{5,3},{6,8},{7,9},{8,6},{9,7},{10,12... | collective-permute-start | bytes 122888 | tf_op jit(solution)/shard_map/ppermute | solution.py:937
  19.1 3.8 %collective-permute-start.6 = (f32[16,256]{1,0:T(8,128)S(1)}, f32[16,256]{1,0:T(8,128)S(1)}, u32[]{:S(2)}, u32[]{:S(2)}) collective-permute-start(f32[16,256]{1,0:T(8,128)S(1)} %get-tuple-element.66), channel_id=1, source_target_pairs={{0,1},{1,0},{2,3},{3,2},{4,5},{5,4},{6,7},{7,6},{8,9},{9,8},{10,11... | collective-permute-start | bytes 49160 | tf_op jit(solution)/shard_map/ppermute | solution.py:940

commit v10 on v8

--- a/solution.py
+++ b/solution.py
@@ -540,14 +540,16 @@
         at_couple, at_col = (0, 0) if dy < 0 else (couples - 1, tile_w - 1)
         edge = jnp.concatenate([p[at_couple][at_col : at_col + 1] for p in parts])
         edges[dy] = edge = unpack_pairs(edge, 1)[0 if dy < 0 else 1]
+    for cross_kind in pairings(nc):
+        right, side_there = facing(cross, nc, cross_kind)
+        edge = jnp.where(right, edges[1], edges[-1])
+        other = cross + jnp.where(right, 1, -1)
         for k, step in ((0, odd_step), (rows // 2 - 1, -odd_step)):
-
-            @pl.when(beside(cross, nc, dy) & beside(down, nd, step))
-            def _(k=k, step=step, dy=dy, edge=edge):
-                both = jnp.where(line % 2 == 0, edge[k : k + 1], summary)
-                at = ((cross + dy) * nd + down + step) * CHUNK
-                for i in range(CHUNK):
-                    chunks[pl.ds(at + i, 1), :] = both[:, i * LANES : (i + 1) * LANES]
+            there = side_there & beside(down, nd, step)
+            both = jnp.where(line % 2 == 0, edge[k : k + 1], summary)
+            at = jnp.where(there, other * nd + down + step, cross * nd + down) * CHUNK
+            for i in range(CHUNK):
+                chunks[pl.ds(at + i, 1), :] = both[:, i * LANES : (i + 1) * LANES]
 
     copy = pltpu.make_async_copy(chunks, chunks_hbm, sem)
     copy.start()

time: 26.7 us -> 26.7 us (level)
  no operation moved by 1% of the time
where the time goes in v10:
time: 26.7 us; the launch traced here: 26.5 us
  starting transfers between devices  14.1 us (53%)
  Pallas kernels  6.47 us (24%)
  waiting for transfers between devices  5.34 us (20%)
  local copies, waits for them, and re-layouts  0.57 us (2%)
    all_to_all x1, starting transfers between devices, body(): lax.all_to_all(chunks, ('cross', 'down'), 0, 0, tiled=True)  7.17 us
    ppermute x2, starting transfers between devices, body(): lax.ppermute(m, axes, pairs_of(nd, nc, None, cross_kind))  4.65 us
    ppermute x2, waiting for transfers between devices, body(): lax.ppermute(m, axes, pairs_of(nd, nc, None, cross_kind))  2.52 us
    all_to_all x1, waiting for transfers between devices, body(): lax.all_to_all(chunks, ('cross', 'down'), 0, 0, tiled=True)  1.9 us
    ppermute x3, starting transfers between devices, body(): received = [lax.ppermute(m, axes, p) for m, p in zip(messages, perms)]  1.26 us
    pallas_call x1, Pallas kernels, body(): call(functools.partial(late_kernel, nd, nc, tiles, rows), [whole(STRIP, l...  1.26 us
    pallas_call x1, Pallas kernels, body(): call(functools.partial(last_kernel, nd, nc), block, [vmem] * (2 + len(res...  1.2 us
    pallas_call x1, Pallas kernels, body(): call(functools.partial(pack_kernel, nd, nc), [block] + shapes + strips, [...  1.17 us
  transfers between devices with their start and end apart: 8, of which 5 were waited for; matrix products, arithmetic and copies ran while one was open for 0% of the time, Pallas kernels for 11%

profile of v10, /device:TPU:0, one launch (start us, length us, event | category | flops | bytes accessed | tf_op | source)
XLA Modules:
  0.0 26.5 jit_solution(9251217562973990380)
XLA Ops:
  0.0 1.2 %shard_map.46 = (f32[8,32,256]{2,1,0:T(8,128)S(1)}, f32[5,32,256]{2,1,0:T(8,128)S(1)}, f32[5,32,256]{2,1,0:T(8,128)S(1)}, f32[2,8,256]{2,1,0:T(8,128)S(1)}, f32[7,8,256]{2,1,0:T(8,128)S(1)}) custom-call(f32[8,32,256]{2,1,0:T(8,128)} %rhs.1, f32[8,32,256]{2,1,0:T(8,128)} %kappa_hbm.1, s32[8,32,256]{2,1,0:T(8,128)} %mask_hbm.1), custom_call_target="tpu_custom_call" | custom-call | tf_op jit(solution)/shard_map/pallas_call | solution.py:838
  1.2 0.5 %collective-permute-start.2 = (f32[5,32,256]{2,1,0:T(8,128)S(1)}, f32[5,32,256]{2,1,0:T(8,128)S(1)}, u32[]{:S(2)}, u32[]{:S(2)}) collective-permute-start(f32[5,32,256]{2,1,0:T(8,128)S(1)} %get-tuple-element.44), channel_id=1, source_target_pairs={{0,2},{1,3},{2,0},{3,1},{4,6},{5,7},{6,4},{7,5},{8,10},{9,11},{10,... | collective-permute-start | bytes 491528 | tf_op jit(solution)/shard_map/ppermute | solution.py:851
  1.7 0.7 %collective-permute-start = (f32[5,32,256]{2,1,0:T(8,128)S(1)}, f32[5,32,256]{2,1,0:T(8,128)S(1)}, u32[]{:S(2)}, u32[]{:S(2)}) collective-permute-start(f32[5,32,256]{2,1,0:T(8,128)S(1)} %get-tuple-element.41), channel_id=1, source_target_pairs={{0,0},{1,1},{2,4},{3,5},{4,2},{5,3},{6,8},{7,9},{8,6},{9,7},{10,12... | collective-permute-start | bytes 491528 | tf_op jit(solution)/shard_map/ppermute | solution.py:851
  2.4 0.4 %collective-permute-done.2.even = f32[5,32,256]{2,1,0:T(8,128)S(1)} collective-permute-done((f32[5,32,256]{2,1,0:T(8,128)S(1)}, f32[5,32,256]{2,1,0:T(8,128)S(1)}, u32[]{:S(2)}, u32[]{:S(2)}) %collective-permute-start.2) | collective-permute-done | bytes 163872 | tf_op jit(solution)/shard_map/ppermute | solution.py:851
  2.7 0.0 copy-start
  2.7 2.9 %collective-permute-start.3 = (f32[9,8,256]{2,1,0:T(8,128)S(1)}, f32[9,8,256]{2,1,0:T(8,128)S(1)}, u32[]{:S(2)}, u32[]{:S(2)}) collective-permute-start(f32[9,8,256]{2,1,0:T(8,128)S(1)} %shard_map.47), channel_id=1, source_target_pairs={{0,1},{1,0},{2,3},{3,2},{4,5},{5,4},{6,7},{7,6},{8,9},{9,8},{10,11... | collective-permute-start | bytes 221192 | tf_op jit(solution)/shard_map/ppermute | solution.py:860
  5.7 0.0 copy-start.1
  5.7 0.1 collective-permute-start.1
  5.8 0.6 %copy-done.1 = s32[1,4]{1,0:T(1,128)S(1)} copy-done((s32[1,4]{1,0:T(1,128)S(1)}, s32[1,4]{1,0:T(1,128)}, u32[]{:S(2)}) %copy-start.1) | copy-done | bytes 40
  6.3 0.2 shard_map.49
  6.5 1.5 %collective-permute-done.3.refs_0_ = f32[9,8,256]{2,1,0:T(8,128)S(1)} collective-permute-done((f32[9,8,256]{2,1,0:T(8,128)S(1)}, f32[9,8,256]{2,1,0:T(8,128)S(1)}, u32[]{:S(2)}, u32[]{:S(2)}) %collective-permute-start.3) | collective-permute-done | bytes 73760 | tf_op jit(solution)/shard_map/ppermute | solution.py:860
  8.0 0.0 copy-done
  8.0 1.0 %shard_map.48 = (f32[11,40,256]{2,1,0:T(8,128)S(1)}, f32[10,40,256]{2,1,0:T(8,128)S(1)}, f32[9,40,256]{2,1,0:T(8,128)S(1)}, f32[9,40,256]{2,1,0:T(8,128)S(1)}, f...) custom-call(f32[8,32,256]{2,1,0:T(8,128)S(1)} %copy-done, ...), custom_call_target="tpu_custom_call" | custom-call | tf_op jit(solution)/shard_map/pallas_call | solution.py:866
  9.0 0.5 %collective-permute-done.1.refs_0_ = f32[2,8,256]{2,1,0:T(8,128)S(1)} collective-permute-done((f32[2,8,256]{2,1,0:T(8,128)S(1)}, f32[2,8,256]{2,1,0:T(8,128)S(1)}, u32[]{:S(2)}, u32[]{:S(2)}) %collective-permute-start.1) | collective-permute-done | bytes 16416 | tf_op jit(solution)/shard_map/ppermute | solution.py:851
  9.6 0.0 collective-permute-done.odd
  9.6 1.3 %shard_map.50 = (f32[8,256]{1,0:T(8,128)S(1)}, f32[2,40,256]{2,1,0:T(8,128)S(1)}, f32[3,40,256]{2,1,0:T(8,128)S(1)}, f32[2,40,256]{2,1,0:T(8,128)S(1)}, f32[1,40...) custom-call(f32[5,32,256]{2,1,0:T(8,128)S(1)} %collective-permute-do, ...), custom_call_target="tpu_custom_call" | custom-call | tf_op jit(solution)/shard_map/pallas_call | solution.py:882
  10.8 7.2 %all-to-all-start = ((f32[32,2,1,128]{3,1,2,0:T(2,128)}), f32[32,2,1,128]{3,1,2,0:T(2,128)S(1)}, u32[]{:S(2)}, u32[]{:S(2)}) async-start(f32[32,2,1,128]{3,1,2,0:T(2,128)} %bitcast.1), calls=%async_computation | async-start | bytes 65536 | tf_op jit(solution)/shard_map/all_to_all | solution.py:905
  18.0 0.3 %collective-permute-start.4 = (f32[40,256]{1,0:T(8,128)S(1)}, f32[40,256]{1,0:T(8,128)S(1)}, u32[]{:S(2)}, u32[]{:S(2)}) collective-permute-start(f32[40,256]{1,0:T(8,128)S(1)} %get-tuple-element.62), channel_id=1, source_target_pairs={{0,2},{1,3},{2,0},{3,1},{4,6},{5,7},{6,4},{7,5},{8,10},{9,11},{10,... | collective-permute-start | bytes 122888 | tf_op jit(solution)/shard_map/ppermute | solution.py:907
  18.3 0.7 %collective-permute-start.5 = (f32[40,256]{1,0:T(8,128)S(1)}, f32[40,256]{1,0:T(8,128)S(1)}, u32[]{:S(2)}, u32[]{:S(2)}) collective-permute-start(f32[40,256]{1,0:T(8,128)S(1)} %get-tuple-element.63), channel_id=1, source_target_pairs={{0,0},{1,1},{2,4},{3,5},{4,2},{5,3},{6,8},{7,9},{8,6},{9,7},{10,12... | collective-permute-start | bytes 122888 | tf_op jit(solution)/shard_map/ppermute | solution.py:906
  19.0 1.7 %collective-permute-start.6 = (f32[8,256]{1,0:T(8,128)S(1)}, f32[8,256]{1,0:T(8,128)S(1)}, u32[]{:S(2)}, u32[]{:S(2)}) collective-permute-start(f32[8,256]{1,0:T(8,128)S(1)} %get-tuple-element.66), channel_id=1, source_target_pairs={{0,1},{1,0},{2,3},{3,2},{4,5},{5,4},{6,7},{7,6},{8,9},{9,8},{10,11... | collective-permute-start | bytes 24584 | tf_op jit(solution)/shard_map/ppermute | solution.py:909
  20.7 0.9 %shard_map.52 = (f32[8,32,256]{2,1,0:T(8,128)S(1)}, f32[2,32,256]{2,1,0:T(8,128)S(1)}, f32[2,32,256]{2,1,0:T(8,128)S(1)}, f32[8,16,256]{2,1,0:T(8,128)S(1)}, f32[2,16,256]{2,1,0:T(8,128)S(1)}) custom-call(f32[10,40,256]{2,1,0:T(8,128)S(1)} %get-tuple-element.47.refs_2_.refs_1_.refs_0_, f32[9,40,256]{2,1,0:T(8,128)S(1)} %get-tuple-element.48.refs_3_.refs_2_.refs_1_, ...), custom_call_target="tpu_custom_call" | custom-call | tf_op jit(solution)/shard_map/pallas_call | solution.py:921
  21.7 1.0 %collective-permute-done.6.refs_0_ = f32[8,256]{1,0:T(8,128)S(1)} collective-permute-done((f32[8,256]{1,0:T(8,128)S(1)}, f32[8,256]{1,0:T(8,128)S(1)}, u32[]{:S(2)}, u32[]{:S(2)}) %collective-permute-start.6) | collective-permute-done | bytes 8224 | tf_op jit(solution)/shard_map/ppermute | solution.py:909
  22.7 0.0 collective-permute-done.4.near
  22.7 0.0 collective-permute-done.5.far
  22.7 0.7 %shard_map.51.base = f32[8,32,256]{2,1,0:T(8,128)S(1)} custom-call(f32[40,256]{1,0:T(8,128)S(1)} %collective-permute-done.4.near, f32[40,256]{1,0:T(8,128)S(1)} %collective-permute-done.5.far, f32[2,2,8,256]{3,2,1,0:T(8,128)S(1)} %get-tuple-element.64.fix, f32[7,40,256]{2,1,0:T(8,128)S(1)} %get-tuple-element.54.refs_9_.pres_early, ...), custom_call_target="tpu_custom_call" | custom-call | tf_op jit(solution)/shard_map/pallas_call | solution.py:912
  23.4 1.9 %all-to-all-done = f32[32,2,1,128]{3,1,2,0:T(2,128)S(1)} async-done(((f32[32,2,1,128]{3,1,2,0:T(2,128)}), f32[32,2,1,128]{3,1,2,0:T(2,128)S(1)}, u32[]{:S(2)}, u32[]{:S(2)}) %all-to-all-start) | async-done | bytes 32800 | tf_op jit(solution)/shard_map/all_to_all | solution.py:905
  25.3 1.2 %shard_map.53 = f32[8,32,256]{2,1,0:T(8,128)} custom-call(f32[64,128]{1,0:T(8,128)S(1)} %bitcast.4, f32[8,32,256]{2,1,0:T(8,128)S(1)} %shard_map.51.base, f32[8,32,256]{2,1,0:T(8,128)S(1)} %get-tuple-element.72.every, f32[2,32,256]{2,1,0:T(8,128)S(1)} %get-tuple-element.73.by_odd, f32[2,32,256]{2,1,0:T(8,128)S(1)} %get-tuple-element.74.by_even, ...), custom_call_target="tpu_custom_call" | custom-call | tf_op jit(solution)/shard_map/pallas_call | solution.py:932
  (1 shorter events, 0.0 us)
Async XLA Ops:
  1.2 1.5 %collective-permute-start.2 = (f32[5,32,256]{2,1,0:T(8,128)S(1)}, f32[5,32,256]{2,1,0:T(8,128)S(1)}, u32[]{:S(2)}, u32[]{:S(2)}) collective-permute-start(f32[5,32,256]{2,1,0:T(8,128)S(1)} %get-tuple-element.44), channel_id=1, source_target_pairs={{0,2},{1,3},{2,0},{3,1},{4,6},{5,7},{6,4},{7,5},{8,10},{9,11},{10,... | collective-permute-start | bytes 491528 | tf_op jit(solution)/shard_map/ppermute | solution.py:851
  1.7 7.9 %collective-permute-start = (f32[5,32,256]{2,1,0:T(8,128)S(1)}, f32[5,32,256]{2,1,0:T(8,128)S(1)}, u32[]{:S(2)}, u32[]{:S(2)}) collective-permute-start(f32[5,32,256]{2,1,0:T(8,128)S(1)} %get-tuple-element.41), channel_id=1, source_target_pairs={{0,0},{1,1},{2,4},{3,5},{4,2},{5,3},{6,8},{7,9},{8,6},{9,7},{10,12... | collective-permute-start | bytes 491528 | tf_op jit(solution)/shard_map/ppermute | solution.py:851
  2.7 5.3 %copy-start = (f32[8,32,256]{2,1,0:T(8,128)S(1)}, f32[8,32,256]{2,1,0:T(8,128)}, u32[]{:S(2)}) copy-start(f32[8,32,256]{2,1,0:T(8,128)} %rhs.1) | copy-start | bytes 786436
  2.7 5.3 %collective-permute-start.3 = (f32[9,8,256]{2,1,0:T(8,128)S(1)}, f32[9,8,256]{2,1,0:T(8,128)S(1)}, u32[]{:S(2)}, u32[]{:S(2)}) collective-permute-start(f32[9,8,256]{2,1,0:T(8,128)S(1)} %shard_map.47), channel_id=1, source_target_pairs={{0,1},{1,0},{2,3},{3,2},{4,5},{5,4},{6,7},{7,6},{8,9},{9,8},{10,11... | collective-permute-start | bytes 221192 | tf_op jit(solution)/shard_map/ppermute | solution.py:860
  5.7 0.7 %copy-start.1 = (s32[1,4]{1,0:T(1,128)S(1)}, s32[1,4]{1,0:T(1,128)}, u32[]{:S(2)}) copy-start(s32[1,4]{1,0:T(1,128)} %route.1) | copy-start | bytes 52
  5.7 3.9 %collective-permute-start.1 = (f32[2,8,256]{2,1,0:T(8,128)S(1)}, f32[2,8,256]{2,1,0:T(8,128)S(1)}, u32[]{:S(2)}, u32[]{:S(2)}) collective-permute-start(f32[2,8,256]{2,1,0:T(8,128)S(1)} %get-tuple-element.42), channel_id=1, source_target_pairs={{0,1},{1,0},{2,5},{3,4},{4,3},{5,2},{6,9},{7,8},{8,7},{9,6},{10,13... | collective-permute-start | bytes 49160 | tf_op jit(solution)/shard_map/ppermute | solution.py:851
  10.8 14.5 %all-to-all-start = ((f32[32,2,1,128]{3,1,2,0:T(2,128)}), f32[32,2,1,128]{3,1,2,0:T(2,128)S(1)}, u32[]{:S(2)}, u32[]{:S(2)}) async-start(f32[32,2,1,128]{3,1,2,0:T(2,128)} %bitcast.1), calls=%async_computation | async-start | bytes 65536 | tf_op jit(solution)/shard_map/all_to_all | solution.py:905
  18.0 4.7 %collective-permute-start.4 = (f32[40,256]{1,0:T(8,128)S(1)}, f32[40,256]{1,0:T(8,128)S(1)}, u32[]{:S(2)}, u32[]{:S(2)}) collective-permute-start(f32[40,256]{1,0:T(8,128)S(1)} %get-tuple-element.62), channel_id=1, source_target_pairs={{0,2},{1,3},{2,0},{3,1},{4,6},{5,7},{6,4},{7,5},{8,10},{9,11},{10,... | collective-permute-start | bytes 122888 | tf_op jit(solution)/shard_map/ppermute | solution.py:907
  18.3 4.4 %collective-permute-start.5 = (f32[40,256]{1,0:T(8,128)S(1)}, f32[40,256]{1,0:T(8,128)S(1)}, u32[]{:S(2)}, u32[]{:S(2)}) collective-permute-start(f32[40,256]{1,0:T(8,128)S(1)} %get-tuple-element.63), channel_id=1, source_target_pairs={{0,0},{1,1},{2,4},{3,5},{4,2},{5,3},{6,8},{7,9},{8,6},{9,7},{10,12... | collective-permute-start | bytes 122888 | tf_op jit(solution)/shard_map/ppermute | solution.py:906
  19.0 3.7 %collective-permute-start.6 = (f32[8,256]{1,0:T(8,128)S(1)}, f32[8,256]{1,0:T(8,128)S(1)}, u32[]{:S(2)}, u32[]{:S(2)}) collective-permute-start(f32[8,256]{1,0:T(8,128)S(1)} %get-tuple-element.66), channel_id=1, source_target_pairs={{0,1},{1,0},{2,3},{3,2},{4,5},{5,4},{6,7},{7,6},{8,9},{9,8},{10,11... | collective-permute-start | bytes 24584 | tf_op jit(solution)/shard_map/ppermute | solution.py:909
